TPU v7x, 256 devices: a whole 4x4x8 slice. The times are simulated.
256 devices in a mesh: dp: 8 (over z), vocab: 32 (over y, x, core).
Axes of the slice: x: 4, y: 4, z: 8, core: 2. Of those that a mesh axis runs over, the one named last changes fastest.
Arguments:
- hidden: bfloat16 [32768, 4096], P(('dp', 'vocab')), may hold values from -4 to 4
- output_weight: bfloat16 [4096, 32768], P(None, 'vocab'), may hold values from -0.09375 to 0.09375
- owners: int32 [32768, 3], P(('dp', 'vocab')), may hold values from 0 to 31, all different within a row; in each aligned block of 128 rows (0 to 127, 128 to 255, ...) at most 16 rows name the same one
- negatives: int32 [32768, 3, 2], P(('dp', 'vocab')), may hold values from 0 to 7
- negative_mask: int32 [32768, 3, 2], P(('dp', 'vocab')), may hold values 0 or 1
- target_block: int32 [32768], P(('dp', 'vocab')), may hold values from 0 to 7
- target_word: int32 [32768], P(('dp', 'vocab')), may hold values from 0 to 127
- log_norm: bfloat16 [32768], P(('dp', 'vocab')), may hold values from 1 to 2
- cotangent: bfloat16 [32768], P(('dp', 'vocab')), may hold values from 4 to 8
Outputs:
- hidden_grad: bfloat16 [32768, 4096], P(('dp', 'vocab'))
- weight_grad: bfloat16 [4096, 32768], P('dp', 'vocab')
Inputs may be any that keep to these rules, and one draw needn't show every extreme that they name: Each row names 3 different owners; among the 128 rows of one device no owner is named by more than 16 rows, and in some device's rows an owner is named by exactly 16.
All inputs are finite; a program needn't handle non-finite values. No bound on the sum of `negative_mask` on one device may be relied on, other than what follows from the above.
Results may differ from a plain program's by a relative error of at most 0.015.
Values may be sent and summed in bfloat16 or wider, within the bound.
No kernel may reach another device: no remote copies, remote signals or barrier semaphores. Data moves between devices by JAX's collectives and lax.ppermute only.
A program may use at most 128 MiB of HBM per device.

v0:
```python
import jax
import jax.numpy as jnp
from jax import lax
from jax.sharding import PartitionSpec as P

BLOCK = 128
BLK_DEV = 8


def body(
    hidden,
    output_weight,
    owners,
    negatives,
    negative_mask,
    target_block,
    target_word,
    log_norm,
    cotangent,
):
    token_total, model_width = hidden.shape
    visits = owners.shape[1]
    owner_count = lax.axis_size("vocab")
    owner_words = output_weight.shape[1]
    capacity = max(2, token_total * visits * 4 // (3 * owner_count))
    entries = token_total * visits
    slot_total = owner_count * capacity
    flat_owner = owners.reshape(entries)
    owner_hot = (flat_owner[:, None] == jnp.arange(owner_count, dtype=jnp.int32)[None, :]).astype(
        jnp.int32
    )
    earlier = jnp.cumsum(owner_hot, axis=0) - owner_hot
    position = jnp.sum(earlier * owner_hot, axis=1)
    slot_index = flat_owner * capacity + position
    entry_ids = jnp.arange(entries, dtype=jnp.int32)
    token_of = entry_ids // visits
    is_first = entry_ids % visits == 0
    cluster_ids = jnp.arange(BLK_DEV, dtype=jnp.int32)
    negative_flat = negatives.reshape(entries, -1)
    mask_flat = negative_mask.reshape(entries, -1)
    target_here = jnp.where(is_first, target_block[token_of], -1)
    matched = (negative_flat[:, :, None] == cluster_ids[None, None, :]) & (
        mask_flat[:, :, None] == 1
    )
    cluster_counts = jnp.sum(jnp.where(matched, 1.0, 0.0), axis=1) + jnp.where(
        target_here[:, None] == cluster_ids[None, :], 1.0, 0.0
    )
    scalars = jnp.stack(
        [
            cotangent[token_of].astype(jnp.float32),
            log_norm[token_of].astype(jnp.float32),
            target_here.astype(jnp.float32),
            target_word[token_of].astype(jnp.float32),
        ],
        axis=1,
    )
    row_meta = jnp.concatenate([cluster_counts, scalars], axis=1).astype(jnp.bfloat16)
    send_meta = (
        jnp.zeros((slot_total, row_meta.shape[1]), jnp.bfloat16)
        .at[slot_index]
        .set(row_meta)
        .reshape(owner_count, capacity, -1)
    )
    send_rows = (
        jnp.zeros((slot_total, model_width), jnp.bfloat16)
        .at[slot_index]
        .set(hidden[token_of])
        .reshape(owner_count, capacity, model_width)
    )
    got_rows, got_meta = (
        lax.all_to_all(send_rows, "vocab", split_axis=0, concat_axis=0, tiled=True),
        lax.all_to_all(send_meta, "vocab", split_axis=0, concat_axis=0, tiled=True),
    )
    arrived_rows = got_rows.reshape(slot_total, model_width)
    arrived_meta = got_meta.reshape(slot_total, -1).astype(jnp.float32)
    scores = jnp.dot(arrived_rows, output_weight, preferred_element_type=jnp.float32)
    word_counts = jnp.broadcast_to(
        arrived_meta[:, :BLK_DEV, None], (slot_total, BLK_DEV, BLOCK)
    ).reshape(slot_total, owner_words)
    token_weight = arrived_meta[:, BLK_DEV]
    log_total = arrived_meta[:, BLK_DEV + 1]
    target_col = arrived_meta[:, BLK_DEV + 2] * BLOCK + arrived_meta[:, BLK_DEV + 3]
    word_position = jnp.arange(owner_words).astype(jnp.float32)
    target_hot = jnp.where(word_position[None, :] == target_col[:, None], 1.0, 0.0)
    score_grad = (
        token_weight[:, None] * (word_counts * jnp.exp(scores - log_total[:, None]) - target_hot)
    ).astype(jnp.bfloat16)
    grad_rows = lax.dot_general(
        score_grad, output_weight, (((1,), (1,)), ((), ())), preferred_element_type=jnp.float32
    )
    grad_rows = grad_rows.astype(jnp.bfloat16).reshape(owner_count, capacity, model_width)
    returned = lax.all_to_all(grad_rows, "vocab", split_axis=0, concat_axis=0, tiled=True)
    per_entry = returned.reshape(slot_total, model_width)[slot_index].astype(jnp.float32)
    hidden_grad = jnp.sum(per_entry.reshape(token_total, visits, model_width), axis=1).astype(
        jnp.bfloat16
    )
    weight_grad = lax.psum_scatter(
        lax.dot_general(
            arrived_rows, score_grad, (((0,), (0,)), ((), ())), preferred_element_type=jnp.float32
        ).astype(jnp.bfloat16),
        "dp",
        scatter_dimension=0,
        tiled=True,
    )
    return (hidden_grad, weight_grad)


def solution(mesh):
    placed = (
        P(("dp", "vocab"), None),
        P(None, "vocab"),
        P(("dp", "vocab"), None),
        P(("dp", "vocab"), None, None),
        P(("dp", "vocab"), None, None),
        P(("dp", "vocab")),
        P(("dp", "vocab")),
        P(("dp", "vocab")),
        P(("dp", "vocab")),
    )
    return jax.shard_map(
        body,
        mesh=mesh,
        in_specs=placed,
        out_specs=(P(("dp", "vocab"), None), P("dp", "vocab")),
        check_vma=False,
    )
```

profile of v0, /device:TPU:192, one launch (start us, length us, event | category | flops | bytes accessed | tf_op | source)
XLA Modules:
  0.0 235.6 jit_solution(5269171881956278782)
XLA Ops:
  7.3 3.5 %gather_fusion = s32[384]{0:T(512)S(1)} fusion(s32[128]{0:T(128)} %param.14, s32[1024]{0:T(1024)S(1)} %pad_clamp_fusion.1), kind=kCustom, calls=%fused_computation | custom fusion | bytes 4608 | tf_op jit(solution)/shard_map/gather | solution.py:41
  10.8 0.8 copy.59
  11.6 0.2 eq.103
  11.8 0.2 eq.99
  12.0 0.7 broadcast_multiply_fusion
  12.7 0.8 copy.62
  13.5 0.2 eq.107
  13.7 0.7 broadcast_compare_fusion
  14.4 0.2 copy.63
  14.6 0.2 eq.113
  14.8 2.7 %gather_fusion.3 = s32[384]{0:T(512)S(1)} fusion(s32[128]{0:T(128)S(1)} %copy-done.1, s32[1024]{0:T(1024)S(1)} %pad_clamp_fusion.1), kind=kCustom, calls=%fused_computation.3 | custom fusion | bytes 4608 | tf_op jit(solution)/shard_map/gather | solution.py:53
  17.6 2.7 %gather_fusion.1 = bf16[384]{0:T(512)(128)(2,1)S(1)} fusion(bf16[128]{0:T(256)(128)(2,1)S(1)} %copy-done.2, s32[1024]{0:T(1024)S(1)} %pad_clamp_fusion.1), kind=kCustom, calls=%fused_computation.1 | custom fusion | bytes 3072 | tf_op jit(solution)/shard_map/gather | solution.py:50
  20.3 2.7 %gather_fusion.2 = bf16[384]{0:T(512)(128)(2,1)S(1)} fusion(bf16[128]{0:T(256)(128)(2,1)S(1)} %copy-done.3, s32[1024]{0:T(1024)S(1)} %pad_clamp_fusion.1), kind=kCustom, calls=%fused_computation.2 | custom fusion | bytes 3072 | tf_op jit(solution)/shard_map/gather | solution.py:51
  23.3 0.9 reduce-window.6
  24.1 0.2 slice_reduce_fusion
  24.5 0.2 mul.41
  24.9 1.5 scatter_custom_fusion
  26.4 0.9 copy.66
  27.3 7.8 %all-to-all-start = ((bf16[32,16,12]{1,2,0:T(8,128)(2,1)}), bf16[32,16,12]{1,2,0:T(8,128)(2,1)S(1)}, u32[]{:S(2)}, u32[]{:S(2)}) async-start(bf16[32,16,12]{1,2,0:T(8,128)(2,1)} %copy.66), calls=%async_computation | async-start | bytes 262144 | tf_op jit(solution)/shard_map/all_to_all | solution.py:72
  35.2 16.6 %scatter_custom_fusion.1 = bf16[512,4096]{1,0:T(8,128)(2,1)} fusion(s32[384]{0:T(512)S(1)} %fusion.34, bf16[128,4096]{1,0:T(8,128)(2,1)S(1)} %copy-done, s32[1024]{0:T(1024)S(1)} %pad_clamp_fusion.1, bf16[]{:T(256)} %constant.15.clone.1), kind=kCustom, calls=%fused_computation.10 | custom fusion | bytes 4194306 | tf_op jit(solution)/shard_map/scatter | solution.py:67
  51.8 7.6 %all-to-all-start.1 = ((bf16[32,16,4096]{2,1,0:T(8,128)(2,1)}), bf16[32,16,4096]{2,1,0:T(8,128)(2,1)}, u32[]{:S(2)}, u32[]{:S(2)}) async-start(bf16[32,16,4096]{2,1,0:T(8,128)(2,1)} %bitcast.49), calls=%async_computation.1 | async-start | bytes 8388608 | tf_op jit(solution)/shard_map/all_to_all | solution.py:71
  60.0 52.9 %all-to-all-done.1 = bf16[32,16,4096]{2,1,0:T(8,128)(2,1)} async-done(((bf16[32,16,4096]{2,1,0:T(8,128)(2,1)}), bf16[32,16,4096]{2,1,0:T(8,128)(2,1)}, u32[]{:S(2)}, u32[]{:S(2)}) %all-to-all-start.1) | async-done | bytes 4194336 | tf_op jit(solution)/shard_map/all_to_all | solution.py:71
  112.9 8.3 %fusion.40 = f32[512,1024]{1,0:T(8,128)S(1)} fusion(bf16[512,4096]{1,0:T(8,128)(2,1)} %bitcast.4, bf16[4096,1024]{1,0:T(8,128)(2,1)} %param.10), kind=kOutput, calls=%fused_computation.77 | convolution fusion | flops 4294967296 | bytes 14680064 | tf_op jit(solution)/shard_map/dot_general | solution.py:76
  121.2 0.6 broadcast_in_dim.57
  121.8 0.7 copy-done.4
  122.6 9.7 %convolution_convert_fusion = bf16[4096,1024]{1,0:T(8,128)(2,1)} fusion(bf16[512,4096]{1,0:T(8,128)(2,1)} %bitcast.4, f32[64,8,8,128]{3,2,1,0:T(8,128)S(1)} %bitcast.51, f32[512,1024]{1,0:T(8,128)S(1)} %fusion.40, f32[1024]{0:T(1024)S(1)} %iota_convert_fusion, f32[512]{0:T(512)S(1)} %bitcast.57, f32[512]{0:T(512)S(1)} %bitcast.59, f32[512]{0:T(512)S(1)} %bitcast.55), kind=kOutput, calls=%fused_computation.8 | convolution fusion | flops 4302831616 | bytes 16787456 | tf_op jit(solution)/shard_map/dot_general | solution.py:98
  132.3 10.9 %convolution_convert_fusion.1 = bf16[512,4096]{1,0:T(8,128)(2,1)} fusion(bf16[4096,1024]{1,0:T(8,128)(2,1)} %param.10, f32[64,8,8,128]{3,2,1,0:T(8,128)S(1)} %bitcast.52, f32[512,1024]{1,0:T(8,128)} %copy-done.4, f32[1024]{0:T(1024)S(1)} %iota_convert_fusion, f32[512]{0:T(512)S(1)} %bitcast.58, f32[512]{0:T(512)S(1)} %bitcast.60, f32[512]{0:T(512)S(1)} %bitcast.56), kind=kOutput, calls=%fused_computation.9 | convolution fusion | flops 4300734464 | bytes 16787456 | tf_op jit(solution)/shard_map/dot_general | solution.py:88
  143.2 5.1 %all-to-all-start.2 = ((bf16[32,16,4096]{2,1,0:T(8,128)(2,1)}), bf16[32,16,4096]{2,1,0:T(8,128)(2,1)}, u32[]{:S(2)}, u32[]{:S(2)}) async-start(bf16[32,16,4096]{2,1,0:T(8,128)(2,1)} %bitcast.50), calls=%async_computation.2 | async-start | bytes 8388608 | tf_op jit(solution)/shard_map/all_to_all | solution.py:92
  148.3 53.4 %all-to-all-done.2 = bf16[32,16,4096]{2,1,0:T(8,128)(2,1)} async-done(((bf16[32,16,4096]{2,1,0:T(8,128)(2,1)}), bf16[32,16,4096]{2,1,0:T(8,128)(2,1)}, u32[]{:S(2)}, u32[]{:S(2)}) %all-to-all-start.2) | async-done | bytes 4194336 | tf_op jit(solution)/shard_map/all_to_all | solution.py:92
  201.7 11.1 %gather_fusion.4 = bf16[384,4096]{1,0:T(8,128)(2,1)} fusion(bf16[512,4096]{1,0:T(8,128)(2,1)} %bitcast.8, s32[1024]{0:T(1024)S(1)} %pad_clamp_fusion), kind=kCustom, calls=%fused_computation.5 | custom fusion | bytes 6292992 | tf_op jit(solution)/shard_map/gather | solution.py:93
  212.8 7.1 %gather.29 = bf16[128,3,4096]{2,1,0:T(4,128)(2,1)} reshape(bf16[384,4096]{1,0:T(8,128)(2,1)} %gather_fusion.4) | data formatting | bytes 6291456 | tf_op jit(solution)/shard_map/gather | solution.py:93
  219.9 8.6 %reduce_sum.35 = bf16[128,4096]{1,0:T(8,128)(2,1)} reduce(bf16[128,3,4096]{2,1,0:T(4,128)(2,1)} %gather.29, bf16[]{:T(256)} %constant.15.clone.1), dimensions={1}, to_apply=%region_6.7 | reduce | flops 1048576 | bytes 4194306 | tf_op jit(solution)/shard_map/reduce_sum | solution.py:94
  (38 shorter events, 1.2 us)
Async XLA Ops:
  7.2 28.0 %copy-start = (bf16[128,4096]{1,0:T(8,128)(2,1)S(1)}, bf16[128,4096]{1,0:T(8,128)(2,1)}, u32[]{:S(2)}) copy-start(bf16[128,4096]{1,0:T(8,128)(2,1)} %param.9) | copy-start | bytes 3145732
  7.2 7.7 %copy-start.1 = (s32[128]{0:T(128)S(1)}, s32[128]{0:T(128)}, u32[]{:S(2)}) copy-start(s32[128]{0:T(128)} %param.15) | copy-start | bytes 1540
  7.2 10.4 %copy-start.2 = (bf16[128]{0:T(256)(128)(2,1)S(1)}, bf16[128]{0:T(256)(128)(2,1)}, u32[]{:S(2)}) copy-start(bf16[128]{0:T(256)(128)(2,1)} %param.17) | copy-start | bytes 772
  7.2 13.1 %copy-start.3 = (bf16[128]{0:T(256)(128)(2,1)S(1)}, bf16[128]{0:T(256)(128)(2,1)}, u32[]{:S(2)}) copy-start(bf16[128]{0:T(256)(128)(2,1)} %param.16) | copy-start | bytes 772
  27.3 24.5 %all-to-all-start = ((bf16[32,16,12]{1,2,0:T(8,128)(2,1)}), bf16[32,16,12]{1,2,0:T(8,128)(2,1)S(1)}, u32[]{:S(2)}, u32[]{:S(2)}) async-start(bf16[32,16,12]{1,2,0:T(8,128)(2,1)} %copy.66), calls=%async_computation | async-start | bytes 262144 | tf_op jit(solution)/shard_map/all_to_all | solution.py:72
  51.8 61.1 %all-to-all-start.1 = ((bf16[32,16,4096]{2,1,0:T(8,128)(2,1)}), bf16[32,16,4096]{2,1,0:T(8,128)(2,1)}, u32[]{:S(2)}, u32[]{:S(2)}) async-start(bf16[32,16,4096]{2,1,0:T(8,128)(2,1)} %bitcast.49), calls=%async_computation.1 | async-start | bytes 8388608 | tf_op jit(solution)/shard_map/all_to_all | solution.py:71
  59.4 169.1 %reduce-scatter.2.cloned.1.call-start = ((), (), s32[]{:S(2)}) async-start(), calls=%async_computation.4 | async-start | bytes 9437184 | tf_op jit(solution)/shard_map/reduce_scatter | solution.py:97
  121.2 1.4 copy-start.4
  143.2 58.6 %all-to-all-start.2 = ((bf16[32,16,4096]{2,1,0:T(8,128)(2,1)}), bf16[32,16,4096]{2,1,0:T(8,128)(2,1)}, u32[]{:S(2)}, u32[]{:S(2)}) async-start(bf16[32,16,4096]{2,1,0:T(8,128)(2,1)} %bitcast.50), calls=%async_computation.2 | async-start | bytes 8388608 | tf_op jit(solution)/shard_map/all_to_all | solution.py:92
Sparse Core Ops, SparseCore 0:
  132.4 89.1 reduce-scatter.1
where the time goes:
time: 240 us; the launch traced here: 236 us
  waiting for transfers between devices  106 us (44%)
  local copies, waits for them, and re-layouts  54.1 us (23%)
  matrix products  28.9 us (12%)
  starting transfers between devices  20.6 us (9%)
  between operations  14.6 us (6%)
  other arithmetic  11.1 us (5%)
    all_to_all x1, waiting for transfers between devices, body(): lax.all_to_all(grad_rows, 'vocab', split_axis=0, concat_axis=0, tiled=True)  53.4 us
    all_to_all x1, waiting for transfers between devices, body(): lax.all_to_all(send_rows, 'vocab', split_axis=0, concat_axis=0, tiled=True)  52.9 us
    gather x2, local copies, waits for them, and re-layouts, body(): returned.reshape(slot_total, model_width)[slot_index].astype(jnp.float32)  18.2 us
    scatter x1, local copies, waits for them, and re-layouts, body(): send_rows = jnp.zeros((slot_total, model_width), jnp.bfloat16).at[slot_in...  16.6 us
    dot_general x1, matrix products, body(): lax.dot_general(score_grad, output_weight, (((1,), (1,)), ((), ())), pref...  10.9 us
    dot_general x1, matrix products, body(): lax.dot_general(arrived_rows, score_grad, (((0,), (0,)), ((), ())), prefe...  9.66 us
    reduce_sum x1, other arithmetic, body(): jnp.sum(per_entry.reshape(token_total, visits, model_width), axis=1)  8.6 us
    dot_general x1, matrix products, body(): jnp.dot(arrived_rows, output_weight, preferred_element_type=jnp.float32)  8.35 us
  transfers between devices with their start and end apart: 4, of which 2 were waited for; matrix products, arithmetic and copies ran while one was open for 23% of the time, Pallas kernels for 0%

commit v1 on v0

v1 whole, which is shorter than its diff:
```python
import jax
import jax.numpy as jnp
from jax import lax
from jax.sharding import PartitionSpec as P

BLOCK = 128
BLK_DEV = 8
META = 128


def body(
    hidden,
    output_weight,
    owners,
    negatives,
    negative_mask,
    target_block,
    target_word,
    log_norm,
    cotangent,
):
    tokens, width = hidden.shape
    visits = owners.shape[1]
    peers = lax.axis_size("vocab")
    words = output_weight.shape[1]
    capacity = max(2, tokens * visits * 4 // (3 * peers))
    slots = peers * capacity
    entries = visits * tokens

    owner = owners.T.reshape(entries)
    owner_hot = owner[:, None] == jnp.arange(peers, dtype=jnp.int32)[None, :]
    entry = jnp.arange(entries, dtype=jnp.int32)
    before = (entry[None, :] < entry[:, None]).astype(jnp.bfloat16)
    earlier = jnp.dot(before, owner_hot.astype(jnp.bfloat16), preferred_element_type=jnp.float32)
    position = jnp.sum(jnp.where(owner_hot, earlier, 0.0), axis=1).astype(jnp.int32)
    slot = owner * capacity + position
    slot_ids = jnp.arange(slots, dtype=jnp.int32)
    place = (slot_ids[:, None] == slot[None, :]).astype(jnp.bfloat16)
    place_token = sum(place[:, v * tokens : (v + 1) * tokens] for v in range(visits))

    cluster = jnp.arange(BLK_DEV, dtype=jnp.int32)
    counts = jnp.sum(
        jnp.where((negatives[..., None] == cluster) & (negative_mask[..., None] == 1), 1.0, 0.0), axis=2
    )
    target_hot = jnp.where(target_block[:, None] == cluster[None, :], 1.0, 0.0)
    counts = counts.at[:, 0].add(target_hot)
    counts = counts.transpose(1, 0, 2).reshape(entries, BLK_DEV)
    first = entry < tokens
    block_here = jnp.where(first, jnp.tile(target_block, visits), -1)
    scalars = jnp.stack(
        [
            jnp.tile(cotangent, visits).astype(jnp.float32),
            jnp.tile(log_norm, visits).astype(jnp.float32),
            block_here.astype(jnp.float32),
            jnp.tile(target_word, visits).astype(jnp.float32),
        ],
        axis=1,
    )
    meta = jnp.concatenate([counts, scalars], axis=1).astype(jnp.bfloat16)
    meta = jnp.pad(meta, ((0, 0), (0, META - meta.shape[1])))

    send = jnp.concatenate(
        [
            jnp.dot(place_token, hidden, preferred_element_type=jnp.float32).astype(jnp.bfloat16),
            jnp.dot(place, meta, preferred_element_type=jnp.float32).astype(jnp.bfloat16),
        ],
        axis=1,
    ).reshape(peers, capacity, width + META)
    got = lax.all_to_all(send, "vocab", split_axis=0, concat_axis=0, tiled=True)
    got = got.reshape(slots, width + META)
    rows = got[:, :width]
    info = got[:, width:].astype(jnp.float32)

    scores = jnp.dot(rows, output_weight, preferred_element_type=jnp.float32)
    word_counts = jnp.broadcast_to(info[:, :BLK_DEV, None], (slots, BLK_DEV, BLOCK)).reshape(slots, words)
    token_weight = info[:, BLK_DEV]
    log_total = info[:, BLK_DEV + 1]
    target_col = info[:, BLK_DEV + 2] * BLOCK + info[:, BLK_DEV + 3]
    word_position = jnp.arange(words).astype(jnp.float32)
    hit = jnp.where(word_position[None, :] == target_col[:, None], 1.0, 0.0)
    score_grad = (
        token_weight[:, None]
        * (jnp.where(word_counts > 0, word_counts * jnp.exp(scores - log_total[:, None]), 0.0) - hit)
    ).astype(jnp.bfloat16)
    weight_part = lax.dot_general(
        rows, score_grad, (((0,), (0,)), ((), ())), preferred_element_type=jnp.float32
    ).astype(jnp.bfloat16)
    weight_grad = lax.psum_scatter(weight_part, "dp", scatter_dimension=0, tiled=True)
    part = lax.dot_general(
        score_grad, output_weight, (((1,), (1,)), ((), ())), preferred_element_type=jnp.float32
    ).astype(jnp.bfloat16)
    back = lax.all_to_all(
        part.reshape(peers, capacity, width), "vocab", split_axis=0, concat_axis=0, tiled=True
    ).reshape(slots, width)
    hidden_grad = lax.dot_general(
        place_token, back, (((0,), (0,)), ((), ())), preferred_element_type=jnp.float32
    ).astype(jnp.bfloat16)
    return (hidden_grad, weight_grad)


def solution(mesh):
    placed = (
        P(("dp", "vocab"), None),
        P(None, "vocab"),
        P(("dp", "vocab"), None),
        P(("dp", "vocab"), None, None),
        P(("dp", "vocab"), None, None),
        P(("dp", "vocab")),
        P(("dp", "vocab")),
        P(("dp", "vocab")),
        P(("dp", "vocab")),
    )
    return jax.shard_map(
        body,
        mesh=mesh,
        in_specs=placed,
        out_specs=(P(("dp", "vocab"), None), P("dp", "vocab")),
        check_vma=False,
    )
```

time: 240 us -> 202 us (0.84)
  the two profiles are of different devices: /device:TPU:192 before, /device:TPU:98 now
where the time goes in v1:
time: 202 us; the launch traced here: 199 us
  waiting for transfers between devices  80.2 us (40%)
  blocking collectives  55.2 us (27%)
  matrix products  31 us (15%)
  between operations  14.1 us (7%)
  starting transfers between devices  7.89 us (4%)
  other arithmetic  7.43 us (4%)
  local copies, waits for them, and re-layouts  3.36 us (2%)
    all_to_all x1, blocking collectives, body(): lax.all_to_all(part.reshape(peers, capacity, width), 'vocab', split_axis=...  55.2 us
    all_to_all x1, waiting for transfers between devices, body(): got = lax.all_to_all(send, 'vocab', split_axis=0, concat_axis=0, tiled=True)  52.6 us
    reduce_scatter x1, waiting for transfers between devices, body(): lax.psum_scatter(weight_part, 'dp', scatter_dimension=0, tiled=True)  27.6 us
    dot_general x1, matrix products, body(): lax.dot_general(rows, score_grad, (((0,), (0,)), ((), ())), preferred_ele...  9.61 us
    dot_general x1, matrix products, body(): lax.dot_general(score_grad, output_weight, (((1,), (1,)), ((), ())), pref...  9.05 us
    dot_general x1, matrix products, body(): scores = jnp.dot(rows, output_weight, preferred_element_type=jnp.float32)  8.16 us
    all_to_all x1, starting transfers between devices, body(): got = lax.all_to_all(send, 'vocab', split_axis=0, concat_axis=0, tiled=True)  7.67 us
  transfers between devices with their start and end apart: 2, of which 2 were waited for; matrix products, arithmetic and copies ran while one was open for 5% of the time, Pallas kernels for 0%

profile of v1, /device:TPU:98, one launch (start us, length us, event | category | flops | bytes accessed | tf_op | source)
XLA Modules:
  0.0 199.2 jit_solution(3962255268743630090)
XLA Ops:
  7.2 0.0 copy-start
  7.2 0.7 convert_convert_fusion
  7.9 0.7 broadcast_bitcast_fusion.2
  8.6 0.7 broadcast_bitcast_fusion.3
  9.3 0.7 broadcast_compare_fusion
  9.9 1.0 fusion.9
  10.9 0.7 convert_add_fusion
  11.6 0.7 broadcast_bitcast_fusion
  12.3 0.7 select_reduce_fusion
  13.0 0.7 fusion.28
  13.6 0.1 fusion.22
  13.8 0.3 convolution_convert_fusion.4
  14.1 0.0 copy-done
  14.1 1.2 convolution_convert_fusion.2
  15.3 2.3 %pad_maximum_fusion = bf16[512,4224]{1,0:T(8,128)(2,1)} fusion(bf16[512,128]{1,0:T(8,128)(2,1)S(1)} %convolution_convert_fusion.4, bf16[512,4096]{1,0:T(8,128)(2,1)S(1)} %convolution_convert_fusion.2), kind=kLoop, calls=%fused_computation.4 | loop fusion | flops 8650752 | bytes 8650752 | tf_op jit(solution)/shard_map/concatenate | solution.py:62
  17.6 7.7 %all-to-all-start = ((bf16[32,16,4224]{2,1,0:T(8,128)(2,1)}), bf16[32,16,4224]{2,1,0:T(8,128)(2,1)}, u32[]{:S(2)}, u32[]{:S(2)}) async-start(bf16[32,16,4224]{2,1,0:T(8,128)(2,1)} %bitcast.58), calls=%async_computation | async-start | bytes 8650752 | tf_op jit(solution)/shard_map/all_to_all | solution.py:69
  25.3 0.2 reduce-scatter.2.cloned.1.call-start
  25.6 52.6 %all-to-all-done = bf16[32,16,4224]{2,1,0:T(8,128)(2,1)} async-done(((bf16[32,16,4224]{2,1,0:T(8,128)(2,1)}), bf16[32,16,4224]{2,1,0:T(8,128)(2,1)}, u32[]{:S(2)}, u32[]{:S(2)}) %all-to-all-start) | async-done | bytes 4325408 | tf_op jit(solution)/shard_map/all_to_all | solution.py:69
  78.2 0.9 slice_convert_fusion
  79.1 0.6 fusion.24
  79.7 8.2 %fusion.1 = f32[512,1024]{1,0:T(8,128)S(1)} fusion(bf16[4096,1024]{1,0:T(8,128)(2,1)} %param.12, bf16[512,4224]{1,0:T(8,128)(2,1)} %bitcast.6), kind=kOutput, calls=%fused_computation.6 | convolution fusion | flops 4294967296 | bytes 14680064 | tf_op jit(solution)/shard_map/dot_general | solution.py:74
  87.8 0.0 copy-start.1
  87.8 0.6 broadcast_in_dim.56
  88.4 0.7 copy-done.1
  89.1 9.6 %convolution_convert_fusion = bf16[4096,1024]{1,0:T(8,128)(2,1)} fusion(bf16[512,4224]{1,0:T(8,128)(2,1)} %bitcast.6, f32[512,1024]{1,0:T(8,128)S(1)} %fusion.1, f32[64,8,8,128]{3,2,1,0:T(8,128)S(1)} %bitcast.62, f32[1024]{0:T(1024)S(1)} %iota_convert_fusion, f32[512]{0:T(512)S(1)} %get-tuple-element.15, f32[512]{0:T(512)S(1)} %get-tuple-element.16, ...), kind=kOutput, calls=%fused_computation | convolution fusion | flops 4303880192 | bytes 16787456 | tf_op jit(solution)/shard_map/dot_general | solution.py:85
  98.8 0.0 reduce-scatter.2.cloned.1.call-update
  98.8 9.1 %convolution_convert_fusion.1 = bf16[512,4096]{1,0:T(8,128)(2,1)S(1)} fusion(bf16[4096,1024]{1,0:T(8,128)(2,1)} %param.12, f32[512,1024]{1,0:T(8,128)} %copy-done.1, f32[64,8,8,128]{3,2,1,0:T(8,128)S(1)} %bitcast.63, f32[1024]{0:T(1024)S(1)} %iota_convert_fusion, f32[512]{0:T(512)S(1)} %get-tuple-element.15, f32[512]{0:T(512)S(1)} %get-tuple-element.16, ...), kind=kOutput, calls=%fused_computation.1 | convolution fusion | flops 4301783040 | bytes 16787456 | tf_op jit(solution)/shard_map/dot_general | solution.py:89
  107.8 55.2 %all_to_all.10 = bf16[32,16,4096]{2,1,0:T(8,128)(2,1)S(1)} all-to-all(bf16[32,16,4096]{2,1,0:T(8,128)(2,1)S(1)} %bitcast.61), channel_id=1, replica_groups=mesh['dp'=8,'vocab'=32] {'vocab'}, dimensions={0} | all-to-all | bytes 8388608 | tf_op jit(solution)/shard_map/all_to_all | solution.py:92
  163.1 1.7 convolution_convert_fusion.3
  164.8 27.6 %reduce-scatter.2.cloned.1.call-done = bf16[512,1024]{1,0:T(8,128)(2,1)} async-done(((bf16[4096,1024]{1,0:T(8,128)(2,1)}), bf16[512,1024]{1,0:T(8,128)(2,1)}) %reduce-scatter.2.cloned.1.call-update) | async-done | bytes 1048592 | tf_op jit(solution)/shard_map/reduce_scatter | solution.py:88
  (7 shorter events, 0.1 us)
Async XLA Ops:
  7.2 6.9 %copy-start = (bf16[128,4096]{1,0:T(8,128)(2,1)S(1)}, bf16[128,4096]{1,0:T(8,128)(2,1)}, u32[]{:S(2)}) copy-start(bf16[128,4096]{1,0:T(8,128)(2,1)} %param.11) | copy-start | bytes 3145732
  17.6 60.5 %all-to-all-start = ((bf16[32,16,4224]{2,1,0:T(8,128)(2,1)}), bf16[32,16,4224]{2,1,0:T(8,128)(2,1)}, u32[]{:S(2)}, u32[]{:S(2)}) async-start(bf16[32,16,4224]{2,1,0:T(8,128)(2,1)} %bitcast.58), calls=%async_computation | async-start | bytes 8650752 | tf_op jit(solution)/shard_map/all_to_all | solution.py:69
  25.3 167.1 %reduce-scatter.2.cloned.1.call-start = ((), (), s32[]{:S(2)}) async-start(), calls=%async_computation.3 | async-start | bytes 9437184 | tf_op jit(solution)/shard_map/reduce_scatter | solution.py:88
  87.8 1.3 copy-start.1
Sparse Core Ops, SparseCore 0:
  98.9 93.4 reduce-scatter.1

commit v2 on v1

v2 whole, which is shorter than its diff:
```python
import functools

import jax
import jax.numpy as jnp
from jax import lax
from jax.experimental import pallas as pl
from jax.experimental.pallas import tpu as pltpu
from jax.sharding import PartitionSpec as P

BLOCK = 128
BLK_DEV = 8
META = 128
GAP = 2
NEAR, STATE, ADD, SUM = 0, 0, 0, 0
MIB = 1 << 20
F32 = jnp.float32
BF16 = jnp.bfloat16
CONTRACT_ROWS = (((0,), (0,)), ((), ()))
CONTRACT_COLS = (((1,), (1,)), ((), ()))


def cost(us):
    return pl.CostEstimate(flops=0, bytes_accessed=int(us * 3.69e6), transcendentals=0)


def params(mib):
    return pltpu.CompilerParams(vmem_limit_bytes=mib * MIB)


def place_kernel(
    capacity,
    hidden_ref,
    owners_ref,
    negatives_ref,
    mask_ref,
    block_ref,
    word_ref,
    norm_ref,
    cot_ref,
    send_ref,
    place_ref,
    send,
    sems,
):
    tokens, width = hidden_ref.shape
    visits, picks = negatives_ref.shape[:2]
    slots = send_ref.shape[0]
    peers = slots // capacity
    owner_iota = lax.broadcasted_iota(jnp.int32, (peers, tokens), 0)
    row = lax.broadcasted_iota(jnp.int32, (tokens, tokens), 0)
    col = lax.broadcasted_iota(jnp.int32, (tokens, tokens), 1)
    before = jnp.where(row < col, 1.0, 0.0).astype(BF16)
    slot_iota = lax.broadcasted_iota(jnp.int32, (slots, tokens), 0)
    cluster = lax.broadcasted_iota(jnp.int32, (BLK_DEV, tokens), 0)
    carried = jnp.zeros((peers, 1), F32)
    block = block_ref[...]
    total = jnp.zeros((slots, tokens), F32)
    info = jnp.zeros((slots, META), F32)
    for v in range(visits):
        owner = owners_ref[v : v + 1, :]
        hot = jnp.where(owner_iota == owner, 1.0, 0.0)
        earlier = jnp.dot(hot.astype(BF16), before, preferred_element_type=F32) + carried
        carried = carried + jnp.sum(hot, axis=1, keepdims=True)
        position = jnp.sum(hot * earlier, axis=0, keepdims=True).astype(jnp.int32)
        place = jnp.where(slot_iota == owner * capacity + position, 1.0, 0.0)
        total = total + place
        counts = jnp.zeros((BLK_DEV, tokens), F32)
        for n in range(picks):
            used = mask_ref[v, n : n + 1, :] == 1
            counts += jnp.where((cluster == negatives_ref[v, n : n + 1, :]) & used, 1.0, 0.0)
        if v == 0:
            counts += jnp.where(cluster == block, 1.0, 0.0)
            here = block.astype(F32)
        else:
            here = jnp.full((1, tokens), -1.0, F32)
        tail = jnp.zeros((META - BLK_DEV - 4, tokens), F32)
        meta = jnp.concatenate(
            [
                counts,
                cot_ref[...].astype(F32),
                norm_ref[...].astype(F32),
                here,
                word_ref[...].astype(F32),
                tail,
            ],
            axis=0,
        ).astype(BF16)
        info += lax.dot_general(
            place.astype(BF16), meta, CONTRACT_COLS, preferred_element_type=F32
        )
    place_tokens = total.astype(BF16)
    place_ref[...] = place_tokens
    send[:, width:] = info.astype(BF16)
    step = 512
    stores = []
    for k, c in enumerate(range(0, width, step)):
        send[:, c : c + step] = jnp.dot(
            place_tokens, hidden_ref[:, c : c + step], preferred_element_type=F32
        ).astype(BF16)
        cut = pl.ds(c, step + META if c + step == width else step)
        stores.append(pltpu.make_async_copy(send.at[:, cut], send_ref.at[:, cut], sems.at[k]))
        stores[-1].start()
    for store in stores:
        store.wait()


def score_kernel(
    chunks_ref, got_ref, weight_ref, grad_ref, up_ref, down_ref, token_ref, rows, weight, meta, acc, sems
):
    steps, _, depth = rows.shape
    loads = []
    for k in range(steps):
        cut = pl.ds(k * depth, depth)
        loads.append(
            (
                pltpu.make_async_copy(got_ref.at[:, cut], rows.at[k], sems.at[0, k]),
                pltpu.make_async_copy(weight_ref.at[cut, :], weight.at[k], sems.at[1, k]),
            )
        )
    last = pltpu.make_async_copy(got_ref.at[:, pl.ds(steps * depth, META)], meta, sems.at[2, 0])
    for pair in loads:
        for load in pair:
            load.start()
    last.start()
    for k, pair in enumerate(loads):
        for load in pair:
            load.wait()
        part = jnp.dot(rows[k], weight[k], preferred_element_type=F32)
        if k == 0:
            acc[...] = part
        else:
            acc[...] += part
    last.wait()
    info = meta[...].astype(F32)
    lane = lax.broadcasted_iota(jnp.int32, (1, BLOCK), 1).astype(F32)
    scale = info[:, BLK_DEV : BLK_DEV + 1]
    norm = info[:, BLK_DEV + 1 : BLK_DEV + 2]
    target = info[:, BLK_DEV + 2 : BLK_DEV + 3] * BLOCK + info[:, BLK_DEV + 3 : BLK_DEV + 4]
    for b in range(BLK_DEV):
        count = info[:, b : b + 1]
        words = slice(b * BLOCK, (b + 1) * BLOCK)
        soft = jnp.where(count > 0, count * jnp.exp(acc[:, words] - norm), 0.0)
        hit = jnp.where(lane + (b * BLOCK) == target, 1.0, 0.0)
        grad_ref[:, words] = (scale * (soft - hit)).astype(BF16)
    half = up_ref.shape[1]
    first = lax.dot_general(
        rows[chunks_ref[steps // 2]], grad_ref[...], CONTRACT_ROWS, preferred_element_type=F32
    )
    up_ref[...] = first[:, :half].astype(BF16)
    down_ref[...] = first[:, half:].astype(BF16)
    token_ref[...] = jnp.zeros_like(token_ref)


def pair_kernel(chunks_ref, rows_up_ref, rows_down_ref, grad_ref, up_ref, down_ref):
    half = up_ref.shape[1]
    up_ref[...] = lax.dot_general(
        rows_up_ref[...], grad_ref[:, half:], CONTRACT_ROWS, preferred_element_type=F32
    ).astype(BF16)
    down_ref[...] = lax.dot_general(
        rows_down_ref[...], grad_ref[:, :half], CONTRACT_ROWS, preferred_element_type=F32
    ).astype(BF16)


def back_kernel(grad_ref, weight_ref, after_ref, part_ref, token_ref, weight, part, sems):
    steps, depth, _ = weight.shape
    loads = [
        pltpu.make_async_copy(weight_ref.at[pl.ds(k * depth, depth), :], weight.at[k], sems.at[0, k])
        for k in range(steps)
    ]
    stores = [
        pltpu.make_async_copy(part.at[k], part_ref.at[:, pl.ds(k * depth, depth)], sems.at[1, k])
        for k in range(steps)
    ]
    for load in loads:
        load.start()
    for k in range(steps):
        loads[k].wait()
        part[k] = lax.dot_general(
            grad_ref[...], weight[k], CONTRACT_COLS, preferred_element_type=F32
        ).astype(BF16)
        stores[k].start()
    for store in stores:
        store.wait()
    token_ref[...] = jnp.zeros_like(token_ref)


def add_kernel(chunks_ref, got_ref, rows_ref, grad_ref, after_ref, out_ref, token_ref):
    out_ref[...] = (
        got_ref[...].astype(F32)
        + lax.dot_general(rows_ref[...], grad_ref[...], CONTRACT_ROWS, preferred_element_type=F32)
    ).astype(BF16)
    token_ref[...] = jnp.zeros_like(token_ref)


def last_kernel(
    chunks_ref, low_up_ref, low_down_ref, high_up_ref, high_down_ref, rows_ref, grad_ref, after_ref, out_ref
):
    half = low_up_ref.shape[1]
    own = lax.dot_general(rows_ref[...], grad_ref[...], CONTRACT_ROWS, preferred_element_type=F32)
    low = low_up_ref[...].astype(F32) + low_down_ref[...].astype(F32)
    high = high_up_ref[...].astype(F32) + high_down_ref[...].astype(F32)
    out_ref[:, :half] = (own[:, :half] + low).astype(BF16)
    out_ref[:, half:] = (own[:, half:] + high).astype(BF16)


def sum_kernel(place_ref, back_ref, after_ref, out_ref, token_ref):
    out_ref[...] = lax.dot_general(
        place_ref[...], back_ref[...], CONTRACT_ROWS, preferred_element_type=F32
    ).astype(BF16)
    token_ref[...] = jnp.zeros_like(token_ref)


def body(
    hidden,
    output_weight,
    owners,
    negatives,
    negative_mask,
    target_block,
    target_word,
    log_norm,
    cotangent,
):
    tokens, width = hidden.shape
    visits = owners.shape[1]
    peers = lax.axis_size("vocab")
    planes = lax.axis_size("dp")
    words = output_weight.shape[1]
    capacity = max(2, tokens * visits * 4 // (3 * peers))
    slots = peers * capacity
    sent = width + META
    chunk = width // planes
    half = words // 2
    weights = pltpu.with_memory_space_constraint(output_weight, pltpu.HBM)
    anywhere = pl.BlockSpec(memory_space=pl.ANY)
    hbm = pl.BlockSpec(memory_space=pltpu.HBM)
    vmem = pl.BlockSpec(memory_space=pltpu.VMEM)
    steps = 8
    depth = width // steps

    send, place = pl.pallas_call(
        functools.partial(place_kernel, capacity),
        in_specs=[vmem] * 8,
        out_specs=[hbm, vmem],
        out_shape=[
            pltpu.HBM((slots, sent), BF16),
            jax.ShapeDtypeStruct((slots, tokens), BF16),
        ],
        scratch_shapes=[pltpu.VMEM((slots, sent), BF16), pltpu.SemaphoreType.DMA((width // 512,))],
        compiler_params=params(24),
        cost_estimate=cost(0),
        name="place_rows",
    )(
        hidden,
        owners.T,
        negatives.transpose(1, 2, 0),
        negative_mask.transpose(1, 2, 0),
        target_block[None, :],
        target_word[None, :],
        log_norm[None, :],
        cotangent[None, :],
    )
    got = lax.all_to_all(
        send.reshape(peers, capacity, sent), "vocab", split_axis=0, concat_axis=0, tiled=True
    ).reshape(slots, sent)

    chunks = lax.rem(lax.axis_index("dp") + jnp.arange(planes, dtype=jnp.int32), planes)
    far = planes // 2

    def rows_spec(k):
        return pl.BlockSpec((slots, chunk), lambda i, c: (0, c[k % planes]))

    def whole(shape):
        return pl.BlockSpec(shape, lambda i, c: (0, 0))

    message = jax.ShapeDtypeStruct((chunk, half), BF16)
    message_spec = whole((chunk, half))
    token = jax.ShapeDtypeStruct((8, 128), F32)
    token_spec = whole((8, 128))
    grad, far_up, far_down, _ = pl.pallas_call(
        score_kernel,
        grid_spec=pltpu.PrefetchScalarGridSpec(
            num_scalar_prefetch=1,
            grid=(1,),
            in_specs=[hbm, hbm],
            out_specs=[whole((slots, words)), message_spec, message_spec, token_spec],
            scratch_shapes=[
                pltpu.VMEM((steps, slots, depth), BF16),
                pltpu.VMEM((steps, depth, words), BF16),
                pltpu.VMEM((slots, META), BF16),
                pltpu.VMEM((slots, words), F32),
                pltpu.SemaphoreType.DMA((3, steps)),
            ],
        ),
        out_shape=[jax.ShapeDtypeStruct((slots, words), BF16), message, message, token],
        compiler_params=params(32),
        cost_estimate=cost(0),
        name="scores",
    )(chunks, got, weights)

    def hop(x, d):
        return lax.ppermute(x, "dp", [(i, (i + d) % planes) for i in range(planes)])

    near = far - 1
    near_up, near_down = pl.pallas_call(
        pair_kernel,
        grid_spec=pltpu.PrefetchScalarGridSpec(
            num_scalar_prefetch=1,
            grid=(1,),
            in_specs=[rows_spec(near), rows_spec(-near), whole((slots, words))],
            out_specs=[message_spec, message_spec],
        ),
        out_shape=[message, message],
        compiler_params=params(16),
        cost_estimate=cost(NEAR),
        name="near_parts",
    )(chunks, got, got, grad)

    def state_parts(after):
        return pl.pallas_call(
            back_kernel,
            in_specs=[vmem, hbm, anywhere],
            out_specs=[hbm, vmem],
            out_shape=[pltpu.HBM((slots, width), BF16), token],
            scratch_shapes=[
                pltpu.VMEM((steps, depth, words), BF16),
                pltpu.VMEM((steps, slots, depth), BF16),
                pltpu.SemaphoreType.DMA((2, steps)),
            ],
            compiler_params=params(24),
            cost_estimate=cost(STATE),
            name="state_parts",
        )(grad, weights, after)

    def add(k, high, arrived, after):
        return pl.pallas_call(
            add_kernel,
            grid_spec=pltpu.PrefetchScalarGridSpec(
                num_scalar_prefetch=1,
                grid=(1,),
                in_specs=[
                    message_spec,
                    rows_spec(k),
                    pl.BlockSpec((slots, half), lambda i, c: (0, high)),
                    anywhere,
                ],
                out_specs=[message_spec, token_spec],
            ),
            out_shape=[message, token],
            compiler_params=params(16),
            cost_estimate=cost(ADD),
            name="add_part",
        )(chunks, arrived, got, grad, after)

    flows = [(1, 0, far, far_up), (-1, 1, far, far_down), (1, 1, near, near_up), (-1, 0, near, near_down)]
    messages = [f[3] for f in flows]
    after = near_up
    event = 0
    for step in range(far):
        for f, (d, high, hops, _) in enumerate(flows):
            if step < hops:
                messages[f] = hop(messages[f], d)
                if step < hops - 1:
                    messages[f], after = add(d * (hops - 1 - step), high, messages[f], after)
                    event += 1
                    if event == GAP:
                        part, after = state_parts(after)
    back = lax.all_to_all(
        part.reshape(peers, capacity, width), "vocab", split_axis=0, concat_axis=0, tiled=True
    ).reshape(slots, width)

    hidden_grad, after = pl.pallas_call(
        sum_kernel,
        grid=(4,),
        in_specs=[
            pl.BlockSpec((slots, tokens), lambda i: (0, 0)),
            pl.BlockSpec((slots, width // 4), lambda i: (0, i)),
            anywhere,
        ],
        out_specs=[
            pl.BlockSpec((tokens, width // 4), lambda i: (0, i)),
            pl.BlockSpec((8, 128), lambda i: (0, 0)),
        ],
        out_shape=[jax.ShapeDtypeStruct((tokens, width), BF16), token],
        compiler_params=params(16),
        cost_estimate=cost(SUM),
        name="sum_parts",
    )(place, back, after)

    weight_grad = pl.pallas_call(
        last_kernel,
        grid_spec=pltpu.PrefetchScalarGridSpec(
            num_scalar_prefetch=1,
            grid=(1,),
            in_specs=[message_spec] * 4 + [rows_spec(0), whole((slots, words)), anywhere],
            out_specs=whole((chunk, words)),
        ),
        out_shape=jax.ShapeDtypeStruct((chunk, words), BF16),
        compiler_params=params(24),
        cost_estimate=cost(0),
        name="last_add",
    )(chunks, messages[0], messages[3], messages[1], messages[2], got, grad, after)
    return (hidden_grad, weight_grad)


def solution(mesh):
    placed = (
        P(("dp", "vocab"), None),
        P(None, "vocab"),
        P(("dp", "vocab"), None),
        P(("dp", "vocab"), None, None),
        P(("dp", "vocab"), None, None),
        P(("dp", "vocab")),
        P(("dp", "vocab")),
        P(("dp", "vocab")),
        P(("dp", "vocab")),
    )
    return jax.shard_map(
        body,
        mesh=mesh,
        in_specs=placed,
        out_specs=(P(("dp", "vocab"), None), P("dp", "vocab")),
        check_vma=False,
    )
```

time: 202 us -> 190 us (0.941)
  blocking collectives: 55.2 us -> 0 us
  Pallas kernels: 0 us -> 54.1 us
  matrix products: 31 us -> 0 us
  starting transfers between devices: 7.89 us -> 36.3 us
  between operations: 14.1 us -> 0.77 us
  waiting for transfers between devices: 80.2 us -> 92 us
  other arithmetic: 7.43 us -> 0.01 us
  local copies, waits for them, and re-layouts: 3.36 us -> 5.89 us
    all_to_all x1 -> x0, blocking collectives: 55.2 us -> none  [body(): lax.all_to_all(part.reshape(peers, capacity, width), 'vocab', split_axis=...]
    pallas_call x0 -> x16, Pallas kernels: none -> 54.1 us  [the longest x10 23.8 us: add(): pl.pallas_call(add_kernel, grid_spec=pltpu.PrefetchScalarGridSpec(num_sca...]
    ppermute x0 -> x14, waiting for transfers between devices: none -> 39.2 us  [hop(): return lax.ppermute(x, 'dp', [(i, (i + d) % planes) for i in range(planes)])]
    dot_general x7 -> x0, matrix products: 31 us -> none  [the longest x1 9.61 us: body(): lax.dot_general(rows, score_grad, (((0,), (0,)), ((), ())), preferred_ele...]
    reduce_scatter x1 -> x0, waiting for transfers between devices: 27.6 us -> none  [body(): lax.psum_scatter(weight_part, 'dp', scatter_dimension=0, tiled=True)]
    ppermute x0 -> x14, starting transfers between devices: none -> 23 us  [hop(): return lax.ppermute(x, 'dp', [(i, (i + d) % planes) for i in range(planes)])]
    all_to_all x1 -> x2, starting transfers between devices: 7.67 us -> 13.3 us  [the longest x1 7.68 us: body(): lax.all_to_all(send.reshape(peers, capacity, sent), 'vocab', split_axis=0...]
    unnamed x9 -> x16, local copies, waits for them, and re-layouts: 2.71 us -> 5.89 us
  transfers between devices with their start and end apart: 2 -> 16, of which waited for: 2 -> 11; matrix products, arithmetic and copies ran while one was open for 5% -> 0% of each run, Pallas kernels for 0% -> 15%
where the time goes in v2:
time: 190 us; the launch traced here: 189 us
  waiting for transfers between devices  92 us (48%)
  Pallas kernels  54.1 us (28%)
  starting transfers between devices  36.3 us (19%)
  local copies, waits for them, and re-layouts  5.89 us (3%)
    all_to_all x1, waiting for transfers between devices, body(): lax.all_to_all(send.reshape(peers, capacity, sent), 'vocab', split_axis=0...  52.8 us
    ppermute x14, waiting for transfers between devices, hop(): return lax.ppermute(x, 'dp', [(i, (i + d) % planes) for i in range(planes)])  39.2 us
    pallas_call x10, Pallas kernels, add(): pl.pallas_call(add_kernel, grid_spec=pltpu.PrefetchScalarGridSpec(num_sca...  23.8 us
    ppermute x14, starting transfers between devices, hop(): return lax.ppermute(x, 'dp', [(i, (i + d) % planes) for i in range(planes)])  23 us
    pallas_call x1, Pallas kernels, body(): pl.pallas_call(score_kernel, grid_spec=pltpu.PrefetchScalarGridSpec(num_s...  8.91 us
    pallas_call x1, Pallas kernels, state_parts(): pl.pallas_call(back_kernel, in_specs=[vmem, hbm, anywhere], out_specs=[hb...  8.22 us
    all_to_all x1, starting transfers between devices, body(): lax.all_to_all(send.reshape(peers, capacity, sent), 'vocab', split_axis=0...  7.68 us
    unnamed x16, local copies, waits for them, and re-layouts  5.89 us
  transfers between devices with their start and end apart: 16, of which 11 were waited for; matrix products, arithmetic and copies ran while one was open for 0% of the time, Pallas kernels for 15%

profile of v2, /device:TPU:98, one launch (start us, length us, event | category | flops | bytes accessed | tf_op | source)
XLA Modules:
  0.0 189.1 jit_solution(9875003651325276400)
XLA Ops:
  6.5 2.7 %place_rows.1 = (bf16[512,4224]{1,0:T(8,128)(2,1)}, bf16[512,128]{1,0:T(8,128)(2,1)S(1)}) custom-call(bf16[128,4096]{1,0:T(8,128)(2,1)S(1)} %copy-done, s32[3,128]{1,0:T(4,128)S(1)} %bitcast.13, s32[3,2,128]{2,1,0:T(2,128)S(1)} %bitcast.11, s32[3,2,128]{2,1,0:T(2,128)S(1)} %bitcast.12, s32[1,128]{1,0:T(1,128)S(1)} %bitcast.14, s32[1,128]{1,0:T(1,128)S(1)} %bitcast.15, ...), custom_call_target="tpu_custom_call" | custom-call | tf_op jit(solution)/shard_map/place_rows/pallas_call | solution.py:241
  9.3 7.7 %all-to-all-start = ((bf16[32,16,4224]{2,1,0:T(8,128)(2,1)}), bf16[32,16,4224]{2,1,0:T(8,128)(2,1)}, u32[]{:S(2)}, u32[]{:S(2)}) async-start(bf16[32,16,4224]{2,1,0:T(8,128)(2,1)} %bitcast.18), calls=%async_computation | async-start | bytes 8650752 | tf_op jit(solution)/shard_map/all_to_all | solution.py:263
  17.0 52.8 %all-to-all-done = bf16[32,16,4224]{2,1,0:T(8,128)(2,1)} async-done(((bf16[32,16,4224]{2,1,0:T(8,128)(2,1)}), bf16[32,16,4224]{2,1,0:T(8,128)(2,1)}, u32[]{:S(2)}, u32[]{:S(2)}) %all-to-all-start) | async-done | bytes 4325408 | tf_op jit(solution)/shard_map/all_to_all | solution.py:263
  69.8 8.9 %scores.1 = (bf16[512,1024]{1,0:T(8,128)(2,1)S(1)}, bf16[512,512]{1,0:T(8,128)(2,1)S(1)}, bf16[512,512]{1,0:T(8,128)(2,1)S(1)}, f32[8,128]{1,0:T(8,128)}) custom-call(s32[8]{0:T(128)S(1)} %compare_select_fusion.chunks_ref, bf16[512,4224]{1,0:T(8,128)(2,1)} %bitcast.8.got_ref.rows_up_ref.rows_down_ref.rows_ref, bf16[4096,1024]{1,0:T(8,128)(2,1)} %weight_ref.3), custom_call_target="tpu_custom_call" | custom-call | tf_op jit(solution)/shard_map/scores/pallas_call | solution.py:280
  78.7 3.2 %collective-permute-start.1 = (bf16[512,512]{1,0:T(8,128)(2,1)S(1)}, bf16[512,512]{1,0:T(8,128)(2,1)S(1)}, u32[]{:S(2)}, u32[]{:S(2)}) collective-permute-start(bf16[512,512]{1,0:T(8,128)(2,1)S(1)} %get-tuple-element.37), channel_id=1, source_target_pairs={{0,32},{32,64},{64,96},{96,128},{128,160},{160,192},{192,224},{224... | collective-permute-start | bytes 1572872 | tf_op jit(solution)/shard_map/ppermute | solution.py:302
  81.9 2.5 %near_parts.1 = (bf16[512,512]{1,0:T(8,128)(2,1)S(1)}, bf16[512,512]{1,0:T(8,128)(2,1)S(1)}) custom-call(s32[8]{0:T(128)S(1)} %compare_select_fusion.chunks_ref, bf16[512,4224]{1,0:T(8,128)(2,1)} %bitcast.8.got_ref.rows_up_ref.rows_down_ref.rows_ref, bf16[512,4224]{1,0:T(8,128)(2,1)} %bitcast.8.got_ref.rows_up_ref.rows_down_ref.rows_ref, ...), custom_call_target="tpu_custom_call" | custom-call | tf_op jit(solution)/shard_map/near_parts/pallas_call | solution.py:305
  84.4 8.5 %collective-permute-done.1.got_ref = bf16[512,512]{1,0:T(8,128)(2,1)S(1)} collective-permute-done((bf16[512,512]{1,0:T(8,128)(2,1)S(1)}, bf16[512,512]{1,0:T(8,128)(2,1)S(1)}, u32[]{:S(2)}, u32[]{:S(2)}) %collective-permute-start.1) | collective-permute-done | bytes 524320 | tf_op jit(solution)/shard_map/ppermute | solution.py:302
  92.9 2.1 %add_part.10 = (bf16[512,512]{1,0:T(8,128)(2,1)S(1)}, f32[8,128]{1,0:T(8,128)S(1)}) custom-call(s32[8]{0:T(128)S(1)} %compare_select_fusion.chunks_ref, bf16[512,512]{1,0:T(8,128)(2,1)S(1)} %collective-permute-done.1.got_ref, bf16[512,4224]{1,0:T(8,128)(2,1)} %bitcast.8.got_ref.rows_up_ref.rows_down_ref.rows_ref, ...), custom_call_target="tpu_custom_call" | custom-call | tf_op jit(solution)/shard_map/add_part/pallas_call | solution.py:336
  96.3 2.1 %add_part.11 = (bf16[512,512]{1,0:T(8,128)(2,1)S(1)}, f32[8,128]{1,0:T(8,128)S(1)}) custom-call(s32[8]{0:T(128)S(1)} %compare_select_fusion.chunks_ref, bf16[512,512]{1,0:T(8,128)(2,1)S(1)} %collective-permute-done.got_ref, bf16[512,4224]{1,0:T(8,128)(2,1)} %bitcast.8.got_ref.rows_up_ref.rows_down_ref.rows_ref, ...), custom_call_target="tpu_custom_call" | custom-call | tf_op jit(solution)/shard_map/add_part/pallas_call | solution.py:336
  98.4 8.2 %state_parts.1 = (bf16[512,4096]{1,0:T(8,128)(2,1)}, f32[8,128]{1,0:T(8,128)S(1)}) custom-call(bf16[512,1024]{1,0:T(8,128)(2,1)S(1)} %get-tuple-element.35.grad_ref, bf16[4096,1024]{1,0:T(8,128)(2,1)} %weight_ref.3, f32[8,128]{1,0:T(8,128)S(1)} %get-tuple-element.40.after_ref), custom_call_target="tpu_custom_call" | custom-call | tf_op jit(solution)/shard_map/state_parts/pallas_call | solution.py:320
  106.6 5.6 %all-to-all-start.1 = ((bf16[32,16,4096]{2,1,0:T(8,128)(2,1)}), bf16[32,16,4096]{2,1,0:T(8,128)(2,1)}, u32[]{:S(2)}, u32[]{:S(2)}) async-start(bf16[32,16,4096]{2,1,0:T(8,128)(2,1)} %bitcast.19), calls=%async_computation.1 | async-start | bytes 8388608 | tf_op jit(solution)/shard_map/all_to_all | solution.py:368
  112.2 2.4 %collective-permute-start.5 = (bf16[512,512]{1,0:T(8,128)(2,1)S(1)}, bf16[512,512]{1,0:T(8,128)(2,1)S(1)}, u32[]{:S(2)}, u32[]{:S(2)}) collective-permute-start(bf16[512,512]{1,0:T(8,128)(2,1)S(1)} %get-tuple-element.38.after_ref), channel_id=1, source_target_pairs={{0,32},{32,64},{64,96},{96,128},{128,160},{160,192},{192,224},{224... | collective-permute-start | bytes 1572872 | tf_op jit(solution)/shard_map/ppermute | solution.py:302
  114.7 3.2 %collective-permute-start.3 = (bf16[512,512]{1,0:T(8,128)(2,1)S(1)}, bf16[512,512]{1,0:T(8,128)(2,1)S(1)}, u32[]{:S(2)}, u32[]{:S(2)}) collective-permute-start(bf16[512,512]{1,0:T(8,128)(2,1)S(1)} %get-tuple-element.43), channel_id=1, source_target_pairs={{0,32},{32,64},{64,96},{96,128},{128,160},{160,192},{192,224},{224... | collective-permute-start | bytes 1572872 | tf_op jit(solution)/shard_map/ppermute | solution.py:302
  117.9 9.2 %collective-permute-done.5.got_ref = bf16[512,512]{1,0:T(8,128)(2,1)S(1)} collective-permute-done((bf16[512,512]{1,0:T(8,128)(2,1)S(1)}, bf16[512,512]{1,0:T(8,128)(2,1)S(1)}, u32[]{:S(2)}, u32[]{:S(2)}) %collective-permute-start.5) | collective-permute-done | bytes 524320 | tf_op jit(solution)/shard_map/ppermute | solution.py:302
  127.1 2.1 %add_part.12 = (bf16[512,512]{1,0:T(8,128)(2,1)S(1)}, f32[8,128]{1,0:T(8,128)S(1)}) custom-call(s32[8]{0:T(128)S(1)} %compare_select_fusion.chunks_ref, bf16[512,512]{1,0:T(8,128)(2,1)S(1)} %collective-permute-done.5.got_ref, bf16[512,4224]{1,0:T(8,128)(2,1)} %bitcast.8.got_ref.rows_up_ref.rows_down_ref.rows_ref, ...), custom_call_target="tpu_custom_call" | custom-call | tf_op jit(solution)/shard_map/add_part/pallas_call | solution.py:336
  129.1 3.6 %collective-permute-start.9 = (bf16[512,512]{1,0:T(8,128)(2,1)S(1)}, bf16[512,512]{1,0:T(8,128)(2,1)S(1)}, u32[]{:S(2)}, u32[]{:S(2)}) collective-permute-start(bf16[512,512]{1,0:T(8,128)(2,1)S(1)} %get-tuple-element.52), channel_id=1, source_target_pairs={{0,32},{32,64},{64,96},{96,128},{128,160},{160,192},{192,224},{224... | collective-permute-start | bytes 1572872 | tf_op jit(solution)/shard_map/ppermute | solution.py:302
  132.8 2.1 %add_part.13 = (bf16[512,512]{1,0:T(8,128)(2,1)S(1)}, f32[8,128]{1,0:T(8,128)S(1)}) custom-call(s32[8]{0:T(128)S(1)} %compare_select_fusion.chunks_ref, bf16[512,512]{1,0:T(8,128)(2,1)S(1)} %collective-permute-done.4.got_ref, bf16[512,4224]{1,0:T(8,128)(2,1)} %bitcast.8.got_ref.rows_up_ref.rows_down_ref.rows_ref, ...), custom_call_target="tpu_custom_call" | custom-call | tf_op jit(solution)/shard_map/add_part/pallas_call | solution.py:336
  134.9 3.4 %collective-permute-done.3.got_ref = bf16[512,512]{1,0:T(8,128)(2,1)S(1)} collective-permute-done((bf16[512,512]{1,0:T(8,128)(2,1)S(1)}, bf16[512,512]{1,0:T(8,128)(2,1)S(1)}, u32[]{:S(2)}, u32[]{:S(2)}) %collective-permute-start.3) | collective-permute-done | bytes 524320 | tf_op jit(solution)/shard_map/ppermute | solution.py:302
  138.3 2.1 %add_part.14 = (bf16[512,512]{1,0:T(8,128)(2,1)S(1)}, f32[8,128]{1,0:T(8,128)S(1)}) custom-call(s32[8]{0:T(128)S(1)} %compare_select_fusion.chunks_ref, bf16[512,512]{1,0:T(8,128)(2,1)S(1)} %collective-permute-done.3.got_ref, bf16[512,4224]{1,0:T(8,128)(2,1)} %bitcast.8.got_ref.rows_up_ref.rows_down_ref.rows_ref, ...), custom_call_target="tpu_custom_call" | custom-call | tf_op jit(solution)/shard_map/add_part/pallas_call | solution.py:336
  140.4 3.9 %collective-permute-start.7 = (bf16[512,512]{1,0:T(8,128)(2,1)S(1)}, bf16[512,512]{1,0:T(8,128)(2,1)S(1)}, u32[]{:S(2)}, u32[]{:S(2)}) collective-permute-start(bf16[512,512]{1,0:T(8,128)(2,1)S(1)} %get-tuple-element.50), channel_id=1, source_target_pairs={{0,32},{32,64},{64,96},{96,128},{128,160},{160,192},{192,224},{224... | collective-permute-start | bytes 1572872 | tf_op jit(solution)/shard_map/ppermute | solution.py:302
  144.2 2.1 %add_part.15 = (bf16[512,512]{1,0:T(8,128)(2,1)S(1)}, f32[8,128]{1,0:T(8,128)S(1)}) custom-call(s32[8]{0:T(128)S(1)} %compare_select_fusion.chunks_ref, bf16[512,512]{1,0:T(8,128)(2,1)S(1)} %collective-permute-done.2.got_ref, bf16[512,4224]{1,0:T(8,128)(2,1)} %bitcast.8.got_ref.rows_up_ref.rows_down_ref.rows_ref, ...), custom_call_target="tpu_custom_call" | custom-call | tf_op jit(solution)/shard_map/add_part/pallas_call | solution.py:336
  146.4 3.2 %collective-permute-done.9.got_ref = bf16[512,512]{1,0:T(8,128)(2,1)S(1)} collective-permute-done((bf16[512,512]{1,0:T(8,128)(2,1)S(1)}, bf16[512,512]{1,0:T(8,128)(2,1)S(1)}, u32[]{:S(2)}, u32[]{:S(2)}) %collective-permute-start.9) | collective-permute-done | bytes 524320 | tf_op jit(solution)/shard_map/ppermute | solution.py:302
  149.5 2.9 %add_part.16 = (bf16[512,512]{1,0:T(8,128)(2,1)}, f32[8,128]{1,0:T(8,128)S(1)}) custom-call(s32[8]{0:T(128)S(1)} %compare_select_fusion.chunks_ref, bf16[512,512]{1,0:T(8,128)(2,1)S(1)} %collective-permute-done.9.got_ref, bf16[512,4224]{1,0:T(8,128)(2,1)} %bitcast.8.got_ref.rows_up_ref.rows_down_ref.rows_ref, ...), custom_call_target="tpu_custom_call" | custom-call | tf_op jit(solution)/shard_map/add_part/pallas_call | solution.py:336
  153.1 2.9 %add_part.17 = (bf16[512,512]{1,0:T(8,128)(2,1)}, f32[8,128]{1,0:T(8,128)S(1)}) custom-call(s32[8]{0:T(128)S(1)} %compare_select_fusion.chunks_ref, bf16[512,512]{1,0:T(8,128)(2,1)S(1)} %collective-permute-done.8.got_ref, bf16[512,4224]{1,0:T(8,128)(2,1)} %bitcast.8.got_ref.rows_up_ref.rows_down_ref.rows_ref, ...), custom_call_target="tpu_custom_call" | custom-call | tf_op jit(solution)/shard_map/add_part/pallas_call | solution.py:336
  156.0 3.2 %collective-permute-start.13 = (bf16[512,512]{1,0:T(8,128)(2,1)}, bf16[512,512]{1,0:T(8,128)(2,1)S(1)}, u32[]{:S(2)}, u32[]{:S(2)}) collective-permute-start(bf16[512,512]{1,0:T(8,128)(2,1)} %get-tuple-element.62), channel_id=1, source_target_pairs={{0,32},{32,64},{64,96},{96,128},{128,160},{160,192},{192,224},{224... | collective-permute-start | bytes 1572872 | tf_op jit(solution)/shard_map/ppermute | solution.py:302
  159.2 1.5 collective-permute-done.7.got_ref
  160.8 2.9 %add_part.18 = (bf16[512,512]{1,0:T(8,128)(2,1)}, f32[8,128]{1,0:T(8,128)S(1)}) custom-call(s32[8]{0:T(128)S(1)} %compare_select_fusion.chunks_ref, bf16[512,512]{1,0:T(8,128)(2,1)S(1)} %collective-permute-done.7.got_ref, bf16[512,4224]{1,0:T(8,128)(2,1)} %bitcast.8.got_ref.rows_up_ref.rows_down_ref.rows_ref, ...), custom_call_target="tpu_custom_call" | custom-call | tf_op jit(solution)/shard_map/add_part/pallas_call | solution.py:336
  164.4 2.8 %add_part.19 = (bf16[512,512]{1,0:T(8,128)(2,1)}, f32[8,128]{1,0:T(8,128)S(1)}) custom-call(s32[8]{0:T(128)S(1)} %compare_select_fusion.chunks_ref, bf16[512,512]{1,0:T(8,128)(2,1)S(1)} %collective-permute-done.6.got_ref, bf16[512,4224]{1,0:T(8,128)(2,1)} %bitcast.8.got_ref.rows_up_ref.rows_down_ref.rows_ref, ...), custom_call_target="tpu_custom_call" | custom-call | tf_op jit(solution)/shard_map/add_part/pallas_call | solution.py:336
  167.2 3.2 %collective-permute-start.10 = (bf16[512,512]{1,0:T(8,128)(2,1)}, bf16[512,512]{1,0:T(8,128)(2,1)S(1)}, u32[]{:S(2)}, u32[]{:S(2)}) collective-permute-start(bf16[512,512]{1,0:T(8,128)(2,1)} %get-tuple-element.59), channel_id=1, source_target_pairs={{0,32},{32,64},{64,96},{96,128},{128,160},{160,192},{192,224},{224... | collective-permute-start | bytes 1572872 | tf_op jit(solution)/shard_map/ppermute | solution.py:302
  170.5 4.6 %sum_parts.1 = (bf16[128,4096]{1,0:T(8,128)(2,1)}, f32[8,128]{1,0:T(8,128)S(1)}) custom-call(bf16[512,128]{1,0:T(8,128)(2,1)S(1)} %get-tuple-element.33.place_ref, bf16[512,4096]{1,0:T(8,128)(2,1)} %bitcast.10.back_ref, f32[8,128]{1,0:T(8,128)S(1)} %get-tuple-element.57.after_ref), custom_call_target="tpu_custom_call" | custom-call | tf_op jit(solution)/shard_map/sum_parts/pallas_call | solution.py:372
  175.6 10.1 %collective-permute-done.12.high_up_ref = bf16[512,512]{1,0:T(8,128)(2,1)S(1)} collective-permute-done((bf16[512,512]{1,0:T(8,128)(2,1)}, bf16[512,512]{1,0:T(8,128)(2,1)S(1)}, u32[]{:S(2)}, u32[]{:S(2)}) %collective-permute-start.12) | collective-permute-done | bytes 524320 | tf_op jit(solution)/shard_map/ppermute | solution.py:302
  185.7 3.3 %last_add.1 = bf16[512,1024]{1,0:T(8,128)(2,1)} custom-call(s32[8]{0:T(128)S(1)} %compare_select_fusion.chunks_ref, bf16[512,512]{1,0:T(8,128)(2,1)S(1)} %collective-permute-done.10.low_up_ref, bf16[512,512]{1,0:T(8,128)(2,1)S(1)} %collective-permute-done.11.low_down_ref, bf16[512,512]{1,0:T(8,128)(2,1)S(1)} %collective-permute-done.12.high_up_ref, ...), custom_call_target="tpu_custom_call" | custom-call | tf_op jit(solution)/shard_map/last_add/pallas_call | solution.py:390
  (33 shorter events, 9.5 us)
Async XLA Ops:
  0.6 1.2 copy-start
  1.9 0.7 copy-start.1
  2.5 0.7 copy-start.2
  3.2 0.7 copy-start.3
  3.9 0.7 copy-start.4
  4.6 0.7 copy-start.5
  5.2 0.7 copy-start.6
  5.9 0.7 copy-start.7
  9.3 60.5 %all-to-all-start = ((bf16[32,16,4224]{2,1,0:T(8,128)(2,1)}), bf16[32,16,4224]{2,1,0:T(8,128)(2,1)}, u32[]{:S(2)}, u32[]{:S(2)}) async-start(bf16[32,16,4224]{2,1,0:T(8,128)(2,1)} %bitcast.18), calls=%async_computation | async-start | bytes 8650752 | tf_op jit(solution)/shard_map/all_to_all | solution.py:263
  78.7 14.2 %collective-permute-start.1 = (bf16[512,512]{1,0:T(8,128)(2,1)S(1)}, bf16[512,512]{1,0:T(8,128)(2,1)S(1)}, u32[]{:S(2)}, u32[]{:S(2)}) collective-permute-start(bf16[512,512]{1,0:T(8,128)(2,1)S(1)} %get-tuple-element.37), channel_id=1, source_target_pairs={{0,32},{32,64},{64,96},{96,128},{128,160},{160,192},{192,224},{224... | collective-permute-start | bytes 1572872 | tf_op jit(solution)/shard_map/ppermute | solution.py:302
  81.9 14.4 %collective-permute-start = (bf16[512,512]{1,0:T(8,128)(2,1)S(1)}, bf16[512,512]{1,0:T(8,128)(2,1)S(1)}, u32[]{:S(2)}, u32[]{:S(2)}) collective-permute-start(bf16[512,512]{1,0:T(8,128)(2,1)S(1)} %get-tuple-element.36), channel_id=1, source_target_pairs={{0,224},{32,0},{64,32},{96,64},{128,96},{160,128},{192,160},{224,1... | collective-permute-start | bytes 1572872 | tf_op jit(solution)/shard_map/ppermute | solution.py:302
  106.6 63.8 %all-to-all-start.1 = ((bf16[32,16,4096]{2,1,0:T(8,128)(2,1)}), bf16[32,16,4096]{2,1,0:T(8,128)(2,1)}, u32[]{:S(2)}, u32[]{:S(2)}) async-start(bf16[32,16,4096]{2,1,0:T(8,128)(2,1)} %bitcast.19), calls=%async_computation.1 | async-start | bytes 8388608 | tf_op jit(solution)/shard_map/all_to_all | solution.py:368
  112.2 14.8 %collective-permute-start.5 = (bf16[512,512]{1,0:T(8,128)(2,1)S(1)}, bf16[512,512]{1,0:T(8,128)(2,1)S(1)}, u32[]{:S(2)}, u32[]{:S(2)}) collective-permute-start(bf16[512,512]{1,0:T(8,128)(2,1)S(1)} %get-tuple-element.38.after_ref), channel_id=1, source_target_pairs={{0,32},{32,64},{64,96},{96,128},{128,160},{160,192},{192,224},{224... | collective-permute-start | bytes 1572872 | tf_op jit(solution)/shard_map/ppermute | solution.py:302
  114.7 18.1 %collective-permute-start.4 = (bf16[512,512]{1,0:T(8,128)(2,1)S(1)}, bf16[512,512]{1,0:T(8,128)(2,1)S(1)}, u32[]{:S(2)}, u32[]{:S(2)}) collective-permute-start(bf16[512,512]{1,0:T(8,128)(2,1)S(1)} %get-tuple-element.44), channel_id=1, source_target_pairs={{0,224},{32,0},{64,32},{96,64},{128,96},{160,128},{192,160},{224,1... | collective-permute-start | bytes 1572872 | tf_op jit(solution)/shard_map/ppermute | solution.py:302
  114.7 23.6 %collective-permute-start.3 = (bf16[512,512]{1,0:T(8,128)(2,1)S(1)}, bf16[512,512]{1,0:T(8,128)(2,1)S(1)}, u32[]{:S(2)}, u32[]{:S(2)}) collective-permute-start(bf16[512,512]{1,0:T(8,128)(2,1)S(1)} %get-tuple-element.43), channel_id=1, source_target_pairs={{0,32},{32,64},{64,96},{96,128},{128,160},{160,192},{192,224},{224... | collective-permute-start | bytes 1572872 | tf_op jit(solution)/shard_map/ppermute | solution.py:302
  117.9 26.3 %collective-permute-start.2 = (bf16[512,512]{1,0:T(8,128)(2,1)S(1)}, bf16[512,512]{1,0:T(8,128)(2,1)S(1)}, u32[]{:S(2)}, u32[]{:S(2)}) collective-permute-start(bf16[512,512]{1,0:T(8,128)(2,1)S(1)} %get-tuple-element.42), channel_id=1, source_target_pairs={{0,224},{32,0},{64,32},{96,64},{128,96},{160,128},{192,160},{224,1... | collective-permute-start | bytes 1572872 | tf_op jit(solution)/shard_map/ppermute | solution.py:302
  129.1 20.4 %collective-permute-start.9 = (bf16[512,512]{1,0:T(8,128)(2,1)S(1)}, bf16[512,512]{1,0:T(8,128)(2,1)S(1)}, u32[]{:S(2)}, u32[]{:S(2)}) collective-permute-start(bf16[512,512]{1,0:T(8,128)(2,1)S(1)} %get-tuple-element.52), channel_id=1, source_target_pairs={{0,32},{32,64},{64,96},{96,128},{128,160},{160,192},{192,224},{224... | collective-permute-start | bytes 1572872 | tf_op jit(solution)/shard_map/ppermute | solution.py:302
  134.8 18.3 %collective-permute-start.8 = (bf16[512,512]{1,0:T(8,128)(2,1)S(1)}, bf16[512,512]{1,0:T(8,128)(2,1)S(1)}, u32[]{:S(2)}, u32[]{:S(2)}) collective-permute-start(bf16[512,512]{1,0:T(8,128)(2,1)S(1)} %get-tuple-element.51), channel_id=1, source_target_pairs={{0,224},{32,0},{64,32},{96,64},{128,96},{160,128},{192,160},{224,1... | collective-permute-start | bytes 1572872 | tf_op jit(solution)/shard_map/ppermute | solution.py:302
  140.4 20.4 %collective-permute-start.7 = (bf16[512,512]{1,0:T(8,128)(2,1)S(1)}, bf16[512,512]{1,0:T(8,128)(2,1)S(1)}, u32[]{:S(2)}, u32[]{:S(2)}) collective-permute-start(bf16[512,512]{1,0:T(8,128)(2,1)S(1)} %get-tuple-element.50), channel_id=1, source_target_pairs={{0,32},{32,64},{64,96},{96,128},{128,160},{160,192},{192,224},{224... | collective-permute-start | bytes 1572872 | tf_op jit(solution)/shard_map/ppermute | solution.py:302
  146.3 18.1 %collective-permute-start.6 = (bf16[512,512]{1,0:T(8,128)(2,1)S(1)}, bf16[512,512]{1,0:T(8,128)(2,1)S(1)}, u32[]{:S(2)}, u32[]{:S(2)}) collective-permute-start(bf16[512,512]{1,0:T(8,128)(2,1)S(1)} %get-tuple-element.49), channel_id=1, source_target_pairs={{0,224},{32,0},{64,32},{96,64},{128,96},{160,128},{192,160},{224,1... | collective-permute-start | bytes 1572872 | tf_op jit(solution)/shard_map/ppermute | solution.py:302
  156.0 19.6 %collective-permute-start.11 = (bf16[512,512]{1,0:T(8,128)(2,1)}, bf16[512,512]{1,0:T(8,128)(2,1)S(1)}, u32[]{:S(2)}, u32[]{:S(2)}) collective-permute-start(bf16[512,512]{1,0:T(8,128)(2,1)} %get-tuple-element.60), channel_id=1, source_target_pairs={{0,224},{32,0},{64,32},{96,64},{128,96},{160,128},{192,160},{224,1... | collective-permute-start | bytes 1572872 | tf_op jit(solution)/shard_map/ppermute | solution.py:302
  156.0 19.6 %collective-permute-start.13 = (bf16[512,512]{1,0:T(8,128)(2,1)}, bf16[512,512]{1,0:T(8,128)(2,1)S(1)}, u32[]{:S(2)}, u32[]{:S(2)}) collective-permute-start(bf16[512,512]{1,0:T(8,128)(2,1)} %get-tuple-element.62), channel_id=1, source_target_pairs={{0,32},{32,64},{64,96},{96,128},{128,160},{160,192},{192,224},{224... | collective-permute-start | bytes 1572872 | tf_op jit(solution)/shard_map/ppermute | solution.py:302
  167.2 18.5 %collective-permute-start.12 = (bf16[512,512]{1,0:T(8,128)(2,1)}, bf16[512,512]{1,0:T(8,128)(2,1)S(1)}, u32[]{:S(2)}, u32[]{:S(2)}) collective-permute-start(bf16[512,512]{1,0:T(8,128)(2,1)} %get-tuple-element.61), channel_id=1, source_target_pairs={{0,224},{32,0},{64,32},{96,64},{128,96},{160,128},{192,160},{224,1... | collective-permute-start | bytes 1572872 | tf_op jit(solution)/shard_map/ppermute | solution.py:302
  167.2 18.5 %collective-permute-start.10 = (bf16[512,512]{1,0:T(8,128)(2,1)}, bf16[512,512]{1,0:T(8,128)(2,1)S(1)}, u32[]{:S(2)}, u32[]{:S(2)}) collective-permute-start(bf16[512,512]{1,0:T(8,128)(2,1)} %get-tuple-element.59), channel_id=1, source_target_pairs={{0,32},{32,64},{64,96},{96,128},{128,160},{160,192},{192,224},{224... | collective-permute-start | bytes 1572872 | tf_op jit(solution)/shard_map/ppermute | solution.py:302

commit v3 on v2

v3 whole, which is shorter than its diff:
```python
import functools

import jax
import jax.numpy as jnp
from jax import lax
from jax.experimental import pallas as pl
from jax.experimental.pallas import tpu as pltpu
from jax.sharding import PartitionSpec as P

BLOCK = 128
BLK_DEV = 8
META = 128
GAP = 0
STEPS = 4
MIB = 1 << 20
F32 = jnp.float32
BF16 = jnp.bfloat16
HOPS_US = (3,) * 10
OWN_US, SUM_US, LATE_US = 100, 0, 0


def cost(us):
    return pl.CostEstimate(flops=int(us * 1.15e9), bytes_accessed=0, transcendentals=0)


CONTRACT_ROWS = (((0,), (0,)), ((), ()))
CONTRACT_COLS = (((1,), (1,)), ((), ()))


def params(mib):
    return pltpu.CompilerParams(vmem_limit_bytes=mib * MIB)


def place_kernel(
    capacity,
    hidden_ref,
    owners_ref,
    negatives_ref,
    mask_ref,
    block_ref,
    word_ref,
    norm_ref,
    cot_ref,
    send_ref,
    place_ref,
    hidden,
    send,
    sems,
):
    tokens, width = hidden_ref.shape
    load = pltpu.make_async_copy(hidden_ref, hidden, sems.at[width // 512])
    load.start()
    visits, picks = negatives_ref.shape[:2]
    slots = send_ref.shape[0]
    peers = slots // capacity
    owner_iota = lax.broadcasted_iota(jnp.int32, (peers, tokens), 0)
    row = lax.broadcasted_iota(jnp.int32, (tokens, tokens), 0)
    col = lax.broadcasted_iota(jnp.int32, (tokens, tokens), 1)
    before = jnp.where(row < col, 1.0, 0.0).astype(BF16)
    slot_iota = lax.broadcasted_iota(jnp.int32, (slots, tokens), 0)
    cluster = lax.broadcasted_iota(jnp.int32, (BLK_DEV, tokens), 0)
    carried = jnp.zeros((peers, 1), F32)
    block = block_ref[...]
    total = jnp.zeros((slots, tokens), F32)
    info = jnp.zeros((slots, META), F32)
    for v in range(visits):
        owner = owners_ref[v : v + 1, :]
        hot = jnp.where(owner_iota == owner, 1.0, 0.0)
        earlier = jnp.dot(hot.astype(BF16), before, preferred_element_type=F32) + carried
        carried = carried + jnp.sum(hot, axis=1, keepdims=True)
        position = jnp.sum(hot * earlier, axis=0, keepdims=True).astype(jnp.int32)
        place = jnp.where(slot_iota == owner * capacity + position, 1.0, 0.0)
        total = total + place
        counts = jnp.zeros((BLK_DEV, tokens), F32)
        for n in range(picks):
            used = mask_ref[v, n : n + 1, :] == 1
            counts += jnp.where((cluster == negatives_ref[v, n : n + 1, :]) & used, 1.0, 0.0)
        if v == 0:
            counts += jnp.where(cluster == block, 1.0, 0.0)
            here = block.astype(F32)
        else:
            here = jnp.full((1, tokens), -1.0, F32)
        tail = jnp.zeros((META - BLK_DEV - 4, tokens), F32)
        meta = jnp.concatenate(
            [
                counts,
                cot_ref[...].astype(F32),
                norm_ref[...].astype(F32),
                here,
                word_ref[...].astype(F32),
                tail,
            ],
            axis=0,
        ).astype(BF16)
        info += lax.dot_general(
            place.astype(BF16), meta, CONTRACT_COLS, preferred_element_type=F32
        )
    place_tokens = total.astype(BF16)
    place_ref[...] = place_tokens
    send[:, width:] = info.astype(BF16)
    step = 512
    load.wait()
    stores = []
    for k, c in enumerate(range(0, width, step)):
        send[:, c : c + step] = jnp.dot(
            place_tokens, hidden[:, c : c + step], preferred_element_type=F32
        ).astype(BF16)
        cut = pl.ds(c, step + META if c + step == width else step)
        stores.append(pltpu.make_async_copy(send.at[:, cut], send_ref.at[:, cut], sems.at[k]))
        stores[-1].start()
    for store in stores:
        store.wait()


def turn_kernel(place_ref, placed_ref):
    placed_ref[...] = place_ref[...].astype(F32).T.astype(BF16)


def score_half(high, chunks_ref, rows_ref, meta_ref, weight, grad_ref, far_ref, near_ref, acc, ready):
    steps, depth, half = weight.shape
    base = high * half
    for k in range(steps):
        ready(k)
        part = jnp.dot(
            rows_ref[:, k * depth : (k + 1) * depth], weight[k], preferred_element_type=F32
        )
        if k == 0:
            acc[...] = part
        else:
            acc[...] += part
    ready(steps)
    info = meta_ref[...].astype(F32)
    lane = lax.broadcasted_iota(jnp.int32, (1, BLOCK), 1).astype(F32)
    scale = info[:, BLK_DEV : BLK_DEV + 1]
    norm = info[:, BLK_DEV + 1 : BLK_DEV + 2]
    target = info[:, BLK_DEV + 2 : BLK_DEV + 3] * BLOCK + info[:, BLK_DEV + 3 : BLK_DEV + 4]
    for b in range(half // BLOCK):
        first = base + b * BLOCK
        count = info[:, first // BLOCK : first // BLOCK + 1]
        words = slice(b * BLOCK, (b + 1) * BLOCK)
        soft = jnp.where(count > 0, count * jnp.exp(acc[:, words] - norm), 0.0)
        hit = jnp.where(lane + first == target, 1.0, 0.0)
        grad_ref[:, words] = (scale * (soft - hit)).astype(BF16)
    chunk = far_ref.shape[0]
    far = rows_ref.shape[1] // chunk // 2
    near = far - 1 if high else far + 1
    for k, out_ref in ((far, far_ref), (near, near_ref)):
        out_ref[...] = lax.dot_general(
            rows_ref[:, pl.ds(pl.multiple_of(chunks_ref[k] * chunk, chunk), chunk)],
            grad_ref[...],
            CONTRACT_ROWS,
            preferred_element_type=F32,
        ).astype(BF16)


def weight_loads(weight_ref, weight, sems, base):
    steps, depth, half = weight.shape
    return [
        pltpu.make_async_copy(
            weight_ref.at[pl.ds(k * depth, depth), pl.ds(base, half)], weight.at[k], sems.at[0, k]
        )
        for k in range(steps)
    ]


def low_kernel(
    chunks_ref, got_ref, weight_ref, after_ref, rows_ref, meta_ref, grad_ref, far_ref, near_ref, weight, acc, sems
):
    steps, depth, _ = weight.shape
    weights = weight_loads(weight_ref, weight, sems, 0)
    loads = []
    for k in range(steps):
        cut = pl.ds(k * depth, depth)
        loads.append(pltpu.make_async_copy(got_ref.at[:, cut], rows_ref.at[:, cut], sems.at[1, k]))
    last = pltpu.make_async_copy(got_ref.at[:, pl.ds(steps * depth, META)], meta_ref, sems.at[0, steps])
    for k in range(steps):
        weights[k].start()
        loads[k].start()
    last.start()

    def ready(k):
        if k == steps:
            last.wait()
        else:
            weights[k].wait()
            loads[k].wait()

    score_half(0, chunks_ref, rows_ref, meta_ref, weight, grad_ref, far_ref, near_ref, acc, ready)


def high_kernel(
    chunks_ref, rows_ref, meta_ref, weight_ref, grad_ref, far_ref, near_ref, weight, acc, sems
):
    loads = weight_loads(weight_ref, weight, sems, weight.shape[2])
    for load in loads:
        load.start()

    def ready(k):
        if k < len(loads):
            loads[k].wait()

    score_half(1, chunks_ref, rows_ref, meta_ref, weight, grad_ref, far_ref, near_ref, acc, ready)


def back_kernel(low_ref, high_ref, weight_ref, after_ref, part_ref, token_ref, grad, weight, part, sems):
    steps, depth, _ = weight.shape
    half = low_ref.shape[1]
    loads = [
        pltpu.make_async_copy(weight_ref.at[pl.ds(k * depth, depth), :], weight.at[k], sems.at[0, k])
        for k in range(steps)
    ]
    stores = [
        pltpu.make_async_copy(part.at[k], part_ref.at[:, pl.ds(k * depth, depth)], sems.at[1, k])
        for k in range(steps)
    ]
    for load in loads:
        load.start()
    grad[:, :half] = low_ref[...]
    grad[:, half:] = high_ref[...]
    for k in range(steps):
        loads[k].wait()
        part[k] = lax.dot_general(
            grad[...], weight[k], CONTRACT_COLS, preferred_element_type=F32
        ).astype(BF16)
        stores[k].start()
    for store in stores:
        store.wait()
    token_ref[...] = jnp.zeros_like(token_ref)


def add_kernel(chunks_ref, got_ref, rows_ref, grad_ref, after_ref, out_ref, token_ref):
    own = lax.dot_general(rows_ref[...], grad_ref[...], CONTRACT_ROWS, preferred_element_type=F32)
    out_ref[...] = (got_ref[...].astype(F32) + own).astype(BF16)
    token_ref[...] = jnp.zeros_like(token_ref)


def own_kernel(chunks_ref, low_near_ref, high_near_ref, rows_ref, low_ref, high_ref, after_ref, out_ref, token_ref):
    half = low_ref.shape[1]
    token_ref[...] = jnp.zeros_like(token_ref)
    for k, near_ref, grad_ref in ((0, low_near_ref, low_ref), (1, high_near_ref, high_ref)):
        own = lax.dot_general(rows_ref[...], grad_ref[...], CONTRACT_ROWS, preferred_element_type=F32)
        out_ref[:, k * half : (k + 1) * half] = near_ref[...].astype(F32) + own


def last_kernel(low_far_ref, high_far_ref, own_ref, after_ref, out_ref):
    half = low_far_ref.shape[1]
    for k, far_ref in enumerate((low_far_ref, high_far_ref)):
        cut = slice(k * half, (k + 1) * half)
        out_ref[:, cut] = (own_ref[:, cut] + far_ref[...].astype(F32)).astype(BF16)


def sum_kernel(placed_ref, back_ref, after_ref, out_ref, token_ref):
    out_ref[...] = jnp.dot(placed_ref[...], back_ref[...], preferred_element_type=F32).astype(BF16)
    token_ref[...] = jnp.zeros_like(token_ref)


def body(
    hidden,
    output_weight,
    owners,
    negatives,
    negative_mask,
    target_block,
    target_word,
    log_norm,
    cotangent,
):
    tokens, width = hidden.shape
    visits = owners.shape[1]
    peers = lax.axis_size("vocab")
    planes = lax.axis_size("dp")
    words = output_weight.shape[1]
    capacity = max(2, tokens * visits * 4 // (3 * peers))
    slots = peers * capacity
    sent = width + META
    chunk = width // planes
    half = words // 2
    def in_hbm(x):
        return pltpu.with_memory_space_constraint(x, pltpu.HBM)

    anywhere = pl.BlockSpec(memory_space=pl.ANY)
    hbm = pl.BlockSpec(memory_space=pltpu.HBM)
    vmem = pl.BlockSpec(memory_space=pltpu.VMEM)
    smem = pl.BlockSpec(memory_space=pltpu.SMEM)
    far = planes // 2
    near = far - 1

    def whole(*shape):
        return pl.BlockSpec(shape, lambda i: (0,) * len(shape))

    smalls = [
        owners.T,
        negatives.transpose(1, 2, 0),
        negative_mask.transpose(1, 2, 0),
        target_block[None, :],
        target_word[None, :],
        log_norm[None, :],
        cotangent[None, :],
    ]
    send, place = pl.pallas_call(
        functools.partial(place_kernel, capacity),
        grid=(1,),
        in_specs=[hbm] + [whole(*x.shape) for x in smalls],
        out_specs=[hbm, whole(slots, tokens)],
        out_shape=[
            pltpu.HBM((slots, sent), BF16),
            jax.ShapeDtypeStruct((slots, tokens), BF16),
        ],
        scratch_shapes=[
            pltpu.VMEM((tokens, width), BF16),
            pltpu.VMEM((slots, sent), BF16),
            pltpu.SemaphoreType.DMA((width // 512 + 1,)),
        ],
        compiler_params=params(24),
        cost_estimate=cost(0),
        name="place_rows",
    )(*[in_hbm(x) for x in (hidden, *smalls)])
    got = lax.all_to_all(
        send.reshape(peers, capacity, sent), "vocab", split_axis=0, concat_axis=0, tiled=True
    ).reshape(slots, sent)

    placed = pl.pallas_call(
        turn_kernel,
        in_specs=[vmem],
        out_specs=vmem,
        out_shape=jax.ShapeDtypeStruct((tokens, slots), BF16),
        cost_estimate=cost(100),
        compiler_params=params(4),
        name="turn_places",
    )(place)
    weights = in_hbm(output_weight)
    got = in_hbm(got)
    chunks = lax.rem(lax.axis_index("dp") + jnp.arange(planes, dtype=jnp.int32), planes)

    message = jax.ShapeDtypeStruct((chunk, half), BF16)
    grad_half = jax.ShapeDtypeStruct((slots, half), BF16)
    token = jax.ShapeDtypeStruct((8, 128), F32)
    acc = pltpu.VMEM((slots, half), F32)
    half_weight = pltpu.VMEM((STEPS, width // STEPS, half), BF16)
    rows, meta, low, low_far, low_near = pl.pallas_call(
        low_kernel,
        in_specs=[smem, hbm, hbm, anywhere],
        out_specs=[vmem] * 5,
        out_shape=[
            jax.ShapeDtypeStruct((slots, width), BF16),
            jax.ShapeDtypeStruct((slots, META), BF16),
            grad_half,
            message,
            message,
        ],
        scratch_shapes=[half_weight, acc, pltpu.SemaphoreType.DMA((2, STEPS + 1))],
        compiler_params=params(20),
        cost_estimate=cost(0),
        name="low_scores",
    )(chunks, got, weights, placed)
    high, high_far, high_near = pl.pallas_call(
        high_kernel,
        in_specs=[smem, vmem, vmem, hbm],
        out_specs=[vmem] * 3,
        out_shape=[grad_half, message, message],
        scratch_shapes=[half_weight, acc, pltpu.SemaphoreType.DMA((1, STEPS))],
        compiler_params=params(20),
        cost_estimate=cost(LATE_US),
        name="high_scores",
    )(chunks, rows, meta, weights)

    def hop(x, d):
        return lax.ppermute(x, "dp", [(i, (i + d) % planes) for i in range(planes)])

    def rows_spec(k):
        return pl.BlockSpec((slots, chunk), lambda i, c: (0, c[k % planes]))

    message_spec = pl.BlockSpec((chunk, half), lambda i, c: (0, 0))
    token_spec = pl.BlockSpec((8, 128), lambda i, c: (0, 0))

    def state_parts(after):
        return pl.pallas_call(
            back_kernel,
            in_specs=[vmem, vmem, hbm, anywhere],
            out_specs=[hbm, vmem],
            out_shape=[pltpu.HBM((slots, width), BF16), token],
            scratch_shapes=[
                pltpu.VMEM((slots, words), BF16),
                pltpu.VMEM((planes, chunk, words), BF16),
                pltpu.VMEM((planes, slots, chunk), BF16),
                pltpu.SemaphoreType.DMA((2, planes)),
            ],
            compiler_params=params(24),
            cost_estimate=cost(LATE_US),
            name="state_parts",
        )(low, high, weights, after)

    def add(k, grad, arrived, after, us):
        return pl.pallas_call(
            add_kernel,
            grid_spec=pltpu.PrefetchScalarGridSpec(
                num_scalar_prefetch=1,
                grid=(1,),
                in_specs=[message_spec, rows_spec(k), message_spec, anywhere],
                out_specs=[message_spec, token_spec],
            ),
            out_shape=[message, token],
            compiler_params=params(12),
            cost_estimate=cost(us),
            name="add_part",
        )(chunks, arrived, got, grad, after)

    flows = [(1, low, far), (-1, low, near), (-1, high, far), (1, high, near)]
    messages = [low_far, low_near, high_far, high_near]
    after = high_near
    event = 0
    for step in range(far):
        for f, (d, grad, hops) in enumerate(flows):
            if step < hops:
                messages[f] = hop(messages[f], d)
                if step < hops - 1:
                    if event == GAP:
                        part, after = state_parts(after)
                    messages[f], after = add(
                        d * (hops - 1 - step), grad, messages[f], after, HOPS_US[event]
                    )
                    event += 1
    back = lax.all_to_all(
        part.reshape(peers, capacity, width), "vocab", split_axis=0, concat_axis=0, tiled=True
    ).reshape(slots, width)

    own, after = pl.pallas_call(
        own_kernel,
        grid_spec=pltpu.PrefetchScalarGridSpec(
            num_scalar_prefetch=1,
            grid=(1,),
            in_specs=[message_spec] * 2 + [rows_spec(0)] + [message_spec] * 2 + [anywhere],
            out_specs=[pl.BlockSpec((chunk, words), lambda i, c: (0, 0)), token_spec],
        ),
        out_shape=[jax.ShapeDtypeStruct((chunk, words), F32), token],
        compiler_params=params(16),
        cost_estimate=cost(OWN_US),
        name="own_part",
    )(chunks, messages[1], messages[3], got, low, high, after)
    pieces = 4
    hidden_grad, after = pl.pallas_call(
        sum_kernel,
        grid=(pieces,),
        in_specs=[
            whole(tokens, slots),
            pl.BlockSpec((slots, width // pieces), lambda i: (0, i)),
            anywhere,
        ],
        out_specs=[pl.BlockSpec((tokens, width // pieces), lambda i: (0, i)), whole(8, 128)],
        out_shape=[jax.ShapeDtypeStruct((tokens, width), BF16), token],
        compiler_params=params(12),
        cost_estimate=cost(SUM_US),
        name="sum_parts",
    )(placed, in_hbm(back), after)

    weight_grad = pl.pallas_call(
        last_kernel,
        in_specs=[vmem, vmem, vmem, anywhere],
        out_specs=vmem,
        out_shape=jax.ShapeDtypeStruct((chunk, words), BF16),
        compiler_params=params(12),
        cost_estimate=cost(0),
        name="last_add",
    )(messages[0], messages[2], own, after)
    return (hidden_grad, weight_grad)


def solution(mesh):
    placed = (
        P(("dp", "vocab"), None),
        P(None, "vocab"),
        P(("dp", "vocab"), None),
        P(("dp", "vocab"), None, None),
        P(("dp", "vocab"), None, None),
        P(("dp", "vocab")),
        P(("dp", "vocab")),
        P(("dp", "vocab")),
        P(("dp", "vocab")),
    )
    return jax.shard_map(
        body,
        mesh=mesh,
        in_specs=placed,
        out_specs=(P(("dp", "vocab"), None), P("dp", "vocab")),
        check_vma=False,
    )
```

time: 190 us -> 175 us (0.921)
  waiting for transfers between devices: 92 us -> 79.1 us
  local copies, waits for them, and re-layouts: 5.89 us -> 0.01 us
  Pallas kernels: 54.1 us -> 57.4 us
    ppermute x14, waiting for transfers between devices: 39.2 us -> 26.4 us  [hop(): return lax.ppermute(x, 'dp', [(i, (i + d) % planes) for i in range(planes)])]
    unnamed x16 -> x4, local copies, waits for them, and re-layouts: 5.89 us -> 0.01 us
    pallas_call x6 -> x8, Pallas kernels: 30.3 us -> 34.9 us  [the longest x1 8.14 us: state_parts(): pl.pallas_call(back_kernel, in_specs=[vmem, vmem, hbm, anywhere], out_spe...]
  transfers between devices with their start and end apart: 16 -> 16, of which waited for: 11 -> 7; matrix products, arithmetic and copies ran while one was open for 0% -> 0% of each run, Pallas kernels for 15% -> 25%
where the time goes in v3:
time: 175 us; the launch traced here: 174 us
  waiting for transfers between devices  79.1 us (45%)
  Pallas kernels  57.4 us (33%)
  starting transfers between devices  37 us (21%)
    all_to_all x1, waiting for transfers between devices, body(): lax.all_to_all(send.reshape(peers, capacity, sent), 'vocab', split_axis=0...  52.7 us
    ppermute x14, waiting for transfers between devices, hop(): return lax.ppermute(x, 'dp', [(i, (i + d) % planes) for i in range(planes)])  26.4 us
    pallas_call x10, Pallas kernels, add(): pl.pallas_call(add_kernel, grid_spec=pltpu.PrefetchScalarGridSpec(num_sca...  22.5 us
    ppermute x14, starting transfers between devices, hop(): return lax.ppermute(x, 'dp', [(i, (i + d) % planes) for i in range(planes)])  22.2 us
    pallas_call x1, Pallas kernels, state_parts(): pl.pallas_call(back_kernel, in_specs=[vmem, vmem, hbm, anywhere], out_spe...  8.14 us
    all_to_all x1, starting transfers between devices, body(): lax.all_to_all(send.reshape(peers, capacity, sent), 'vocab', split_axis=0...  7.68 us
    pallas_call x1, Pallas kernels, body(): pl.pallas_call(low_kernel, in_specs=[smem, hbm, hbm, anywhere], out_specs...  7.14 us
    all_to_all x1, starting transfers between devices, body(): lax.all_to_all(part.reshape(peers, capacity, width), 'vocab', split_axis=...  7.09 us
  transfers between devices with their start and end apart: 16, of which 7 were waited for; matrix products, arithmetic and copies ran while one was open for 0% of the time, Pallas kernels for 25%

profile of v3, /device:TPU:98, one launch (start us, length us, event | category | flops | bytes accessed | tf_op | source)
XLA Modules:
  0.0 174.3 jit_solution(2872348336208576028)
XLA Ops:
  0.6 4.8 %place_rows.1 = (bf16[512,4224]{1,0:T(8,128)(2,1)}, bf16[512,128]{1,0:T(8,128)(2,1)S(1)}) custom-call(bf16[128,4096]{1,0:T(8,128)(2,1)} %hidden_ref.1, s32[3,128]{1,0:T(4,128)} %bitcast.15, s32[3,2,128]{2,1,0:T(2,128)} %bitcast.13, s32[3,2,128]{2,1,0:T(2,128)} %bitcast.14, s32[1,128]{1,0:T(1,128)} %bitcast.16, s32[1,128]{1,0:T(1,128)} %bitcast.17, ...), custom_call_target="tpu_custom_call" | custom-call | tf_op jit(solution)/shard_map/place_rows/pallas_call | solution.py:300
  5.5 7.7 %all-to-all-start = ((bf16[32,16,4224]{2,1,0:T(8,128)(2,1)}), bf16[32,16,4224]{2,1,0:T(8,128)(2,1)}, u32[]{:S(2)}, u32[]{:S(2)}) async-start(bf16[32,16,4224]{2,1,0:T(8,128)(2,1)} %bitcast.11), calls=%async_computation | async-start | bytes 8650752 | tf_op jit(solution)/shard_map/all_to_all | solution.py:318
  13.3 52.7 %all-to-all-done = bf16[32,16,4224]{2,1,0:T(8,128)(2,1)} async-done(((bf16[32,16,4224]{2,1,0:T(8,128)(2,1)}), bf16[32,16,4224]{2,1,0:T(8,128)(2,1)}, u32[]{:S(2)}, u32[]{:S(2)}) %all-to-all-start) | async-done | bytes 4325408 | tf_op jit(solution)/shard_map/all_to_all | solution.py:318
  66.0 7.1 %low_scores.1 = (bf16[512,4096]{1,0:T(8,128)(2,1)S(1)}, bf16[512,128]{1,0:T(8,128)(2,1)S(1)}, bf16[512,512]{1,0:T(8,128)(2,1)S(1)}, bf16[512,512]{1,0:T(8,128)(2,1)}, bf16[512,512]{1,0:T(8,128)(2,1)}) custom-call(s32[8]{0:T(128)S(1)} %compare_select_fusion.chunks_ref, bf16[512,4224]{1,0:T(8,128)(2,1)} %bitcast.8.got_ref.rows_ref, ...), custom_call_target="tpu_custom_call" | custom-call | tf_op jit(solution)/shard_map/low_scores/pallas_call | solution.py:340
  73.1 3.2 %collective-permute-start.1 = (bf16[512,512]{1,0:T(8,128)(2,1)}, bf16[512,512]{1,0:T(8,128)(2,1)}, u32[]{:S(2)}, u32[]{:S(2)}) collective-permute-start(bf16[512,512]{1,0:T(8,128)(2,1)} %get-tuple-element.47), channel_id=1, source_target_pairs={{0,32},{32,64},{64,96},{96,128},{128,160},{160,192},{192,224},{224... | collective-permute-start | bytes 1572872 | tf_op jit(solution)/shard_map/ppermute | solution.py:368
  76.3 5.3 %high_scores.1 = (bf16[512,512]{1,0:T(8,128)(2,1)S(1)}, bf16[512,512]{1,0:T(8,128)(2,1)S(1)}, bf16[512,512]{1,0:T(8,128)(2,1)S(1)}) custom-call(s32[8]{0:T(128)S(1)} %compare_select_fusion.chunks_ref, bf16[512,4096]{1,0:T(8,128)(2,1)S(1)} %get-tuple-element.41.rows_ref, bf16[512,128]{1,0:T(8,128)(2,1)S(1)} %get-tuple-element.42.meta_ref, ...), custom_call_target="tpu_custom_call" | custom-call | tf_op jit(solution)/shard_map/high_scores/pallas_call | solution.py:356
  81.7 3.5 %collective-permute-start.4 = (bf16[512,512]{1,0:T(8,128)(2,1)S(1)}, bf16[512,512]{1,0:T(8,128)(2,1)S(1)}, u32[]{:S(2)}, u32[]{:S(2)}) collective-permute-start(bf16[512,512]{1,0:T(8,128)(2,1)S(1)} %get-tuple-element.44.after_ref), channel_id=1, source_target_pairs={{0,32},{32,64},{64,96},{96,128},{128,160},{160,192},{192,224},{224... | collective-permute-start | bytes 1572872 | tf_op jit(solution)/shard_map/ppermute | solution.py:368
  85.2 8.1 %state_parts.1 = (bf16[512,4096]{1,0:T(8,128)(2,1)}, f32[8,128]{1,0:T(8,128)S(1)}) custom-call(bf16[512,512]{1,0:T(8,128)(2,1)S(1)} %get-tuple-element.40.low_ref.grad_ref, bf16[512,512]{1,0:T(8,128)(2,1)S(1)} %get-tuple-element.43.high_ref.grad_ref, bf16[4096,1024]{1,0:T(8,128)(2,1)} %weight_ref.5, bf16[512,512]{1,0:T(8,128)(2,1)S(1)} %get-tuple-element.44.after_ref), custom_call_target="tpu_custom_call" | custom-call | tf_op jit(solution)/shard_map/state_parts/pallas_call | solution.py:377
  93.4 7.1 %all-to-all-start.1 = ((bf16[32,16,4096]{2,1,0:T(8,128)(2,1)}), bf16[32,16,4096]{2,1,0:T(8,128)(2,1)}, u32[]{:S(2)}, u32[]{:S(2)}) async-start(bf16[32,16,4096]{2,1,0:T(8,128)(2,1)} %bitcast.12), calls=%async_computation.1 | async-start | bytes 8388608 | tf_op jit(solution)/shard_map/all_to_all | solution.py:423
  100.5 2.2 %add_part.10 = (bf16[512,512]{1,0:T(8,128)(2,1)S(1)}, f32[8,128]{1,0:T(8,128)S(1)}) custom-call(s32[8]{0:T(128)S(1)} %compare_select_fusion.chunks_ref, bf16[512,512]{1,0:T(8,128)(2,1)} %collective-permute-done.1.got_ref, bf16[512,4224]{1,0:T(8,128)(2,1)} %bitcast.8.got_ref.rows_ref, bf16[512,512]{1,0:T(8,128)(2,1)S(1)} %get-tuple-element.40.low_ref.grad_ref, ...), custom_call_target="tpu_custom_call" | custom-call | flops 3449999872 | tf_op jit(solution)/shard_map/add_part/pallas_call | solution.py:394
  102.7 1.8 %collective-permute-start.3 = (bf16[512,512]{1,0:T(8,128)(2,1)S(1)}, bf16[512,512]{1,0:T(8,128)(2,1)S(1)}, u32[]{:S(2)}, u32[]{:S(2)}) collective-permute-start(bf16[512,512]{1,0:T(8,128)(2,1)S(1)} %get-tuple-element.51), channel_id=1, source_target_pairs={{0,32},{32,64},{64,96},{96,128},{128,160},{160,192},{192,224},{224... | collective-permute-start | bytes 1572872 | tf_op jit(solution)/shard_map/ppermute | solution.py:368
  104.5 2.2 %add_part.11 = (bf16[512,512]{1,0:T(8,128)(2,1)S(1)}, f32[8,128]{1,0:T(8,128)S(1)}) custom-call(s32[8]{0:T(128)S(1)} %compare_select_fusion.chunks_ref, bf16[512,512]{1,0:T(8,128)(2,1)} %collective-permute-done.got_ref, bf16[512,4224]{1,0:T(8,128)(2,1)} %bitcast.8.got_ref.rows_ref, bf16[512,512]{1,0:T(8,128)(2,1)S(1)} %get-tuple-element.40.low_ref.grad_ref, ...), custom_call_target="tpu_custom_call" | custom-call | flops 3449999872 | tf_op jit(solution)/shard_map/add_part/pallas_call | solution.py:394
  107.1 2.1 %add_part.12 = (bf16[512,512]{1,0:T(8,128)(2,1)S(1)}, f32[8,128]{1,0:T(8,128)S(1)}) custom-call(s32[8]{0:T(128)S(1)} %compare_select_fusion.chunks_ref, bf16[512,512]{1,0:T(8,128)(2,1)S(1)} %collective-permute-done.5.got_ref, bf16[512,4224]{1,0:T(8,128)(2,1)} %bitcast.8.got_ref.rows_ref, bf16[512,512]{1,0:T(8,128)(2,1)S(1)} %get-tuple-element.43.high_ref.grad_ref, ...), custom_call_target="tpu_custom_call" | custom-call | flops 3449999872 | tf_op jit(solution)/shard_map/add_part/pallas_call | solution.py:394
  109.3 2.1 %add_part.13 = (bf16[512,512]{1,0:T(8,128)(2,1)S(1)}, f32[8,128]{1,0:T(8,128)S(1)}) custom-call(s32[8]{0:T(128)S(1)} %compare_select_fusion.chunks_ref, bf16[512,512]{1,0:T(8,128)(2,1)S(1)} %collective-permute-done.4.got_ref, bf16[512,4224]{1,0:T(8,128)(2,1)} %bitcast.8.got_ref.rows_ref, bf16[512,512]{1,0:T(8,128)(2,1)S(1)} %get-tuple-element.43.high_ref.grad_ref, ...), custom_call_target="tpu_custom_call" | custom-call | flops 3449999872 | tf_op jit(solution)/shard_map/add_part/pallas_call | solution.py:394
  111.3 3.3 %collective-permute-start.7 = (bf16[512,512]{1,0:T(8,128)(2,1)S(1)}, bf16[512,512]{1,0:T(8,128)(2,1)S(1)}, u32[]{:S(2)}, u32[]{:S(2)}) collective-permute-start(bf16[512,512]{1,0:T(8,128)(2,1)S(1)} %get-tuple-element.58), channel_id=1, source_target_pairs={{0,32},{32,64},{64,96},{96,128},{128,160},{160,192},{192,224},{224... | collective-permute-start | bytes 1572872 | tf_op jit(solution)/shard_map/ppermute | solution.py:368
  114.6 2.9 %collective-permute-done.3.got_ref = bf16[512,512]{1,0:T(8,128)(2,1)S(1)} collective-permute-done((bf16[512,512]{1,0:T(8,128)(2,1)S(1)}, bf16[512,512]{1,0:T(8,128)(2,1)S(1)}, u32[]{:S(2)}, u32[]{:S(2)}) %collective-permute-start.3) | collective-permute-done | bytes 524320 | tf_op jit(solution)/shard_map/ppermute | solution.py:368
  117.5 2.1 %add_part.14 = (bf16[512,512]{1,0:T(8,128)(2,1)S(1)}, f32[8,128]{1,0:T(8,128)S(1)}) custom-call(s32[8]{0:T(128)S(1)} %compare_select_fusion.chunks_ref, bf16[512,512]{1,0:T(8,128)(2,1)S(1)} %collective-permute-done.3.got_ref, bf16[512,4224]{1,0:T(8,128)(2,1)} %bitcast.8.got_ref.rows_ref, bf16[512,512]{1,0:T(8,128)(2,1)S(1)} %get-tuple-element.40.low_ref.grad_ref, ...), custom_call_target="tpu_custom_call" | custom-call | flops 3449999872 | tf_op jit(solution)/shard_map/add_part/pallas_call | solution.py:394
  119.6 3.0 %collective-permute-start.11 = (bf16[512,512]{1,0:T(8,128)(2,1)S(1)}, bf16[512,512]{1,0:T(8,128)(2,1)S(1)}, u32[]{:S(2)}, u32[]{:S(2)}) collective-permute-start(bf16[512,512]{1,0:T(8,128)(2,1)S(1)} %get-tuple-element.64), channel_id=1, source_target_pairs={{0,32},{32,64},{64,96},{96,128},{128,160},{160,192},{192,224},{224... | collective-permute-start | bytes 1572872 | tf_op jit(solution)/shard_map/ppermute | solution.py:368
  122.8 2.1 %add_part.15 = (bf16[512,512]{1,0:T(8,128)(2,1)S(1)}, f32[8,128]{1,0:T(8,128)S(1)}) custom-call(s32[8]{0:T(128)S(1)} %compare_select_fusion.chunks_ref, bf16[512,512]{1,0:T(8,128)(2,1)S(1)} %collective-permute-done.2.got_ref, bf16[512,4224]{1,0:T(8,128)(2,1)} %bitcast.8.got_ref.rows_ref, bf16[512,512]{1,0:T(8,128)(2,1)S(1)} %get-tuple-element.40.low_ref.grad_ref, ...), custom_call_target="tpu_custom_call" | custom-call | flops 3449999872 | tf_op jit(solution)/shard_map/add_part/pallas_call | solution.py:394
  124.9 8.1 %collective-permute-done.8.got_ref = bf16[512,512]{1,0:T(8,128)(2,1)S(1)} collective-permute-done((bf16[512,512]{1,0:T(8,128)(2,1)S(1)}, bf16[512,512]{1,0:T(8,128)(2,1)S(1)}, u32[]{:S(2)}, u32[]{:S(2)}) %collective-permute-start.8) | collective-permute-done | bytes 524320 | tf_op jit(solution)/shard_map/ppermute | solution.py:368
  133.0 2.1 %add_part.16 = (bf16[512,512]{1,0:T(8,128)(2,1)S(1)}, f32[8,128]{1,0:T(8,128)S(1)}) custom-call(s32[8]{0:T(128)S(1)} %compare_select_fusion.chunks_ref, bf16[512,512]{1,0:T(8,128)(2,1)S(1)} %collective-permute-done.8.got_ref, bf16[512,4224]{1,0:T(8,128)(2,1)} %bitcast.8.got_ref.rows_ref, bf16[512,512]{1,0:T(8,128)(2,1)S(1)} %get-tuple-element.43.high_ref.grad_ref, ...), custom_call_target="tpu_custom_call" | custom-call | flops 3449999872 | tf_op jit(solution)/shard_map/add_part/pallas_call | solution.py:394
  135.1 2.1 %add_part.17 = (bf16[512,512]{1,0:T(8,128)(2,1)S(1)}, f32[8,128]{1,0:T(8,128)S(1)}) custom-call(s32[8]{0:T(128)S(1)} %compare_select_fusion.chunks_ref, bf16[512,512]{1,0:T(8,128)(2,1)S(1)} %collective-permute-done.7.got_ref, bf16[512,4224]{1,0:T(8,128)(2,1)} %bitcast.8.got_ref.rows_ref, bf16[512,512]{1,0:T(8,128)(2,1)S(1)} %get-tuple-element.43.high_ref.grad_ref, ...), custom_call_target="tpu_custom_call" | custom-call | flops 3449999872 | tf_op jit(solution)/shard_map/add_part/pallas_call | solution.py:394
  137.2 3.5 %collective-permute-start.9 = (bf16[512,512]{1,0:T(8,128)(2,1)S(1)}, bf16[512,512]{1,0:T(8,128)(2,1)S(1)}, u32[]{:S(2)}, u32[]{:S(2)}) collective-permute-start(bf16[512,512]{1,0:T(8,128)(2,1)S(1)} %get-tuple-element.62), channel_id=1, source_target_pairs={{0,32},{32,64},{64,96},{96,128},{128,160},{160,192},{192,224},{224... | collective-permute-start | bytes 1572872 | tf_op jit(solution)/shard_map/ppermute | solution.py:368
  140.7 2.9 %add_part.18 = (bf16[512,512]{1,0:T(8,128)(2,1)}, f32[8,128]{1,0:T(8,128)S(1)}) custom-call(s32[8]{0:T(128)S(1)} %compare_select_fusion.chunks_ref, bf16[512,512]{1,0:T(8,128)(2,1)S(1)} %collective-permute-done.11.got_ref, bf16[512,4224]{1,0:T(8,128)(2,1)} %bitcast.8.got_ref.rows_ref, bf16[512,512]{1,0:T(8,128)(2,1)S(1)} %get-tuple-element.40.low_ref.grad_ref, ...), custom_call_target="tpu_custom_call" | custom-call | flops 3449999872 | tf_op jit(solution)/shard_map/add_part/pallas_call | solution.py:394
  143.6 7.6 %collective-permute-done.10.got_ref = bf16[512,512]{1,0:T(8,128)(2,1)S(1)} collective-permute-done((bf16[512,512]{1,0:T(8,128)(2,1)S(1)}, bf16[512,512]{1,0:T(8,128)(2,1)S(1)}, u32[]{:S(2)}, u32[]{:S(2)}) %collective-permute-start.10) | collective-permute-done | bytes 524320 | tf_op jit(solution)/shard_map/ppermute | solution.py:368
  151.2 2.9 %add_part.19 = (bf16[512,512]{1,0:T(8,128)(2,1)}, f32[8,128]{1,0:T(8,128)S(1)}) custom-call(s32[8]{0:T(128)S(1)} %compare_select_fusion.chunks_ref, bf16[512,512]{1,0:T(8,128)(2,1)S(1)} %collective-permute-done.10.got_ref, bf16[512,4224]{1,0:T(8,128)(2,1)} %bitcast.8.got_ref.rows_ref, bf16[512,512]{1,0:T(8,128)(2,1)S(1)} %get-tuple-element.43.high_ref.grad_ref, ...), custom_call_target="tpu_custom_call" | custom-call | flops 3449999872 | tf_op jit(solution)/shard_map/add_part/pallas_call | solution.py:394
  154.1 3.2 %collective-permute-start.12 = (bf16[512,512]{1,0:T(8,128)(2,1)}, bf16[512,512]{1,0:T(8,128)(2,1)}, u32[]{:S(2)}, u32[]{:S(2)}) collective-permute-start(bf16[512,512]{1,0:T(8,128)(2,1)} %get-tuple-element.70), channel_id=1, source_target_pairs={{0,32},{32,64},{64,96},{96,128},{128,160},{160,192},{192,224},{224... | collective-permute-start | bytes 1572872 | tf_op jit(solution)/shard_map/ppermute | solution.py:368
  157.3 5.1 %collective-permute-done.6.low_near_ref = bf16[512,512]{1,0:T(8,128)(2,1)S(1)} collective-permute-done((bf16[512,512]{1,0:T(8,128)(2,1)S(1)}, bf16[512,512]{1,0:T(8,128)(2,1)S(1)}, u32[]{:S(2)}, u32[]{:S(2)}) %collective-permute-start.6) | collective-permute-done | bytes 524320 | tf_op jit(solution)/shard_map/ppermute | solution.py:368
  162.4 2.3 %own_part.1 = (f32[512,1024]{1,0:T(8,128)S(1)}, f32[8,128]{1,0:T(8,128)S(1)}) custom-call(s32[8]{0:T(128)S(1)} %compare_select_fusion.chunks_ref, bf16[512,512]{1,0:T(8,128)(2,1)S(1)} %collective-permute-done.6.low_near_ref, bf16[512,512]{1,0:T(8,128)(2,1)S(1)} %collective-permute-done.9.high_near_ref, bf16[512,4224]{1,0:T(8,128)(2,1)} %bitcast.8.got_ref.rows_ref, ...), custom_call_target="tpu_custom_call" | custom-call | flops 115000000512 | tf_op jit(solution)/shard_map/own_part/pallas_call | solution.py:427
  164.8 4.6 %sum_parts.1 = (bf16[128,4096]{1,0:T(8,128)(2,1)}, f32[8,128]{1,0:T(8,128)S(1)}) custom-call(bf16[128,512]{1,0:T(8,128)(2,1)S(1)} %copy-done.1, bf16[512,4096]{1,0:T(8,128)(2,1)} %bitcast.10.back_ref, f32[8,128]{1,0:T(8,128)S(1)} %get-tuple-element.68.after_ref), custom_call_target="tpu_custom_call" | custom-call | tf_op jit(solution)/shard_map/sum_parts/pallas_call | solution.py:441
  169.4 2.5 %collective-permute-done.13.high_far_ref = bf16[512,512]{1,0:T(8,128)(2,1)} collective-permute-done((bf16[512,512]{1,0:T(8,128)(2,1)}, bf16[512,512]{1,0:T(8,128)(2,1)}, u32[]{:S(2)}, u32[]{:S(2)}) %collective-permute-start.13) | collective-permute-done | bytes 524320 | tf_op jit(solution)/shard_map/ppermute | solution.py:368
  171.8 2.4 %last_add.1 = bf16[512,1024]{1,0:T(8,128)(2,1)} custom-call(bf16[512,512]{1,0:T(8,128)(2,1)} %collective-permute-done.12.low_far_ref, bf16[512,512]{1,0:T(8,128)(2,1)} %collective-permute-done.13.high_far_ref, f32[512,1024]{1,0:T(8,128)S(1)} %get-tuple-element.72.own_ref, f32[8,128]{1,0:T(8,128)S(1)} %get-tuple-element.73.after_ref), custom_call_target="tpu_custom_call" | custom-call | tf_op jit(solution)/shard_map/last_add/pallas_call | solution.py:456
  (23 shorter events, 1.0 us)
Async XLA Ops:
  5.5 60.5 %all-to-all-start = ((bf16[32,16,4224]{2,1,0:T(8,128)(2,1)}), bf16[32,16,4224]{2,1,0:T(8,128)(2,1)}, u32[]{:S(2)}, u32[]{:S(2)}) async-start(bf16[32,16,4224]{2,1,0:T(8,128)(2,1)} %bitcast.11), calls=%async_computation | async-start | bytes 8650752 | tf_op jit(solution)/shard_map/all_to_all | solution.py:318
  13.3 59.9 %copy-start = (bf16[128,512]{1,0:T(8,128)(2,1)}, bf16[128,512]{1,0:T(8,128)(2,1)S(1)}, u32[]{:S(2)}) copy-start(bf16[128,512]{1,0:T(8,128)(2,1)S(1)} %turn_places.1.after_ref.placed_ref) | copy-start | bytes 393220
  73.1 27.3 %collective-permute-start.1 = (bf16[512,512]{1,0:T(8,128)(2,1)}, bf16[512,512]{1,0:T(8,128)(2,1)}, u32[]{:S(2)}, u32[]{:S(2)}) collective-permute-start(bf16[512,512]{1,0:T(8,128)(2,1)} %get-tuple-element.47), channel_id=1, source_target_pairs={{0,32},{32,64},{64,96},{96,128},{128,160},{160,192},{192,224},{224... | collective-permute-start | bytes 1572872 | tf_op jit(solution)/shard_map/ppermute | solution.py:368
  76.3 28.2 %collective-permute-start = (bf16[512,512]{1,0:T(8,128)(2,1)}, bf16[512,512]{1,0:T(8,128)(2,1)}, u32[]{:S(2)}, u32[]{:S(2)}) collective-permute-start(bf16[512,512]{1,0:T(8,128)(2,1)} %get-tuple-element.46), channel_id=1, source_target_pairs={{0,224},{32,0},{64,32},{96,64},{128,96},{160,128},{192,160},{224,1... | collective-permute-start | bytes 1572872 | tf_op jit(solution)/shard_map/ppermute | solution.py:368
  81.7 25.4 %collective-permute-start.5 = (bf16[512,512]{1,0:T(8,128)(2,1)S(1)}, bf16[512,512]{1,0:T(8,128)(2,1)S(1)}, u32[]{:S(2)}, u32[]{:S(2)}) collective-permute-start(bf16[512,512]{1,0:T(8,128)(2,1)S(1)} %get-tuple-element.52), channel_id=1, source_target_pairs={{0,224},{32,0},{64,32},{96,64},{128,96},{160,128},{192,160},{224,1... | collective-permute-start | bytes 1572872 | tf_op jit(solution)/shard_map/ppermute | solution.py:368
  81.7 27.5 %collective-permute-start.4 = (bf16[512,512]{1,0:T(8,128)(2,1)S(1)}, bf16[512,512]{1,0:T(8,128)(2,1)S(1)}, u32[]{:S(2)}, u32[]{:S(2)}) collective-permute-start(bf16[512,512]{1,0:T(8,128)(2,1)S(1)} %get-tuple-element.44.after_ref), channel_id=1, source_target_pairs={{0,32},{32,64},{64,96},{96,128},{128,160},{160,192},{192,224},{224... | collective-permute-start | bytes 1572872 | tf_op jit(solution)/shard_map/ppermute | solution.py:368
  93.4 71.4 %all-to-all-start.1 = ((bf16[32,16,4096]{2,1,0:T(8,128)(2,1)}), bf16[32,16,4096]{2,1,0:T(8,128)(2,1)}, u32[]{:S(2)}, u32[]{:S(2)}) async-start(bf16[32,16,4096]{2,1,0:T(8,128)(2,1)} %bitcast.12), calls=%async_computation.1 | async-start | bytes 8388608 | tf_op jit(solution)/shard_map/all_to_all | solution.py:423
  102.7 14.8 %collective-permute-start.3 = (bf16[512,512]{1,0:T(8,128)(2,1)S(1)}, bf16[512,512]{1,0:T(8,128)(2,1)S(1)}, u32[]{:S(2)}, u32[]{:S(2)}) collective-permute-start(bf16[512,512]{1,0:T(8,128)(2,1)S(1)} %get-tuple-element.51), channel_id=1, source_target_pairs={{0,32},{32,64},{64,96},{96,128},{128,160},{160,192},{192,224},{224... | collective-permute-start | bytes 1572872 | tf_op jit(solution)/shard_map/ppermute | solution.py:368
  106.7 16.1 %collective-permute-start.2 = (bf16[512,512]{1,0:T(8,128)(2,1)S(1)}, bf16[512,512]{1,0:T(8,128)(2,1)S(1)}, u32[]{:S(2)}, u32[]{:S(2)}) collective-permute-start(bf16[512,512]{1,0:T(8,128)(2,1)S(1)} %get-tuple-element.50), channel_id=1, source_target_pairs={{0,224},{32,0},{64,32},{96,64},{128,96},{160,128},{192,160},{224,1... | collective-permute-start | bytes 1572872 | tf_op jit(solution)/shard_map/ppermute | solution.py:368
  109.2 23.8 %collective-permute-start.8 = (bf16[512,512]{1,0:T(8,128)(2,1)S(1)}, bf16[512,512]{1,0:T(8,128)(2,1)S(1)}, u32[]{:S(2)}, u32[]{:S(2)}) collective-permute-start(bf16[512,512]{1,0:T(8,128)(2,1)S(1)} %get-tuple-element.59), channel_id=1, source_target_pairs={{0,224},{32,0},{64,32},{96,64},{128,96},{160,128},{192,160},{224,1... | collective-permute-start | bytes 1572872 | tf_op jit(solution)/shard_map/ppermute | solution.py:368
  111.3 23.8 %collective-permute-start.7 = (bf16[512,512]{1,0:T(8,128)(2,1)S(1)}, bf16[512,512]{1,0:T(8,128)(2,1)S(1)}, u32[]{:S(2)}, u32[]{:S(2)}) collective-permute-start(bf16[512,512]{1,0:T(8,128)(2,1)S(1)} %get-tuple-element.58), channel_id=1, source_target_pairs={{0,32},{32,64},{64,96},{96,128},{128,160},{160,192},{192,224},{224... | collective-permute-start | bytes 1572872 | tf_op jit(solution)/shard_map/ppermute | solution.py:368
  119.6 21.1 %collective-permute-start.11 = (bf16[512,512]{1,0:T(8,128)(2,1)S(1)}, bf16[512,512]{1,0:T(8,128)(2,1)S(1)}, u32[]{:S(2)}, u32[]{:S(2)}) collective-permute-start(bf16[512,512]{1,0:T(8,128)(2,1)S(1)} %get-tuple-element.64), channel_id=1, source_target_pairs={{0,32},{32,64},{64,96},{96,128},{128,160},{160,192},{192,224},{224... | collective-permute-start | bytes 1572872 | tf_op jit(solution)/shard_map/ppermute | solution.py:368
  135.0 16.1 %collective-permute-start.10 = (bf16[512,512]{1,0:T(8,128)(2,1)S(1)}, bf16[512,512]{1,0:T(8,128)(2,1)S(1)}, u32[]{:S(2)}, u32[]{:S(2)}) collective-permute-start(bf16[512,512]{1,0:T(8,128)(2,1)S(1)} %get-tuple-element.63), channel_id=1, source_target_pairs={{0,224},{32,0},{64,32},{96,64},{128,96},{160,128},{192,160},{224,1... | collective-permute-start | bytes 1572872 | tf_op jit(solution)/shard_map/ppermute | solution.py:368
  137.2 20.1 %collective-permute-start.9 = (bf16[512,512]{1,0:T(8,128)(2,1)S(1)}, bf16[512,512]{1,0:T(8,128)(2,1)S(1)}, u32[]{:S(2)}, u32[]{:S(2)}) collective-permute-start(bf16[512,512]{1,0:T(8,128)(2,1)S(1)} %get-tuple-element.62), channel_id=1, source_target_pairs={{0,32},{32,64},{64,96},{96,128},{128,160},{160,192},{192,224},{224... | collective-permute-start | bytes 1572872 | tf_op jit(solution)/shard_map/ppermute | solution.py:368
  140.7 21.7 %collective-permute-start.6 = (bf16[512,512]{1,0:T(8,128)(2,1)S(1)}, bf16[512,512]{1,0:T(8,128)(2,1)S(1)}, u32[]{:S(2)}, u32[]{:S(2)}) collective-permute-start(bf16[512,512]{1,0:T(8,128)(2,1)S(1)} %get-tuple-element.57), channel_id=1, source_target_pairs={{0,224},{32,0},{64,32},{96,64},{128,96},{160,128},{192,160},{224,1... | collective-permute-start | bytes 1572872 | tf_op jit(solution)/shard_map/ppermute | solution.py:368
  154.1 17.8 %collective-permute-start.13 = (bf16[512,512]{1,0:T(8,128)(2,1)}, bf16[512,512]{1,0:T(8,128)(2,1)}, u32[]{:S(2)}, u32[]{:S(2)}) collective-permute-start(bf16[512,512]{1,0:T(8,128)(2,1)} %get-tuple-element.71), channel_id=1, source_target_pairs={{0,224},{32,0},{64,32},{96,64},{128,96},{160,128},{192,160},{224,1... | collective-permute-start | bytes 1572872 | tf_op jit(solution)/shard_map/ppermute | solution.py:368
  154.1 17.8 %collective-permute-start.12 = (bf16[512,512]{1,0:T(8,128)(2,1)}, bf16[512,512]{1,0:T(8,128)(2,1)}, u32[]{:S(2)}, u32[]{:S(2)}) collective-permute-start(bf16[512,512]{1,0:T(8,128)(2,1)} %get-tuple-element.70), channel_id=1, source_target_pairs={{0,32},{32,64},{64,96},{96,128},{128,160},{160,192},{192,224},{224... | collective-permute-start | bytes 1572872 | tf_op jit(solution)/shard_map/ppermute | solution.py:368
  162.4 2.4 %copy-start.1 = (bf16[128,512]{1,0:T(8,128)(2,1)S(1)}, bf16[128,512]{1,0:T(8,128)(2,1)}, u32[]{:S(2)}) copy-start(bf16[128,512]{1,0:T(8,128)(2,1)} %copy-done) | copy-start | bytes 393220

commit v4 on v3

--- a/solution.py
+++ b/solution.py
@@ -12,11 +12,12 @@
 META = 128
 GAP = 0
 STEPS = 4
+LOW_BLOCKS = 5
 MIB = 1 << 20
 F32 = jnp.float32
 BF16 = jnp.bfloat16
 HOPS_US = (3,) * 10
-OWN_US, SUM_US, LATE_US = 100, 0, 0
+OWN_US, SUM_US, HIGH_US, STATE_US, LAST_US = 100, 0, 0, 0, 0
 
 
 def cost(us):
@@ -116,9 +117,8 @@
     placed_ref[...] = place_ref[...].astype(F32).T.astype(BF16)
 
 
-def score_half(high, chunks_ref, rows_ref, meta_ref, weight, grad_ref, far_ref, near_ref, acc, ready):
+def score_half(base, chunks_ref, rows_ref, meta_ref, weight, grad_ref, far_ref, near_ref, acc, ready):
     steps, depth, half = weight.shape
-    base = high * half
     for k in range(steps):
         ready(k)
         part = jnp.dot(
@@ -143,7 +143,7 @@
         grad_ref[:, words] = (scale * (soft - hit)).astype(BF16)
     chunk = far_ref.shape[0]
     far = rows_ref.shape[1] // chunk // 2
-    near = far - 1 if high else far + 1
+    near = far - 1 if base else far + 1
     for k, out_ref in ((far, far_ref), (near, near_ref)):
         out_ref[...] = lax.dot_general(
             rows_ref[:, pl.ds(pl.multiple_of(chunks_ref[k] * chunk, chunk), chunk)],
@@ -154,29 +154,44 @@
 
 
 def weight_loads(weight_ref, weight, sems, base):
-    steps, depth, half = weight.shape
+    steps, depth, some = weight.shape
     return [
         pltpu.make_async_copy(
-            weight_ref.at[pl.ds(k * depth, depth), pl.ds(base, half)], weight.at[k], sems.at[0, k]
+            weight_ref.at[pl.ds(k * depth, depth), pl.ds(base, some)], weight.at[k], sems.at[k]
         )
         for k in range(steps)
     ]
 
 
 def low_kernel(
-    chunks_ref, got_ref, weight_ref, after_ref, rows_ref, meta_ref, grad_ref, far_ref, near_ref, weight, acc, sems
+    chunks_ref,
+    got_ref,
+    weight_ref,
+    after_ref,
+    rows_ref,
+    meta_ref,
+    low_weight,
+    high_weight,
+    grad_ref,
+    far_ref,
+    near_ref,
+    acc,
+    sems,
 ):
-    steps, depth, _ = weight.shape
-    weights = weight_loads(weight_ref, weight, sems, 0)
+    steps, depth, some = low_weight.shape
+    weights = weight_loads(weight_ref, low_weight, sems.at[0], 0)
+    others = weight_loads(weight_ref, high_weight, sems.at[1], some)
     loads = []
     for k in range(steps):
         cut = pl.ds(k * depth, depth)
-        loads.append(pltpu.make_async_copy(got_ref.at[:, cut], rows_ref.at[:, cut], sems.at[1, k]))
-    last = pltpu.make_async_copy(got_ref.at[:, pl.ds(steps * depth, META)], meta_ref, sems.at[0, steps])
+        loads.append(pltpu.make_async_copy(got_ref.at[:, cut], rows_ref.at[:, cut], sems.at[2, k]))
+    last = pltpu.make_async_copy(got_ref.at[:, pl.ds(steps * depth, META)], meta_ref, sems.at[3, 0])
     for k in range(steps):
         weights[k].start()
         loads[k].start()
     last.start()
+    for other in others:
+        other.start()
 
     def ready(k):
         if k == steps:
@@ -185,43 +200,35 @@
             weights[k].wait()
             loads[k].wait()
 
-    score_half(0, chunks_ref, rows_ref, meta_ref, weight, grad_ref, far_ref, near_ref, acc, ready)
-
-
-def high_kernel(
-    chunks_ref, rows_ref, meta_ref, weight_ref, grad_ref, far_ref, near_ref, weight, acc, sems
+    score_half(0, chunks_ref, rows_ref, meta_ref, low_weight, grad_ref, far_ref, near_ref, acc, ready)
+    for other in others:
+        other.wait()
+
+
+def high_kernel(base, chunks_ref, rows_ref, meta_ref, weight, grad_ref, far_ref, near_ref, acc):
+    score_half(
+        base, chunks_ref, rows_ref, meta_ref, weight, grad_ref, far_ref, near_ref, acc, lambda k: None
+    )
+
+
+def back_kernel(
+    low_ref, high_ref, low_weight, high_weight, after_ref, part_ref, token_ref, part, sems
 ):
-    loads = weight_loads(weight_ref, weight, sems, weight.shape[2])
-    for load in loads:
-        load.start()
-
-    def ready(k):
-        if k < len(loads):
-            loads[k].wait()
-
-    score_half(1, chunks_ref, rows_ref, meta_ref, weight, grad_ref, far_ref, near_ref, acc, ready)
-
-
-def back_kernel(low_ref, high_ref, weight_ref, after_ref, part_ref, token_ref, grad, weight, part, sems):
-    steps, depth, _ = weight.shape
-    half = low_ref.shape[1]
-    loads = [
-        pltpu.make_async_copy(weight_ref.at[pl.ds(k * depth, depth), :], weight.at[k], sems.at[0, k])
-        for k in range(steps)
-    ]
-    stores = [
-        pltpu.make_async_copy(part.at[k], part_ref.at[:, pl.ds(k * depth, depth)], sems.at[1, k])
-        for k in range(steps)
-    ]
-    for load in loads:
-        load.start()
-    grad[:, :half] = low_ref[...]
-    grad[:, half:] = high_ref[...]
-    for k in range(steps):
-        loads[k].wait()
-        part[k] = lax.dot_general(
-            grad[...], weight[k], CONTRACT_COLS, preferred_element_type=F32
-        ).astype(BF16)
+    steps, depth, _ = low_weight.shape
+    pieces, _, piece = part.shape
+    stores = []
+    for k in range(pieces):
+        step, place = divmod(k * piece, depth)
+        cut = slice(place, place + piece)
+        total = lax.dot_general(
+            low_ref[...], low_weight[step, cut, :], CONTRACT_COLS, preferred_element_type=F32
+        ) + lax.dot_general(
+            high_ref[...], high_weight[step, cut, :], CONTRACT_COLS, preferred_element_type=F32
+        )
+        part[k] = total.astype(BF16)
+        stores.append(
+            pltpu.make_async_copy(part.at[k], part_ref.at[:, pl.ds(k * piece, piece)], sems.at[k])
+        )
         stores[k].start()
     for store in stores:
         store.wait()
@@ -234,23 +241,49 @@
     token_ref[...] = jnp.zeros_like(token_ref)
 
 
-def own_kernel(chunks_ref, low_near_ref, high_near_ref, rows_ref, low_ref, high_ref, after_ref, out_ref, token_ref):
-    half = low_ref.shape[1]
+def own_kernel(
+    chunks_ref, low_near_ref, high_near_ref, rows_ref, low_ref, high_ref, after_ref, out_ref, token_ref
+):
     token_ref[...] = jnp.zeros_like(token_ref)
-    for k, near_ref, grad_ref in ((0, low_near_ref, low_ref), (1, high_near_ref, high_ref)):
+    base = 0
+    for near_ref, grad_ref in ((low_near_ref, low_ref), (high_near_ref, high_ref)):
         own = lax.dot_general(rows_ref[...], grad_ref[...], CONTRACT_ROWS, preferred_element_type=F32)
-        out_ref[:, k * half : (k + 1) * half] = near_ref[...].astype(F32) + own
-
-
-def last_kernel(low_far_ref, high_far_ref, own_ref, after_ref, out_ref):
-    half = low_far_ref.shape[1]
-    for k, far_ref in enumerate((low_far_ref, high_far_ref)):
-        cut = slice(k * half, (k + 1) * half)
-        out_ref[:, cut] = (own_ref[:, cut] + far_ref[...].astype(F32)).astype(BF16)
-
-
-def sum_kernel(placed_ref, back_ref, after_ref, out_ref, token_ref):
-    out_ref[...] = jnp.dot(placed_ref[...], back_ref[...], preferred_element_type=F32).astype(BF16)
+        out_ref[:, base : base + grad_ref.shape[1]] = near_ref[...].astype(F32) + own
+        base += grad_ref.shape[1]
+
+
+def last_kernel(low_far_ref, high_far_ref, own_ref, after_ref, out_ref, out, sems):
+    pieces = sems.shape[0]
+    piece = out.shape[0] // pieces
+    base = low_far_ref.shape[1]
+    stores = []
+    for k in range(pieces):
+        rows = slice(k * piece, (k + 1) * piece)
+        out[rows, :base] = (own_ref[rows, :base] + low_far_ref[rows, :].astype(F32)).astype(BF16)
+        out[rows, base:] = (own_ref[rows, base:] + high_far_ref[rows, :].astype(F32)).astype(BF16)
+        cut = pl.ds(k * piece, piece)
+        stores.append(pltpu.make_async_copy(out.at[cut, :], out_ref.at[cut, :], sems.at[k]))
+        stores[k].start()
+    for store in stores:
+        store.wait()
+
+
+def sum_kernel(placed_ref, back_ref, after_ref, out_ref, token_ref, back, out, sems):
+    pieces = sems.shape[1]
+    piece = back.shape[1] // pieces
+    loads, stores = [], []
+    for k in range(pieces):
+        cut = pl.ds(k * piece, piece)
+        loads.append(pltpu.make_async_copy(back_ref.at[:, cut], back.at[:, cut], sems.at[0, k]))
+        stores.append(pltpu.make_async_copy(out.at[:, cut], out_ref.at[:, cut], sems.at[1, k]))
+        loads[k].start()
+    for k in range(pieces):
+        loads[k].wait()
+        cut = slice(k * piece, (k + 1) * piece)
+        out[:, cut] = jnp.dot(placed_ref[...], back[:, cut], preferred_element_type=F32).astype(BF16)
+        stores[k].start()
+    for store in stores:
+        store.wait()
     token_ref[...] = jnp.zeros_like(token_ref)
 
 
@@ -274,7 +307,7 @@
     slots = peers * capacity
     sent = width + META
     chunk = width // planes
-    half = words // 2
+    base = LOW_BLOCKS * BLOCK
     def in_hbm(x):
         return pltpu.with_memory_space_constraint(x, pltpu.HBM)
 
@@ -332,37 +365,40 @@
     got = in_hbm(got)
     chunks = lax.rem(lax.axis_index("dp") + jnp.arange(planes, dtype=jnp.int32), planes)
 
-    message = jax.ShapeDtypeStruct((chunk, half), BF16)
-    grad_half = jax.ShapeDtypeStruct((slots, half), BF16)
+    def like(*shape):
+        return jax.ShapeDtypeStruct(shape, BF16)
+
     token = jax.ShapeDtypeStruct((8, 128), F32)
-    acc = pltpu.VMEM((slots, half), F32)
-    half_weight = pltpu.VMEM((STEPS, width // STEPS, half), BF16)
-    rows, meta, low, low_far, low_near = pl.pallas_call(
+    depth = width // STEPS
+    rest = words - base
+    rows, meta, low_weight, high_weight, low, low_far, low_near = pl.pallas_call(
         low_kernel,
         in_specs=[smem, hbm, hbm, anywhere],
-        out_specs=[vmem] * 5,
+        out_specs=[vmem] * 7,
         out_shape=[
-            jax.ShapeDtypeStruct((slots, width), BF16),
-            jax.ShapeDtypeStruct((slots, META), BF16),
-            grad_half,
-            message,
-            message,
+            like(slots, width),
+            like(slots, META),
+            like(STEPS, depth, base),
+            like(STEPS, depth, rest),
+            like(slots, base),
+            like(chunk, base),
+            like(chunk, base),
         ],
-        scratch_shapes=[half_weight, acc, pltpu.SemaphoreType.DMA((2, STEPS + 1))],
-        compiler_params=params(20),
+        scratch_shapes=[pltpu.VMEM((slots, base), F32), pltpu.SemaphoreType.DMA((4, STEPS))],
+        compiler_params=params(24),
         cost_estimate=cost(0),
         name="low_scores",
     )(chunks, got, weights, placed)
     high, high_far, high_near = pl.pallas_call(
-        high_kernel,
-        in_specs=[smem, vmem, vmem, hbm],
+        functools.partial(high_kernel, base),
+        in_specs=[smem, vmem, vmem, vmem],
         out_specs=[vmem] * 3,
-        out_shape=[grad_half, message, message],
-        scratch_shapes=[half_weight, acc, pltpu.SemaphoreType.DMA((1, STEPS))],
-        compiler_params=params(20),
-        cost_estimate=cost(LATE_US),
+        out_shape=[like(slots, rest), like(chunk, rest), like(chunk, rest)],
+        scratch_shapes=[pltpu.VMEM((slots, rest), F32)],
+        compiler_params=params(16),
+        cost_estimate=cost(HIGH_US),
         name="high_scores",
-    )(chunks, rows, meta, weights)
+    )(chunks, rows, meta, high_weight)
 
     def hop(x, d):
         return lax.ppermute(x, "dp", [(i, (i + d) % planes) for i in range(planes)])
@@ -370,36 +406,37 @@
     def rows_spec(k):
         return pl.BlockSpec((slots, chunk), lambda i, c: (0, c[k % planes]))
 
-    message_spec = pl.BlockSpec((chunk, half), lambda i, c: (0, 0))
+    def message_spec(some):
+        return pl.BlockSpec((chunk, some), lambda i, c: (0, 0))
+
     token_spec = pl.BlockSpec((8, 128), lambda i, c: (0, 0))
 
     def state_parts(after):
         return pl.pallas_call(
             back_kernel,
-            in_specs=[vmem, vmem, hbm, anywhere],
+            in_specs=[vmem, vmem, vmem, vmem, anywhere],
             out_specs=[hbm, vmem],
             out_shape=[pltpu.HBM((slots, width), BF16), token],
             scratch_shapes=[
-                pltpu.VMEM((slots, words), BF16),
-                pltpu.VMEM((planes, chunk, words), BF16),
                 pltpu.VMEM((planes, slots, chunk), BF16),
-                pltpu.SemaphoreType.DMA((2, planes)),
+                pltpu.SemaphoreType.DMA((planes,)),
             ],
-            compiler_params=params(24),
-            cost_estimate=cost(LATE_US),
+            compiler_params=params(16),
+            cost_estimate=cost(STATE_US),
             name="state_parts",
-        )(low, high, weights, after)
+        )(low, high, low_weight, high_weight, after)
 
     def add(k, grad, arrived, after, us):
+        some = grad.shape[1]
         return pl.pallas_call(
             add_kernel,
             grid_spec=pltpu.PrefetchScalarGridSpec(
                 num_scalar_prefetch=1,
                 grid=(1,),
-                in_specs=[message_spec, rows_spec(k), message_spec, anywhere],
-                out_specs=[message_spec, token_spec],
+                in_specs=[message_spec(some), rows_spec(k), message_spec(some), anywhere],
+                out_specs=[message_spec(some), token_spec],
             ),
-            out_shape=[message, token],
+            out_shape=[like(chunk, some), token],
             compiler_params=params(12),
             cost_estimate=cost(us),
             name="add_part",
@@ -429,7 +466,14 @@
         grid_spec=pltpu.PrefetchScalarGridSpec(
             num_scalar_prefetch=1,
             grid=(1,),
-            in_specs=[message_spec] * 2 + [rows_spec(0)] + [message_spec] * 2 + [anywhere],
+            in_specs=[
+                message_spec(base),
+                message_spec(rest),
+                rows_spec(0),
+                message_spec(base),
+                message_spec(rest),
+                anywhere,
+            ],
             out_specs=[pl.BlockSpec((chunk, words), lambda i, c: (0, 0)), token_spec],
         ),
         out_shape=[jax.ShapeDtypeStruct((chunk, words), F32), token],
@@ -437,29 +481,28 @@
         cost_estimate=cost(OWN_US),
         name="own_part",
     )(chunks, messages[1], messages[3], got, low, high, after)
-    pieces = 4
     hidden_grad, after = pl.pallas_call(
         sum_kernel,
-        grid=(pieces,),
-        in_specs=[
-            whole(tokens, slots),
-            pl.BlockSpec((slots, width // pieces), lambda i: (0, i)),
-            anywhere,
+        in_specs=[vmem, hbm, anywhere],
+        out_specs=[hbm, vmem],
+        out_shape=[pltpu.HBM((tokens, width), BF16), token],
+        scratch_shapes=[
+            pltpu.VMEM((slots, width), BF16),
+            pltpu.VMEM((tokens, width), BF16),
+            pltpu.SemaphoreType.DMA((2, STEPS)),
         ],
-        out_specs=[pl.BlockSpec((tokens, width // pieces), lambda i: (0, i)), whole(8, 128)],
-        out_shape=[jax.ShapeDtypeStruct((tokens, width), BF16), token],
         compiler_params=params(12),
         cost_estimate=cost(SUM_US),
         name="sum_parts",
     )(placed, in_hbm(back), after)
-
     weight_grad = pl.pallas_call(
         last_kernel,
         in_specs=[vmem, vmem, vmem, anywhere],
-        out_specs=vmem,
-        out_shape=jax.ShapeDtypeStruct((chunk, words), BF16),
+        out_specs=hbm,
+        out_shape=pltpu.HBM((chunk, words), BF16),
+        scratch_shapes=[pltpu.VMEM((chunk, words), BF16), pltpu.SemaphoreType.DMA((2,))],
         compiler_params=params(12),
-        cost_estimate=cost(0),
+        cost_estimate=cost(LAST_US),
         name="last_add",
     )(messages[0], messages[2], own, after)
     return (hidden_grad, weight_grad)

time: 175 us -> 175 us (level)
    pallas_call x3, Pallas kernels: 18 us -> 13.5 us  [the longest x1 6.49 us: state_parts(): pl.pallas_call(back_kernel, in_specs=[vmem, vmem, vmem, vmem, anywhere],...]
    pallas_call x1, Pallas kernels: 7.14 us -> 10.1 us  [body(): pl.pallas_call(low_kernel, in_specs=[smem, hbm, hbm, anywhere], out_specs...]
  transfers between devices with their start and end apart: 16 -> 16, of which waited for: 7 -> 8; matrix products, arithmetic and copies ran while one was open for 0% -> 0% of each run, Pallas kernels for 25% -> 22%
where the time goes in v4:
time: 175 us; the launch traced here: 174 us
  waiting for transfers between devices  78.3 us (45%)
  Pallas kernels  56 us (32%)
  starting transfers between devices  37.7 us (22%)
    all_to_all x1, waiting for transfers between devices, body(): lax.all_to_all(send.reshape(peers, capacity, sent), 'vocab', split_axis=0...  52.7 us
    ppermute x14, waiting for transfers between devices, hop(): return lax.ppermute(x, 'dp', [(i, (i + d) % planes) for i in range(planes)])  25.6 us
    pallas_call x10, Pallas kernels, add(): pl.pallas_call(add_kernel, grid_spec=pltpu.PrefetchScalarGridSpec(num_sca...  23 us
    ppermute x14, starting transfers between devices, hop(): return lax.ppermute(x, 'dp', [(i, (i + d) % planes) for i in range(planes)])  22.9 us
    pallas_call x1, Pallas kernels, body(): pl.pallas_call(low_kernel, in_specs=[smem, hbm, hbm, anywhere], out_specs...  10.1 us
    all_to_all x1, starting transfers between devices, body(): lax.all_to_all(send.reshape(peers, capacity, sent), 'vocab', split_axis=0...  7.68 us
    all_to_all x1, starting transfers between devices, body(): lax.all_to_all(part.reshape(peers, capacity, width), 'vocab', split_axis=...  7.1 us
    pallas_call x1, Pallas kernels, state_parts(): pl.pallas_call(back_kernel, in_specs=[vmem, vmem, vmem, vmem, anywhere],...  6.49 us
  transfers between devices with their start and end apart: 16, of which 8 were waited for; matrix products, arithmetic and copies ran while one was open for 0% of the time, Pallas kernels for 22%

profile of v4, /device:TPU:98, one launch (start us, length us, event | category | flops | bytes accessed | tf_op | source)
XLA Modules:
  0.0 174.1 jit_solution(17055733791912156454)
XLA Ops:
  0.6 4.8 %place_rows.1 = (bf16[512,4224]{1,0:T(8,128)(2,1)}, bf16[512,128]{1,0:T(8,128)(2,1)S(1)}) custom-call(bf16[128,4096]{1,0:T(8,128)(2,1)} %hidden_ref.1, s32[3,128]{1,0:T(4,128)} %bitcast.15, s32[3,2,128]{2,1,0:T(2,128)} %bitcast.13, s32[3,2,128]{2,1,0:T(2,128)} %bitcast.14, s32[1,128]{1,0:T(1,128)} %bitcast.16, s32[1,128]{1,0:T(1,128)} %bitcast.17, ...), custom_call_target="tpu_custom_call" | custom-call | tf_op jit(solution)/shard_map/place_rows/pallas_call | solution.py:333
  5.5 7.7 %all-to-all-start = ((bf16[32,16,4224]{2,1,0:T(8,128)(2,1)}), bf16[32,16,4224]{2,1,0:T(8,128)(2,1)}, u32[]{:S(2)}, u32[]{:S(2)}) async-start(bf16[32,16,4224]{2,1,0:T(8,128)(2,1)} %bitcast.11), calls=%async_computation | async-start | bytes 8650752 | tf_op jit(solution)/shard_map/all_to_all | solution.py:351
  13.3 52.7 %all-to-all-done = bf16[32,16,4224]{2,1,0:T(8,128)(2,1)} async-done(((bf16[32,16,4224]{2,1,0:T(8,128)(2,1)}), bf16[32,16,4224]{2,1,0:T(8,128)(2,1)}, u32[]{:S(2)}, u32[]{:S(2)}) %all-to-all-start) | async-done | bytes 4325408 | tf_op jit(solution)/shard_map/all_to_all | solution.py:351
  66.0 10.1 %low_scores.1 = (bf16[512,4096]{1,0:T(8,128)(2,1)S(1)}, bf16[512,128]{1,0:T(8,128)(2,1)S(1)}, bf16[4,1024,640]{2,1,0:T(8,128)(2,1)S(1)}, bf16[4,1024,384]{2,1,0:...) custom-call(s32[8]{0:T(128)S(1)} %compare_select_fusion.chunks_ref, ...), custom_call_target="tpu_custom_call" | custom-call | tf_op jit(solution)/shard_map/low_scores/pallas_call | solution.py:374
  76.1 3.2 %collective-permute-start.1 = (bf16[512,640]{1,0:T(8,128)(2,1)}, bf16[512,640]{1,0:T(8,128)(2,1)S(1)}, u32[]{:S(2)}, u32[]{:S(2)}) collective-permute-start(bf16[512,640]{1,0:T(8,128)(2,1)} %get-tuple-element.51), channel_id=1, source_target_pairs={{0,32},{32,64},{64,96},{96,128},{128,160},{160,192},{192,224},{224... | collective-permute-start | bytes 1966088 | tf_op jit(solution)/shard_map/ppermute | solution.py:404
  79.3 3.7 %high_scores.1 = (bf16[512,384]{1,0:T(8,128)(2,1)S(1)}, bf16[512,384]{1,0:T(8,128)(2,1)S(1)}, bf16[512,384]{1,0:T(8,128)(2,1)S(1)}) custom-call(s32[8]{0:T(128)S(1)} %compare_select_fusion.chunks_ref, bf16[512,4096]{1,0:T(8,128)(2,1)S(1)} %get-tuple-element.43.rows_ref, bf16[512,128]{1,0:T(8,128)(2,1)S(1)} %get-tuple-element.44.meta_ref, ...), custom_call_target="tpu_custom_call" | custom-call | tf_op jit(solution)/shard_map/high_scores/pallas_call | solution.py:392
  83.0 3.5 %collective-permute-start.4 = (bf16[512,384]{1,0:T(8,128)(2,1)S(1)}, bf16[512,384]{1,0:T(8,128)(2,1)}, u32[]{:S(2)}, u32[]{:S(2)}) collective-permute-start(bf16[512,384]{1,0:T(8,128)(2,1)S(1)} %get-tuple-element.48.after_ref), channel_id=1, source_target_pairs={{0,32},{32,64},{64,96},{96,128},{128,160},{160,192},{192,224},{224... | collective-permute-start | bytes 1179656 | tf_op jit(solution)/shard_map/ppermute | solution.py:404
  86.5 6.5 %state_parts.1 = (bf16[512,4096]{1,0:T(8,128)(2,1)}, f32[8,128]{1,0:T(8,128)S(1)}) custom-call(bf16[512,640]{1,0:T(8,128)(2,1)S(1)} %get-tuple-element.42.low_ref.grad_ref, bf16[512,384]{1,0:T(8,128)(2,1)S(1)} %get-tuple-element.46.high_ref.grad_ref, bf16[4,1024,640]{2,1,0:T(8,128)(2,1)S(1)} %get-tuple-element.47.low_weight, ...), custom_call_target="tpu_custom_call" | custom-call | tf_op jit(solution)/shard_map/state_parts/pallas_call | solution.py:415
  93.0 7.1 %all-to-all-start.1 = ((bf16[32,16,4096]{2,1,0:T(8,128)(2,1)}), bf16[32,16,4096]{2,1,0:T(8,128)(2,1)}, u32[]{:S(2)}, u32[]{:S(2)}) async-start(bf16[32,16,4096]{2,1,0:T(8,128)(2,1)} %bitcast.12), calls=%async_computation.1 | async-start | bytes 8388608 | tf_op jit(solution)/shard_map/all_to_all | solution.py:460
  100.2 2.2 %add_part.10 = (bf16[512,640]{1,0:T(8,128)(2,1)S(1)}, f32[8,128]{1,0:T(8,128)S(1)}) custom-call(s32[8]{0:T(128)S(1)} %compare_select_fusion.chunks_ref, bf16[512,640]{1,0:T(8,128)(2,1)S(1)} %collective-permute-done.1.got_ref, bf16[512,4224]{1,0:T(8,128)(2,1)} %bitcast.8.got_ref.rows_ref, bf16[512,640]{1,0:T(8,128)(2,1)S(1)} %get-tuple-element.42.low_ref.grad_ref, ...), custom_call_target="tpu_custom_call" | custom-call | flops 3449999872 | tf_op jit(solution)/shard_map/add_part/pallas_call | solution.py:431
  102.4 3.3 %collective-permute-start.3 = (bf16[512,640]{1,0:T(8,128)(2,1)S(1)}, bf16[512,640]{1,0:T(8,128)(2,1)S(1)}, u32[]{:S(2)}, u32[]{:S(2)}) collective-permute-start(bf16[512,640]{1,0:T(8,128)(2,1)S(1)} %get-tuple-element.55), channel_id=1, source_target_pairs={{0,32},{32,64},{64,96},{96,128},{128,160},{160,192},{192,224},{224... | collective-permute-start | bytes 1966088 | tf_op jit(solution)/shard_map/ppermute | solution.py:404
  105.7 2.2 %add_part.11 = (bf16[512,640]{1,0:T(8,128)(2,1)S(1)}, f32[8,128]{1,0:T(8,128)S(1)}) custom-call(s32[8]{0:T(128)S(1)} %compare_select_fusion.chunks_ref, bf16[512,640]{1,0:T(8,128)(2,1)S(1)} %collective-permute-done.got_ref, bf16[512,4224]{1,0:T(8,128)(2,1)} %bitcast.8.got_ref.rows_ref, bf16[512,640]{1,0:T(8,128)(2,1)S(1)} %get-tuple-element.42.low_ref.grad_ref, ...), custom_call_target="tpu_custom_call" | custom-call | flops 3449999872 | tf_op jit(solution)/shard_map/add_part/pallas_call | solution.py:431
  108.0 5.6 %collective-permute-done.5.got_ref = bf16[512,384]{1,0:T(8,128)(2,1)S(1)} collective-permute-done((bf16[512,384]{1,0:T(8,128)(2,1)}, bf16[512,384]{1,0:T(8,128)(2,1)S(1)}, u32[]{:S(2)}, u32[]{:S(2)}) %collective-permute-start.5) | collective-permute-done | bytes 393248 | tf_op jit(solution)/shard_map/ppermute | solution.py:404
  113.6 2.1 %add_part.12 = (bf16[512,384]{1,0:T(8,128)(2,1)S(1)}, f32[8,128]{1,0:T(8,128)S(1)}) custom-call(s32[8]{0:T(128)S(1)} %compare_select_fusion.chunks_ref, bf16[512,384]{1,0:T(8,128)(2,1)S(1)} %collective-permute-done.5.got_ref, bf16[512,4224]{1,0:T(8,128)(2,1)} %bitcast.8.got_ref.rows_ref, bf16[512,384]{1,0:T(8,128)(2,1)S(1)} %get-tuple-element.46.high_ref.grad_ref, ...), custom_call_target="tpu_custom_call" | custom-call | flops 3449999872 | tf_op jit(solution)/shard_map/add_part/pallas_call | solution.py:431
  115.7 2.2 %add_part.13 = (bf16[512,384]{1,0:T(8,128)(2,1)S(1)}, f32[8,128]{1,0:T(8,128)S(1)}) custom-call(s32[8]{0:T(128)S(1)} %compare_select_fusion.chunks_ref, bf16[512,384]{1,0:T(8,128)(2,1)} %collective-permute-done.4.got_ref, bf16[512,4224]{1,0:T(8,128)(2,1)} %bitcast.8.got_ref.rows_ref, bf16[512,384]{1,0:T(8,128)(2,1)S(1)} %get-tuple-element.46.high_ref.grad_ref, ...), custom_call_target="tpu_custom_call" | custom-call | flops 3449999872 | tf_op jit(solution)/shard_map/add_part/pallas_call | solution.py:431
  117.9 2.0 %collective-permute-start.8 = (bf16[512,384]{1,0:T(8,128)(2,1)S(1)}, bf16[512,384]{1,0:T(8,128)(2,1)S(1)}, u32[]{:S(2)}, u32[]{:S(2)}) collective-permute-start(bf16[512,384]{1,0:T(8,128)(2,1)S(1)} %get-tuple-element.63), channel_id=1, source_target_pairs={{0,224},{32,0},{64,32},{96,64},{128,96},{160,128},{192,160},{224,1... | collective-permute-start | bytes 1179656 | tf_op jit(solution)/shard_map/ppermute | solution.py:404
  120.9 2.2 %add_part.14 = (bf16[512,640]{1,0:T(8,128)(2,1)S(1)}, f32[8,128]{1,0:T(8,128)S(1)}) custom-call(s32[8]{0:T(128)S(1)} %compare_select_fusion.chunks_ref, bf16[512,640]{1,0:T(8,128)(2,1)S(1)} %collective-permute-done.3.got_ref, bf16[512,4224]{1,0:T(8,128)(2,1)} %bitcast.8.got_ref.rows_ref, bf16[512,640]{1,0:T(8,128)(2,1)S(1)} %get-tuple-element.42.low_ref.grad_ref, ...), custom_call_target="tpu_custom_call" | custom-call | flops 3449999872 | tf_op jit(solution)/shard_map/add_part/pallas_call | solution.py:431
  123.1 3.8 %collective-permute-start.11 = (bf16[512,640]{1,0:T(8,128)(2,1)S(1)}, bf16[512,640]{1,0:T(8,128)(2,1)S(1)}, u32[]{:S(2)}, u32[]{:S(2)}) collective-permute-start(bf16[512,640]{1,0:T(8,128)(2,1)S(1)} %get-tuple-element.68), channel_id=1, source_target_pairs={{0,32},{32,64},{64,96},{96,128},{128,160},{160,192},{192,224},{224... | collective-permute-start | bytes 1966088 | tf_op jit(solution)/shard_map/ppermute | solution.py:404
  127.6 2.2 %add_part.15 = (bf16[512,640]{1,0:T(8,128)(2,1)S(1)}, f32[8,128]{1,0:T(8,128)S(1)}) custom-call(s32[8]{0:T(128)S(1)} %compare_select_fusion.chunks_ref, bf16[512,640]{1,0:T(8,128)(2,1)S(1)} %collective-permute-done.2.got_ref, bf16[512,4224]{1,0:T(8,128)(2,1)} %bitcast.8.got_ref.rows_ref, bf16[512,640]{1,0:T(8,128)(2,1)S(1)} %get-tuple-element.42.low_ref.grad_ref, ...), custom_call_target="tpu_custom_call" | custom-call | flops 3449999872 | tf_op jit(solution)/shard_map/add_part/pallas_call | solution.py:431
  129.8 5.4 %collective-permute-done.8.got_ref = bf16[512,384]{1,0:T(8,128)(2,1)S(1)} collective-permute-done((bf16[512,384]{1,0:T(8,128)(2,1)S(1)}, bf16[512,384]{1,0:T(8,128)(2,1)S(1)}, u32[]{:S(2)}, u32[]{:S(2)}) %collective-permute-start.8) | collective-permute-done | bytes 393248 | tf_op jit(solution)/shard_map/ppermute | solution.py:404
  135.3 2.1 %add_part.16 = (bf16[512,384]{1,0:T(8,128)(2,1)S(1)}, f32[8,128]{1,0:T(8,128)S(1)}) custom-call(s32[8]{0:T(128)S(1)} %compare_select_fusion.chunks_ref, bf16[512,384]{1,0:T(8,128)(2,1)S(1)} %collective-permute-done.8.got_ref, bf16[512,4224]{1,0:T(8,128)(2,1)} %bitcast.8.got_ref.rows_ref, bf16[512,384]{1,0:T(8,128)(2,1)S(1)} %get-tuple-element.46.high_ref.grad_ref, ...), custom_call_target="tpu_custom_call" | custom-call | flops 3449999872 | tf_op jit(solution)/shard_map/add_part/pallas_call | solution.py:431
  137.8 2.1 %add_part.17 = (bf16[512,384]{1,0:T(8,128)(2,1)S(1)}, f32[8,128]{1,0:T(8,128)S(1)}) custom-call(s32[8]{0:T(128)S(1)} %compare_select_fusion.chunks_ref, bf16[512,384]{1,0:T(8,128)(2,1)S(1)} %collective-permute-done.7.got_ref, bf16[512,4224]{1,0:T(8,128)(2,1)} %bitcast.8.got_ref.rows_ref, bf16[512,384]{1,0:T(8,128)(2,1)S(1)} %get-tuple-element.46.high_ref.grad_ref, ...), custom_call_target="tpu_custom_call" | custom-call | flops 3449999872 | tf_op jit(solution)/shard_map/add_part/pallas_call | solution.py:431
  139.8 3.3 %collective-permute-start.9 = (bf16[512,384]{1,0:T(8,128)(2,1)S(1)}, bf16[512,384]{1,0:T(8,128)(2,1)S(1)}, u32[]{:S(2)}, u32[]{:S(2)}) collective-permute-start(bf16[512,384]{1,0:T(8,128)(2,1)S(1)} %get-tuple-element.66), channel_id=1, source_target_pairs={{0,32},{32,64},{64,96},{96,128},{128,160},{160,192},{192,224},{224... | collective-permute-start | bytes 1179656 | tf_op jit(solution)/shard_map/ppermute | solution.py:404
  143.1 3.0 %add_part.18 = (bf16[512,640]{1,0:T(8,128)(2,1)}, f32[8,128]{1,0:T(8,128)S(1)}) custom-call(s32[8]{0:T(128)S(1)} %compare_select_fusion.chunks_ref, bf16[512,640]{1,0:T(8,128)(2,1)S(1)} %collective-permute-done.11.got_ref, bf16[512,4224]{1,0:T(8,128)(2,1)} %bitcast.8.got_ref.rows_ref, bf16[512,640]{1,0:T(8,128)(2,1)S(1)} %get-tuple-element.42.low_ref.grad_ref, ...), custom_call_target="tpu_custom_call" | custom-call | flops 3449999872 | tf_op jit(solution)/shard_map/add_part/pallas_call | solution.py:431
  146.1 4.8 %collective-permute-done.10.got_ref = bf16[512,384]{1,0:T(8,128)(2,1)S(1)} collective-permute-done((bf16[512,384]{1,0:T(8,128)(2,1)S(1)}, bf16[512,384]{1,0:T(8,128)(2,1)S(1)}, u32[]{:S(2)}, u32[]{:S(2)}) %collective-permute-start.10) | collective-permute-done | bytes 393248 | tf_op jit(solution)/shard_map/ppermute | solution.py:404
  150.9 2.8 %add_part.19 = (bf16[512,384]{1,0:T(8,128)(2,1)}, f32[8,128]{1,0:T(8,128)S(1)}) custom-call(s32[8]{0:T(128)S(1)} %compare_select_fusion.chunks_ref, bf16[512,384]{1,0:T(8,128)(2,1)S(1)} %collective-permute-done.10.got_ref, bf16[512,4224]{1,0:T(8,128)(2,1)} %bitcast.8.got_ref.rows_ref, bf16[512,384]{1,0:T(8,128)(2,1)S(1)} %get-tuple-element.46.high_ref.grad_ref, ...), custom_call_target="tpu_custom_call" | custom-call | flops 3449999872 | tf_op jit(solution)/shard_map/add_part/pallas_call | solution.py:431
  153.7 3.2 %collective-permute-start.12 = (bf16[512,640]{1,0:T(8,128)(2,1)}, bf16[512,640]{1,0:T(8,128)(2,1)S(1)}, u32[]{:S(2)}, u32[]{:S(2)}) collective-permute-start(bf16[512,640]{1,0:T(8,128)(2,1)} %get-tuple-element.74), channel_id=1, source_target_pairs={{0,32},{32,64},{64,96},{96,128},{128,160},{160,192},{192,224},{224... | collective-permute-start | bytes 1966088 | tf_op jit(solution)/shard_map/ppermute | solution.py:404
  156.9 8.0 %collective-permute-done.6.low_near_ref = bf16[512,640]{1,0:T(8,128)(2,1)S(1)} collective-permute-done((bf16[512,640]{1,0:T(8,128)(2,1)S(1)}, bf16[512,640]{1,0:T(8,128)(2,1)S(1)}, u32[]{:S(2)}, u32[]{:S(2)}) %collective-permute-start.6) | collective-permute-done | bytes 655392 | tf_op jit(solution)/shard_map/ppermute | solution.py:404
  164.9 1.0 copy-done.3
  165.9 2.5 %own_part.1 = (f32[512,1024]{1,0:T(8,128)S(1)}, f32[8,128]{1,0:T(8,128)S(1)}) custom-call(s32[8]{0:T(128)S(1)} %compare_select_fusion.chunks_ref, bf16[512,640]{1,0:T(8,128)(2,1)S(1)} %collective-permute-done.6.low_near_ref, bf16[512,384]{1,0:T(8,128)(2,1)S(1)} %collective-permute-done.9.high_near_ref, bf16[512,4224]{1,0:T(8,128)(2,1)} %bitcast.8.got_ref.rows_ref, ...), custom_call_target="tpu_custom_call" | custom-call | flops 115000000512 | tf_op jit(solution)/shard_map/own_part/pallas_call | solution.py:464
  168.5 3.3 %sum_parts.1 = (bf16[128,4096]{1,0:T(8,128)(2,1)}, f32[8,128]{1,0:T(8,128)S(1)}) custom-call(bf16[128,512]{1,0:T(8,128)(2,1)S(1)} %copy-done.1, bf16[512,4096]{1,0:T(8,128)(2,1)} %bitcast.10.back_ref, f32[8,128]{1,0:T(8,128)S(1)} %get-tuple-element.72.after_ref), custom_call_target="tpu_custom_call" | custom-call | tf_op jit(solution)/shard_map/sum_parts/pallas_call | solution.py:484
  171.9 2.1 %last_add.1 = bf16[512,1024]{1,0:T(8,128)(2,1)} custom-call(bf16[512,640]{1,0:T(8,128)(2,1)S(1)} %collective-permute-done.12.low_far_ref, bf16[512,384]{1,0:T(8,128)(2,1)} %collective-permute-done.13.high_far_ref, f32[512,1024]{1,0:T(8,128)S(1)} %get-tuple-element.76.own_ref, f32[8,128]{1,0:T(8,128)S(1)} %get-tuple-element.77.after_ref), custom_call_target="tpu_custom_call" | custom-call | tf_op jit(solution)/shard_map/last_add/pallas_call | solution.py:498
  (29 shorter events, 2.6 us)
Async XLA Ops:
  5.5 60.5 %all-to-all-start = ((bf16[32,16,4224]{2,1,0:T(8,128)(2,1)}), bf16[32,16,4224]{2,1,0:T(8,128)(2,1)}, u32[]{:S(2)}, u32[]{:S(2)}) async-start(bf16[32,16,4224]{2,1,0:T(8,128)(2,1)} %bitcast.11), calls=%async_computation | async-start | bytes 8650752 | tf_op jit(solution)/shard_map/all_to_all | solution.py:351
  13.3 62.8 %copy-start = (bf16[128,512]{1,0:T(8,128)(2,1)}, bf16[128,512]{1,0:T(8,128)(2,1)S(1)}, u32[]{:S(2)}) copy-start(bf16[128,512]{1,0:T(8,128)(2,1)S(1)} %turn_places.1.after_ref.placed_ref) | copy-start | bytes 393220
  76.1 24.1 %collective-permute-start.1 = (bf16[512,640]{1,0:T(8,128)(2,1)}, bf16[512,640]{1,0:T(8,128)(2,1)S(1)}, u32[]{:S(2)}, u32[]{:S(2)}) collective-permute-start(bf16[512,640]{1,0:T(8,128)(2,1)} %get-tuple-element.51), channel_id=1, source_target_pairs={{0,32},{32,64},{64,96},{96,128},{128,160},{160,192},{192,224},{224... | collective-permute-start | bytes 1966088 | tf_op jit(solution)/shard_map/ppermute | solution.py:404
  79.3 26.4 %collective-permute-start = (bf16[512,640]{1,0:T(8,128)(2,1)S(1)}, bf16[512,640]{1,0:T(8,128)(2,1)S(1)}, u32[]{:S(2)}, u32[]{:S(2)}) collective-permute-start(bf16[512,640]{1,0:T(8,128)(2,1)S(1)} %get-tuple-element.50), channel_id=1, source_target_pairs={{0,224},{32,0},{64,32},{96,64},{128,96},{160,128},{192,160},{224,1... | collective-permute-start | bytes 1966088 | tf_op jit(solution)/shard_map/ppermute | solution.py:404
  83.0 10.0 %copy-start.4 = (bf16[512,384]{1,0:T(8,128)(2,1)}, bf16[512,384]{1,0:T(8,128)(2,1)S(1)}, u32[]{:S(2)}) copy-start(bf16[512,384]{1,0:T(8,128)(2,1)S(1)} %get-tuple-element.56) | copy-start | bytes 1179652
  83.0 67.9 %copy-start.2 = (bf16[512,384]{1,0:T(8,128)(2,1)}, bf16[512,384]{1,0:T(8,128)(2,1)S(1)}, u32[]{:S(2)}) copy-start(bf16[512,384]{1,0:T(8,128)(2,1)S(1)} %get-tuple-element.46.high_ref.grad_ref) | copy-start | bytes 1179652
  83.0 32.6 %collective-permute-start.4 = (bf16[512,384]{1,0:T(8,128)(2,1)S(1)}, bf16[512,384]{1,0:T(8,128)(2,1)}, u32[]{:S(2)}, u32[]{:S(2)}) collective-permute-start(bf16[512,384]{1,0:T(8,128)(2,1)S(1)} %get-tuple-element.48.after_ref), channel_id=1, source_target_pairs={{0,32},{32,64},{64,96},{96,128},{128,160},{160,192},{192,224},{224... | collective-permute-start | bytes 1179656 | tf_op jit(solution)/shard_map/ppermute | solution.py:404
  93.0 75.4 %all-to-all-start.1 = ((bf16[32,16,4096]{2,1,0:T(8,128)(2,1)}), bf16[32,16,4096]{2,1,0:T(8,128)(2,1)}, u32[]{:S(2)}, u32[]{:S(2)}) async-start(bf16[32,16,4096]{2,1,0:T(8,128)(2,1)} %bitcast.12), calls=%async_computation.1 | async-start | bytes 8388608 | tf_op jit(solution)/shard_map/all_to_all | solution.py:460
  100.1 13.5 %collective-permute-start.5 = (bf16[512,384]{1,0:T(8,128)(2,1)}, bf16[512,384]{1,0:T(8,128)(2,1)S(1)}, u32[]{:S(2)}, u32[]{:S(2)}) collective-permute-start(bf16[512,384]{1,0:T(8,128)(2,1)} %copy-done.4), channel_id=1, source_target_pairs={{0,224},{32,0},{64,32},{96,64},{128,96},{160,128},{192,160},{224,1... | collective-permute-start | bytes 1179656 | tf_op jit(solution)/shard_map/ppermute | solution.py:404
  102.4 18.4 %collective-permute-start.3 = (bf16[512,640]{1,0:T(8,128)(2,1)S(1)}, bf16[512,640]{1,0:T(8,128)(2,1)S(1)}, u32[]{:S(2)}, u32[]{:S(2)}) collective-permute-start(bf16[512,640]{1,0:T(8,128)(2,1)S(1)} %get-tuple-element.55), channel_id=1, source_target_pairs={{0,32},{32,64},{64,96},{96,128},{128,160},{160,192},{192,224},{224... | collective-permute-start | bytes 1966088 | tf_op jit(solution)/shard_map/ppermute | solution.py:404
  107.9 19.7 %collective-permute-start.2 = (bf16[512,640]{1,0:T(8,128)(2,1)S(1)}, bf16[512,640]{1,0:T(8,128)(2,1)S(1)}, u32[]{:S(2)}, u32[]{:S(2)}) collective-permute-start(bf16[512,640]{1,0:T(8,128)(2,1)S(1)} %get-tuple-element.54), channel_id=1, source_target_pairs={{0,224},{32,0},{64,32},{96,64},{128,96},{160,128},{192,160},{224,1... | collective-permute-start | bytes 1966088 | tf_op jit(solution)/shard_map/ppermute | solution.py:404
  117.8 19.9 %collective-permute-start.7 = (bf16[512,384]{1,0:T(8,128)(2,1)S(1)}, bf16[512,384]{1,0:T(8,128)(2,1)S(1)}, u32[]{:S(2)}, u32[]{:S(2)}) collective-permute-start(bf16[512,384]{1,0:T(8,128)(2,1)S(1)} %get-tuple-element.62), channel_id=1, source_target_pairs={{0,32},{32,64},{64,96},{96,128},{128,160},{160,192},{192,224},{224... | collective-permute-start | bytes 1179656 | tf_op jit(solution)/shard_map/ppermute | solution.py:404
  117.9 17.3 %collective-permute-start.8 = (bf16[512,384]{1,0:T(8,128)(2,1)S(1)}, bf16[512,384]{1,0:T(8,128)(2,1)S(1)}, u32[]{:S(2)}, u32[]{:S(2)}) collective-permute-start(bf16[512,384]{1,0:T(8,128)(2,1)S(1)} %get-tuple-element.63), channel_id=1, source_target_pairs={{0,224},{32,0},{64,32},{96,64},{128,96},{160,128},{192,160},{224,1... | collective-permute-start | bytes 1179656 | tf_op jit(solution)/shard_map/ppermute | solution.py:404
  123.1 20.1 %collective-permute-start.11 = (bf16[512,640]{1,0:T(8,128)(2,1)S(1)}, bf16[512,640]{1,0:T(8,128)(2,1)S(1)}, u32[]{:S(2)}, u32[]{:S(2)}) collective-permute-start(bf16[512,640]{1,0:T(8,128)(2,1)S(1)} %get-tuple-element.68), channel_id=1, source_target_pairs={{0,32},{32,64},{64,96},{96,128},{128,160},{160,192},{192,224},{224... | collective-permute-start | bytes 1966088 | tf_op jit(solution)/shard_map/ppermute | solution.py:404
  137.3 13.6 %collective-permute-start.10 = (bf16[512,384]{1,0:T(8,128)(2,1)S(1)}, bf16[512,384]{1,0:T(8,128)(2,1)S(1)}, u32[]{:S(2)}, u32[]{:S(2)}) collective-permute-start(bf16[512,384]{1,0:T(8,128)(2,1)S(1)} %get-tuple-element.67), channel_id=1, source_target_pairs={{0,224},{32,0},{64,32},{96,64},{128,96},{160,128},{192,160},{224,1... | collective-permute-start | bytes 1179656 | tf_op jit(solution)/shard_map/ppermute | solution.py:404
  137.7 27.3 %collective-permute-start.6 = (bf16[512,640]{1,0:T(8,128)(2,1)S(1)}, bf16[512,640]{1,0:T(8,128)(2,1)S(1)}, u32[]{:S(2)}, u32[]{:S(2)}) collective-permute-start(bf16[512,640]{1,0:T(8,128)(2,1)S(1)} %get-tuple-element.61), channel_id=1, source_target_pairs={{0,224},{32,0},{64,32},{96,64},{128,96},{160,128},{192,160},{224,1... | collective-permute-start | bytes 1966088 | tf_op jit(solution)/shard_map/ppermute | solution.py:404
  139.8 17.1 %collective-permute-start.9 = (bf16[512,384]{1,0:T(8,128)(2,1)S(1)}, bf16[512,384]{1,0:T(8,128)(2,1)S(1)}, u32[]{:S(2)}, u32[]{:S(2)}) collective-permute-start(bf16[512,384]{1,0:T(8,128)(2,1)S(1)} %get-tuple-element.66), channel_id=1, source_target_pairs={{0,32},{32,64},{64,96},{96,128},{128,160},{160,192},{192,224},{224... | collective-permute-start | bytes 1179656 | tf_op jit(solution)/shard_map/ppermute | solution.py:404
  153.7 18.2 %collective-permute-start.13 = (bf16[512,384]{1,0:T(8,128)(2,1)}, bf16[512,384]{1,0:T(8,128)(2,1)}, u32[]{:S(2)}, u32[]{:S(2)}) collective-permute-start(bf16[512,384]{1,0:T(8,128)(2,1)} %get-tuple-element.75), channel_id=1, source_target_pairs={{0,224},{32,0},{64,32},{96,64},{128,96},{160,128},{192,160},{224,1... | collective-permute-start | bytes 1179656 | tf_op jit(solution)/shard_map/ppermute | solution.py:404
  153.7 18.2 %collective-permute-start.12 = (bf16[512,640]{1,0:T(8,128)(2,1)}, bf16[512,640]{1,0:T(8,128)(2,1)S(1)}, u32[]{:S(2)}, u32[]{:S(2)}) collective-permute-start(bf16[512,640]{1,0:T(8,128)(2,1)} %get-tuple-element.74), channel_id=1, source_target_pairs={{0,32},{32,64},{64,96},{96,128},{128,160},{160,192},{192,224},{224... | collective-permute-start | bytes 1966088 | tf_op jit(solution)/shard_map/ppermute | solution.py:404
  164.9 1.0 copy-start.3
  165.9 2.5 %copy-start.1 = (bf16[128,512]{1,0:T(8,128)(2,1)S(1)}, bf16[128,512]{1,0:T(8,128)(2,1)}, u32[]{:S(2)}) copy-start(bf16[128,512]{1,0:T(8,128)(2,1)} %copy-done) | copy-start | bytes 393220

commit v5 on v4

--- a/solution.py
+++ b/solution.py
@@ -11,7 +11,8 @@
 BLK_DEV = 8
 META = 128
 GAP = 0
-STEPS = 4
+STEPS = 8
+AHEAD = 2
 LOW_BLOCKS = 5
 MIB = 1 << 20
 F32 = jnp.float32
@@ -186,19 +187,25 @@
         cut = pl.ds(k * depth, depth)
         loads.append(pltpu.make_async_copy(got_ref.at[:, cut], rows_ref.at[:, cut], sems.at[2, k]))
     last = pltpu.make_async_copy(got_ref.at[:, pl.ds(steps * depth, META)], meta_ref, sems.at[3, 0])
-    for k in range(steps):
-        weights[k].start()
-        loads[k].start()
-    last.start()
-    for other in others:
-        other.start()
+    queue = [(weights[k], loads[k]) for k in range(steps)]
+    queue[0] += (last,)
+    queue += [(others[k], others[k + 1]) for k in range(0, steps, 2)]
+
+    def start(k):
+        for load in queue[k] if k < len(queue) else ():
+            load.start()
+
+    for k in range(AHEAD):
+        start(k)
 
     def ready(k):
         if k == steps:
-            last.wait()
+            for late in range(steps + AHEAD, len(queue)):
+                start(late)
         else:
-            weights[k].wait()
-            loads[k].wait()
+            for load in queue[k]:
+                load.wait()
+            start(k + AHEAD)
 
     score_half(0, chunks_ref, rows_ref, meta_ref, low_weight, grad_ref, far_ref, near_ref, acc, ready)
     for other in others:

time: 175 us -> 176 us (level)
  transfers between devices with their start and end apart: 16 -> 16, of which waited for: 8 -> 7; matrix products, arithmetic and copies ran while one was open for 0% -> 0% of each run, Pallas kernels for 22% -> 23%
where the time goes in v5:
time: 176 us; the launch traced here: 175 us
  waiting for transfers between devices  78.2 us (44%)
  Pallas kernels  56.6 us (32%)
  starting transfers between devices  37.7 us (21%)
    all_to_all x1, waiting for transfers between devices, body(): lax.all_to_all(send.reshape(peers, capacity, sent), 'vocab', split_axis=0...  52.7 us
    ppermute x14, waiting for transfers between devices, hop(): return lax.ppermute(x, 'dp', [(i, (i + d) % planes) for i in range(planes)])  25.5 us
    pallas_call x10, Pallas kernels, add(): pl.pallas_call(add_kernel, grid_spec=pltpu.PrefetchScalarGridSpec(num_sca...  23 us
    ppermute x14, starting transfers between devices, hop(): return lax.ppermute(x, 'dp', [(i, (i + d) % planes) for i in range(planes)])  22.9 us
    pallas_call x1, Pallas kernels, body(): pl.pallas_call(low_kernel, in_specs=[smem, hbm, hbm, anywhere], out_specs...  10.2 us
    all_to_all x1, starting transfers between devices, body(): lax.all_to_all(send.reshape(peers, capacity, sent), 'vocab', split_axis=0...  7.68 us
    all_to_all x1, starting transfers between devices, body(): lax.all_to_all(part.reshape(peers, capacity, width), 'vocab', split_axis=...  7.1 us
    pallas_call x1, Pallas kernels, state_parts(): pl.pallas_call(back_kernel, in_specs=[vmem, vmem, vmem, vmem, anywhere],...  6.49 us
  transfers between devices with their start and end apart: 16, of which 7 were waited for; matrix products, arithmetic and copies ran while one was open for 0% of the time, Pallas kernels for 23%

profile of v5, /device:TPU:98, one launch (start us, length us, event | category | flops | bytes accessed | tf_op | source)
XLA Modules:
  0.0 174.6 jit_solution(16682378742639696693)
XLA Ops:
  0.6 4.8 %place_rows.1 = (bf16[512,4224]{1,0:T(8,128)(2,1)}, bf16[512,128]{1,0:T(8,128)(2,1)S(1)}) custom-call(bf16[128,4096]{1,0:T(8,128)(2,1)} %hidden_ref.1, s32[3,128]{1,0:T(4,128)} %bitcast.15, s32[3,2,128]{2,1,0:T(2,128)} %bitcast.13, s32[3,2,128]{2,1,0:T(2,128)} %bitcast.14, s32[1,128]{1,0:T(1,128)} %bitcast.16, s32[1,128]{1,0:T(1,128)} %bitcast.17, ...), custom_call_target="tpu_custom_call" | custom-call | tf_op jit(solution)/shard_map/place_rows/pallas_call | solution.py:340
  5.5 7.7 %all-to-all-start = ((bf16[32,16,4224]{2,1,0:T(8,128)(2,1)}), bf16[32,16,4224]{2,1,0:T(8,128)(2,1)}, u32[]{:S(2)}, u32[]{:S(2)}) async-start(bf16[32,16,4224]{2,1,0:T(8,128)(2,1)} %bitcast.11), calls=%async_computation | async-start | bytes 8650752 | tf_op jit(solution)/shard_map/all_to_all | solution.py:358
  13.3 52.7 %all-to-all-done = bf16[32,16,4224]{2,1,0:T(8,128)(2,1)} async-done(((bf16[32,16,4224]{2,1,0:T(8,128)(2,1)}), bf16[32,16,4224]{2,1,0:T(8,128)(2,1)}, u32[]{:S(2)}, u32[]{:S(2)}) %all-to-all-start) | async-done | bytes 4325408 | tf_op jit(solution)/shard_map/all_to_all | solution.py:358
  66.0 10.2 %low_scores.1 = (bf16[512,4096]{1,0:T(8,128)(2,1)S(1)}, bf16[512,128]{1,0:T(8,128)(2,1)S(1)}, bf16[8,512,640]{2,1,0:T(8,128)(2,1)S(1)}, bf16[8,512,384]{2,1,0:T(...) custom-call(s32[8]{0:T(128)S(1)} %compare_select_fusion.chunks_ref, ...), custom_call_target="tpu_custom_call" | custom-call | tf_op jit(solution)/shard_map/low_scores/pallas_call | solution.py:381
  76.2 3.2 %collective-permute-start.1 = (bf16[512,640]{1,0:T(8,128)(2,1)}, bf16[512,640]{1,0:T(8,128)(2,1)S(1)}, u32[]{:S(2)}, u32[]{:S(2)}) collective-permute-start(bf16[512,640]{1,0:T(8,128)(2,1)} %get-tuple-element.51), channel_id=1, source_target_pairs={{0,32},{32,64},{64,96},{96,128},{128,160},{160,192},{192,224},{224... | collective-permute-start | bytes 1966088 | tf_op jit(solution)/shard_map/ppermute | solution.py:411
  79.4 3.7 %high_scores.1 = (bf16[512,384]{1,0:T(8,128)(2,1)S(1)}, bf16[512,384]{1,0:T(8,128)(2,1)S(1)}, bf16[512,384]{1,0:T(8,128)(2,1)S(1)}) custom-call(s32[8]{0:T(128)S(1)} %compare_select_fusion.chunks_ref, bf16[512,4096]{1,0:T(8,128)(2,1)S(1)} %get-tuple-element.43.rows_ref, bf16[512,128]{1,0:T(8,128)(2,1)S(1)} %get-tuple-element.44.meta_ref, ...), custom_call_target="tpu_custom_call" | custom-call | tf_op jit(solution)/shard_map/high_scores/pallas_call | solution.py:399
  83.1 3.5 %collective-permute-start.4 = (bf16[512,384]{1,0:T(8,128)(2,1)S(1)}, bf16[512,384]{1,0:T(8,128)(2,1)}, u32[]{:S(2)}, u32[]{:S(2)}) collective-permute-start(bf16[512,384]{1,0:T(8,128)(2,1)S(1)} %get-tuple-element.48.after_ref), channel_id=1, source_target_pairs={{0,32},{32,64},{64,96},{96,128},{128,160},{160,192},{192,224},{224... | collective-permute-start | bytes 1179656 | tf_op jit(solution)/shard_map/ppermute | solution.py:411
  86.6 6.5 %state_parts.1 = (bf16[512,4096]{1,0:T(8,128)(2,1)}, f32[8,128]{1,0:T(8,128)S(1)}) custom-call(bf16[512,640]{1,0:T(8,128)(2,1)S(1)} %get-tuple-element.42.low_ref.grad_ref, bf16[512,384]{1,0:T(8,128)(2,1)S(1)} %get-tuple-element.46.high_ref.grad_ref, bf16[8,512,640]{2,1,0:T(8,128)(2,1)S(1)} %get-tuple-element.47.low_weight, ...), custom_call_target="tpu_custom_call" | custom-call | tf_op jit(solution)/shard_map/state_parts/pallas_call | solution.py:422
  93.1 7.1 %all-to-all-start.1 = ((bf16[32,16,4096]{2,1,0:T(8,128)(2,1)}), bf16[32,16,4096]{2,1,0:T(8,128)(2,1)}, u32[]{:S(2)}, u32[]{:S(2)}) async-start(bf16[32,16,4096]{2,1,0:T(8,128)(2,1)} %bitcast.12), calls=%async_computation.1 | async-start | bytes 8388608 | tf_op jit(solution)/shard_map/all_to_all | solution.py:467
  100.3 2.2 %add_part.10 = (bf16[512,640]{1,0:T(8,128)(2,1)S(1)}, f32[8,128]{1,0:T(8,128)S(1)}) custom-call(s32[8]{0:T(128)S(1)} %compare_select_fusion.chunks_ref, bf16[512,640]{1,0:T(8,128)(2,1)S(1)} %collective-permute-done.1.got_ref, bf16[512,4224]{1,0:T(8,128)(2,1)} %bitcast.8.got_ref.rows_ref, bf16[512,640]{1,0:T(8,128)(2,1)S(1)} %get-tuple-element.42.low_ref.grad_ref, ...), custom_call_target="tpu_custom_call" | custom-call | flops 3449999872 | tf_op jit(solution)/shard_map/add_part/pallas_call | solution.py:438
  102.5 3.3 %collective-permute-start.3 = (bf16[512,640]{1,0:T(8,128)(2,1)S(1)}, bf16[512,640]{1,0:T(8,128)(2,1)S(1)}, u32[]{:S(2)}, u32[]{:S(2)}) collective-permute-start(bf16[512,640]{1,0:T(8,128)(2,1)S(1)} %get-tuple-element.55), channel_id=1, source_target_pairs={{0,32},{32,64},{64,96},{96,128},{128,160},{160,192},{192,224},{224... | collective-permute-start | bytes 1966088 | tf_op jit(solution)/shard_map/ppermute | solution.py:411
  105.8 2.2 %add_part.11 = (bf16[512,640]{1,0:T(8,128)(2,1)S(1)}, f32[8,128]{1,0:T(8,128)S(1)}) custom-call(s32[8]{0:T(128)S(1)} %compare_select_fusion.chunks_ref, bf16[512,640]{1,0:T(8,128)(2,1)S(1)} %collective-permute-done.got_ref, bf16[512,4224]{1,0:T(8,128)(2,1)} %bitcast.8.got_ref.rows_ref, bf16[512,640]{1,0:T(8,128)(2,1)S(1)} %get-tuple-element.42.low_ref.grad_ref, ...), custom_call_target="tpu_custom_call" | custom-call | flops 3449999872 | tf_op jit(solution)/shard_map/add_part/pallas_call | solution.py:438
  108.1 5.6 %collective-permute-done.5.got_ref = bf16[512,384]{1,0:T(8,128)(2,1)S(1)} collective-permute-done((bf16[512,384]{1,0:T(8,128)(2,1)}, bf16[512,384]{1,0:T(8,128)(2,1)S(1)}, u32[]{:S(2)}, u32[]{:S(2)}) %collective-permute-start.5) | collective-permute-done | bytes 393248 | tf_op jit(solution)/shard_map/ppermute | solution.py:411
  113.7 2.1 %add_part.12 = (bf16[512,384]{1,0:T(8,128)(2,1)S(1)}, f32[8,128]{1,0:T(8,128)S(1)}) custom-call(s32[8]{0:T(128)S(1)} %compare_select_fusion.chunks_ref, bf16[512,384]{1,0:T(8,128)(2,1)S(1)} %collective-permute-done.5.got_ref, bf16[512,4224]{1,0:T(8,128)(2,1)} %bitcast.8.got_ref.rows_ref, bf16[512,384]{1,0:T(8,128)(2,1)S(1)} %get-tuple-element.46.high_ref.grad_ref, ...), custom_call_target="tpu_custom_call" | custom-call | flops 3449999872 | tf_op jit(solution)/shard_map/add_part/pallas_call | solution.py:438
  115.8 2.2 %add_part.13 = (bf16[512,384]{1,0:T(8,128)(2,1)S(1)}, f32[8,128]{1,0:T(8,128)S(1)}) custom-call(s32[8]{0:T(128)S(1)} %compare_select_fusion.chunks_ref, bf16[512,384]{1,0:T(8,128)(2,1)} %collective-permute-done.4.got_ref, bf16[512,4224]{1,0:T(8,128)(2,1)} %bitcast.8.got_ref.rows_ref, bf16[512,384]{1,0:T(8,128)(2,1)S(1)} %get-tuple-element.46.high_ref.grad_ref, ...), custom_call_target="tpu_custom_call" | custom-call | flops 3449999872 | tf_op jit(solution)/shard_map/add_part/pallas_call | solution.py:438
  118.0 2.0 %collective-permute-start.8 = (bf16[512,384]{1,0:T(8,128)(2,1)S(1)}, bf16[512,384]{1,0:T(8,128)(2,1)S(1)}, u32[]{:S(2)}, u32[]{:S(2)}) collective-permute-start(bf16[512,384]{1,0:T(8,128)(2,1)S(1)} %get-tuple-element.63), channel_id=1, source_target_pairs={{0,224},{32,0},{64,32},{96,64},{128,96},{160,128},{192,160},{224,1... | collective-permute-start | bytes 1179656 | tf_op jit(solution)/shard_map/ppermute | solution.py:411
  121.0 2.2 %add_part.14 = (bf16[512,640]{1,0:T(8,128)(2,1)S(1)}, f32[8,128]{1,0:T(8,128)S(1)}) custom-call(s32[8]{0:T(128)S(1)} %compare_select_fusion.chunks_ref, bf16[512,640]{1,0:T(8,128)(2,1)S(1)} %collective-permute-done.3.got_ref, bf16[512,4224]{1,0:T(8,128)(2,1)} %bitcast.8.got_ref.rows_ref, bf16[512,640]{1,0:T(8,128)(2,1)S(1)} %get-tuple-element.42.low_ref.grad_ref, ...), custom_call_target="tpu_custom_call" | custom-call | flops 3449999872 | tf_op jit(solution)/shard_map/add_part/pallas_call | solution.py:438
  123.1 3.8 %collective-permute-start.11 = (bf16[512,640]{1,0:T(8,128)(2,1)S(1)}, bf16[512,640]{1,0:T(8,128)(2,1)S(1)}, u32[]{:S(2)}, u32[]{:S(2)}) collective-permute-start(bf16[512,640]{1,0:T(8,128)(2,1)S(1)} %get-tuple-element.68), channel_id=1, source_target_pairs={{0,32},{32,64},{64,96},{96,128},{128,160},{160,192},{192,224},{224... | collective-permute-start | bytes 1966088 | tf_op jit(solution)/shard_map/ppermute | solution.py:411
  127.7 2.2 %add_part.15 = (bf16[512,640]{1,0:T(8,128)(2,1)S(1)}, f32[8,128]{1,0:T(8,128)S(1)}) custom-call(s32[8]{0:T(128)S(1)} %compare_select_fusion.chunks_ref, bf16[512,640]{1,0:T(8,128)(2,1)S(1)} %collective-permute-done.2.got_ref, bf16[512,4224]{1,0:T(8,128)(2,1)} %bitcast.8.got_ref.rows_ref, bf16[512,640]{1,0:T(8,128)(2,1)S(1)} %get-tuple-element.42.low_ref.grad_ref, ...), custom_call_target="tpu_custom_call" | custom-call | flops 3449999872 | tf_op jit(solution)/shard_map/add_part/pallas_call | solution.py:438
  129.9 5.4 %collective-permute-done.8.got_ref = bf16[512,384]{1,0:T(8,128)(2,1)S(1)} collective-permute-done((bf16[512,384]{1,0:T(8,128)(2,1)S(1)}, bf16[512,384]{1,0:T(8,128)(2,1)S(1)}, u32[]{:S(2)}, u32[]{:S(2)}) %collective-permute-start.8) | collective-permute-done | bytes 393248 | tf_op jit(solution)/shard_map/ppermute | solution.py:411
  135.4 2.1 %add_part.16 = (bf16[512,384]{1,0:T(8,128)(2,1)S(1)}, f32[8,128]{1,0:T(8,128)S(1)}) custom-call(s32[8]{0:T(128)S(1)} %compare_select_fusion.chunks_ref, bf16[512,384]{1,0:T(8,128)(2,1)S(1)} %collective-permute-done.8.got_ref, bf16[512,4224]{1,0:T(8,128)(2,1)} %bitcast.8.got_ref.rows_ref, bf16[512,384]{1,0:T(8,128)(2,1)S(1)} %get-tuple-element.46.high_ref.grad_ref, ...), custom_call_target="tpu_custom_call" | custom-call | flops 3449999872 | tf_op jit(solution)/shard_map/add_part/pallas_call | solution.py:438
  137.8 2.1 %add_part.17 = (bf16[512,384]{1,0:T(8,128)(2,1)S(1)}, f32[8,128]{1,0:T(8,128)S(1)}) custom-call(s32[8]{0:T(128)S(1)} %compare_select_fusion.chunks_ref, bf16[512,384]{1,0:T(8,128)(2,1)S(1)} %collective-permute-done.7.got_ref, bf16[512,4224]{1,0:T(8,128)(2,1)} %bitcast.8.got_ref.rows_ref, bf16[512,384]{1,0:T(8,128)(2,1)S(1)} %get-tuple-element.46.high_ref.grad_ref, ...), custom_call_target="tpu_custom_call" | custom-call | flops 3449999872 | tf_op jit(solution)/shard_map/add_part/pallas_call | solution.py:438
  139.9 3.3 %collective-permute-start.9 = (bf16[512,384]{1,0:T(8,128)(2,1)S(1)}, bf16[512,384]{1,0:T(8,128)(2,1)S(1)}, u32[]{:S(2)}, u32[]{:S(2)}) collective-permute-start(bf16[512,384]{1,0:T(8,128)(2,1)S(1)} %get-tuple-element.66), channel_id=1, source_target_pairs={{0,32},{32,64},{64,96},{96,128},{128,160},{160,192},{192,224},{224... | collective-permute-start | bytes 1179656 | tf_op jit(solution)/shard_map/ppermute | solution.py:411
  143.2 3.0 %add_part.18 = (bf16[512,640]{1,0:T(8,128)(2,1)}, f32[8,128]{1,0:T(8,128)S(1)}) custom-call(s32[8]{0:T(128)S(1)} %compare_select_fusion.chunks_ref, bf16[512,640]{1,0:T(8,128)(2,1)S(1)} %collective-permute-done.11.got_ref, bf16[512,4224]{1,0:T(8,128)(2,1)} %bitcast.8.got_ref.rows_ref, bf16[512,640]{1,0:T(8,128)(2,1)S(1)} %get-tuple-element.42.low_ref.grad_ref, ...), custom_call_target="tpu_custom_call" | custom-call | flops 3449999872 | tf_op jit(solution)/shard_map/add_part/pallas_call | solution.py:438
  146.2 4.8 %collective-permute-done.10.got_ref = bf16[512,384]{1,0:T(8,128)(2,1)S(1)} collective-permute-done((bf16[512,384]{1,0:T(8,128)(2,1)S(1)}, bf16[512,384]{1,0:T(8,128)(2,1)S(1)}, u32[]{:S(2)}, u32[]{:S(2)}) %collective-permute-start.10) | collective-permute-done | bytes 393248 | tf_op jit(solution)/shard_map/ppermute | solution.py:411
  151.0 2.8 %add_part.19 = (bf16[512,384]{1,0:T(8,128)(2,1)}, f32[8,128]{1,0:T(8,128)S(1)}) custom-call(s32[8]{0:T(128)S(1)} %compare_select_fusion.chunks_ref, bf16[512,384]{1,0:T(8,128)(2,1)S(1)} %collective-permute-done.10.got_ref, bf16[512,4224]{1,0:T(8,128)(2,1)} %bitcast.8.got_ref.rows_ref, bf16[512,384]{1,0:T(8,128)(2,1)S(1)} %get-tuple-element.46.high_ref.grad_ref, ...), custom_call_target="tpu_custom_call" | custom-call | flops 3449999872 | tf_op jit(solution)/shard_map/add_part/pallas_call | solution.py:438
  153.8 3.2 %collective-permute-start.12 = (bf16[512,640]{1,0:T(8,128)(2,1)}, bf16[512,640]{1,0:T(8,128)(2,1)S(1)}, u32[]{:S(2)}, u32[]{:S(2)}) collective-permute-start(bf16[512,640]{1,0:T(8,128)(2,1)} %get-tuple-element.74), channel_id=1, source_target_pairs={{0,32},{32,64},{64,96},{96,128},{128,160},{160,192},{192,224},{224... | collective-permute-start | bytes 1966088 | tf_op jit(solution)/shard_map/ppermute | solution.py:411
  157.0 8.0 %collective-permute-done.6.low_near_ref = bf16[512,640]{1,0:T(8,128)(2,1)S(1)} collective-permute-done((bf16[512,640]{1,0:T(8,128)(2,1)S(1)}, bf16[512,640]{1,0:T(8,128)(2,1)S(1)}, u32[]{:S(2)}, u32[]{:S(2)}) %collective-permute-start.6) | collective-permute-done | bytes 655392 | tf_op jit(solution)/shard_map/ppermute | solution.py:411
  165.0 1.0 copy-done.3
  166.0 2.5 %own_part.1 = (f32[512,1024]{1,0:T(8,128)S(1)}, f32[8,128]{1,0:T(8,128)S(1)}) custom-call(s32[8]{0:T(128)S(1)} %compare_select_fusion.chunks_ref, bf16[512,640]{1,0:T(8,128)(2,1)S(1)} %collective-permute-done.6.low_near_ref, bf16[512,384]{1,0:T(8,128)(2,1)S(1)} %collective-permute-done.9.high_near_ref, bf16[512,4224]{1,0:T(8,128)(2,1)} %bitcast.8.got_ref.rows_ref, ...), custom_call_target="tpu_custom_call" | custom-call | flops 115000000512 | tf_op jit(solution)/shard_map/own_part/pallas_call | solution.py:471
  168.5 3.7 %sum_parts.1 = (bf16[128,4096]{1,0:T(8,128)(2,1)}, f32[8,128]{1,0:T(8,128)S(1)}) custom-call(bf16[128,512]{1,0:T(8,128)(2,1)S(1)} %copy-done.1, bf16[512,4096]{1,0:T(8,128)(2,1)} %bitcast.10.back_ref, f32[8,128]{1,0:T(8,128)S(1)} %get-tuple-element.72.after_ref), custom_call_target="tpu_custom_call" | custom-call | tf_op jit(solution)/shard_map/sum_parts/pallas_call | solution.py:491
  172.3 2.1 %last_add.1 = bf16[512,1024]{1,0:T(8,128)(2,1)} custom-call(bf16[512,640]{1,0:T(8,128)(2,1)S(1)} %collective-permute-done.12.low_far_ref, bf16[512,384]{1,0:T(8,128)(2,1)} %collective-permute-done.13.high_far_ref, f32[512,1024]{1,0:T(8,128)S(1)} %get-tuple-element.76.own_ref, f32[8,128]{1,0:T(8,128)S(1)} %get-tuple-element.77.after_ref), custom_call_target="tpu_custom_call" | custom-call | tf_op jit(solution)/shard_map/last_add/pallas_call | solution.py:505
  (29 shorter events, 2.5 us)
Async XLA Ops:
  5.5 60.5 %all-to-all-start = ((bf16[32,16,4224]{2,1,0:T(8,128)(2,1)}), bf16[32,16,4224]{2,1,0:T(8,128)(2,1)}, u32[]{:S(2)}, u32[]{:S(2)}) async-start(bf16[32,16,4224]{2,1,0:T(8,128)(2,1)} %bitcast.11), calls=%async_computation | async-start | bytes 8650752 | tf_op jit(solution)/shard_map/all_to_all | solution.py:358
  13.3 62.9 %copy-start = (bf16[128,512]{1,0:T(8,128)(2,1)}, bf16[128,512]{1,0:T(8,128)(2,1)S(1)}, u32[]{:S(2)}) copy-start(bf16[128,512]{1,0:T(8,128)(2,1)S(1)} %turn_places.1.after_ref.placed_ref) | copy-start | bytes 393220
  76.2 24.1 %collective-permute-start.1 = (bf16[512,640]{1,0:T(8,128)(2,1)}, bf16[512,640]{1,0:T(8,128)(2,1)S(1)}, u32[]{:S(2)}, u32[]{:S(2)}) collective-permute-start(bf16[512,640]{1,0:T(8,128)(2,1)} %get-tuple-element.51), channel_id=1, source_target_pairs={{0,32},{32,64},{64,96},{96,128},{128,160},{160,192},{192,224},{224... | collective-permute-start | bytes 1966088 | tf_op jit(solution)/shard_map/ppermute | solution.py:411
  79.4 26.4 %collective-permute-start = (bf16[512,640]{1,0:T(8,128)(2,1)S(1)}, bf16[512,640]{1,0:T(8,128)(2,1)S(1)}, u32[]{:S(2)}, u32[]{:S(2)}) collective-permute-start(bf16[512,640]{1,0:T(8,128)(2,1)S(1)} %get-tuple-element.50), channel_id=1, source_target_pairs={{0,224},{32,0},{64,32},{96,64},{128,96},{160,128},{192,160},{224,1... | collective-permute-start | bytes 1966088 | tf_op jit(solution)/shard_map/ppermute | solution.py:411
  83.1 10.0 %copy-start.4 = (bf16[512,384]{1,0:T(8,128)(2,1)}, bf16[512,384]{1,0:T(8,128)(2,1)S(1)}, u32[]{:S(2)}) copy-start(bf16[512,384]{1,0:T(8,128)(2,1)S(1)} %get-tuple-element.56) | copy-start | bytes 1179652
  83.1 67.9 %copy-start.2 = (bf16[512,384]{1,0:T(8,128)(2,1)}, bf16[512,384]{1,0:T(8,128)(2,1)S(1)}, u32[]{:S(2)}) copy-start(bf16[512,384]{1,0:T(8,128)(2,1)S(1)} %get-tuple-element.46.high_ref.grad_ref) | copy-start | bytes 1179652
  83.1 32.6 %collective-permute-start.4 = (bf16[512,384]{1,0:T(8,128)(2,1)S(1)}, bf16[512,384]{1,0:T(8,128)(2,1)}, u32[]{:S(2)}, u32[]{:S(2)}) collective-permute-start(bf16[512,384]{1,0:T(8,128)(2,1)S(1)} %get-tuple-element.48.after_ref), channel_id=1, source_target_pairs={{0,32},{32,64},{64,96},{96,128},{128,160},{160,192},{192,224},{224... | collective-permute-start | bytes 1179656 | tf_op jit(solution)/shard_map/ppermute | solution.py:411
  93.1 75.4 %all-to-all-start.1 = ((bf16[32,16,4096]{2,1,0:T(8,128)(2,1)}), bf16[32,16,4096]{2,1,0:T(8,128)(2,1)}, u32[]{:S(2)}, u32[]{:S(2)}) async-start(bf16[32,16,4096]{2,1,0:T(8,128)(2,1)} %bitcast.12), calls=%async_computation.1 | async-start | bytes 8388608 | tf_op jit(solution)/shard_map/all_to_all | solution.py:467
  100.2 13.5 %collective-permute-start.5 = (bf16[512,384]{1,0:T(8,128)(2,1)}, bf16[512,384]{1,0:T(8,128)(2,1)S(1)}, u32[]{:S(2)}, u32[]{:S(2)}) collective-permute-start(bf16[512,384]{1,0:T(8,128)(2,1)} %copy-done.4), channel_id=1, source_target_pairs={{0,224},{32,0},{64,32},{96,64},{128,96},{160,128},{192,160},{224,1... | collective-permute-start | bytes 1179656 | tf_op jit(solution)/shard_map/ppermute | solution.py:411
  102.5 18.4 %collective-permute-start.3 = (bf16[512,640]{1,0:T(8,128)(2,1)S(1)}, bf16[512,640]{1,0:T(8,128)(2,1)S(1)}, u32[]{:S(2)}, u32[]{:S(2)}) collective-permute-start(bf16[512,640]{1,0:T(8,128)(2,1)S(1)} %get-tuple-element.55), channel_id=1, source_target_pairs={{0,32},{32,64},{64,96},{96,128},{128,160},{160,192},{192,224},{224... | collective-permute-start | bytes 1966088 | tf_op jit(solution)/shard_map/ppermute | solution.py:411
  108.0 19.7 %collective-permute-start.2 = (bf16[512,640]{1,0:T(8,128)(2,1)S(1)}, bf16[512,640]{1,0:T(8,128)(2,1)S(1)}, u32[]{:S(2)}, u32[]{:S(2)}) collective-permute-start(bf16[512,640]{1,0:T(8,128)(2,1)S(1)} %get-tuple-element.54), channel_id=1, source_target_pairs={{0,224},{32,0},{64,32},{96,64},{128,96},{160,128},{192,160},{224,1... | collective-permute-start | bytes 1966088 | tf_op jit(solution)/shard_map/ppermute | solution.py:411
  117.9 19.9 %collective-permute-start.7 = (bf16[512,384]{1,0:T(8,128)(2,1)S(1)}, bf16[512,384]{1,0:T(8,128)(2,1)S(1)}, u32[]{:S(2)}, u32[]{:S(2)}) collective-permute-start(bf16[512,384]{1,0:T(8,128)(2,1)S(1)} %get-tuple-element.62), channel_id=1, source_target_pairs={{0,32},{32,64},{64,96},{96,128},{128,160},{160,192},{192,224},{224... | collective-permute-start | bytes 1179656 | tf_op jit(solution)/shard_map/ppermute | solution.py:411
  118.0 17.3 %collective-permute-start.8 = (bf16[512,384]{1,0:T(8,128)(2,1)S(1)}, bf16[512,384]{1,0:T(8,128)(2,1)S(1)}, u32[]{:S(2)}, u32[]{:S(2)}) collective-permute-start(bf16[512,384]{1,0:T(8,128)(2,1)S(1)} %get-tuple-element.63), channel_id=1, source_target_pairs={{0,224},{32,0},{64,32},{96,64},{128,96},{160,128},{192,160},{224,1... | collective-permute-start | bytes 1179656 | tf_op jit(solution)/shard_map/ppermute | solution.py:411
  123.1 20.1 %collective-permute-start.11 = (bf16[512,640]{1,0:T(8,128)(2,1)S(1)}, bf16[512,640]{1,0:T(8,128)(2,1)S(1)}, u32[]{:S(2)}, u32[]{:S(2)}) collective-permute-start(bf16[512,640]{1,0:T(8,128)(2,1)S(1)} %get-tuple-element.68), channel_id=1, source_target_pairs={{0,32},{32,64},{64,96},{96,128},{128,160},{160,192},{192,224},{224... | collective-permute-start | bytes 1966088 | tf_op jit(solution)/shard_map/ppermute | solution.py:411
  137.4 13.6 %collective-permute-start.10 = (bf16[512,384]{1,0:T(8,128)(2,1)S(1)}, bf16[512,384]{1,0:T(8,128)(2,1)S(1)}, u32[]{:S(2)}, u32[]{:S(2)}) collective-permute-start(bf16[512,384]{1,0:T(8,128)(2,1)S(1)} %get-tuple-element.67), channel_id=1, source_target_pairs={{0,224},{32,0},{64,32},{96,64},{128,96},{160,128},{192,160},{224,1... | collective-permute-start | bytes 1179656 | tf_op jit(solution)/shard_map/ppermute | solution.py:411
  137.7 27.3 %collective-permute-start.6 = (bf16[512,640]{1,0:T(8,128)(2,1)S(1)}, bf16[512,640]{1,0:T(8,128)(2,1)S(1)}, u32[]{:S(2)}, u32[]{:S(2)}) collective-permute-start(bf16[512,640]{1,0:T(8,128)(2,1)S(1)} %get-tuple-element.61), channel_id=1, source_target_pairs={{0,224},{32,0},{64,32},{96,64},{128,96},{160,128},{192,160},{224,1... | collective-permute-start | bytes 1966088 | tf_op jit(solution)/shard_map/ppermute | solution.py:411
  139.9 17.1 %collective-permute-start.9 = (bf16[512,384]{1,0:T(8,128)(2,1)S(1)}, bf16[512,384]{1,0:T(8,128)(2,1)S(1)}, u32[]{:S(2)}, u32[]{:S(2)}) collective-permute-start(bf16[512,384]{1,0:T(8,128)(2,1)S(1)} %get-tuple-element.66), channel_id=1, source_target_pairs={{0,32},{32,64},{64,96},{96,128},{128,160},{160,192},{192,224},{224... | collective-permute-start | bytes 1179656 | tf_op jit(solution)/shard_map/ppermute | solution.py:411
  153.8 18.5 %collective-permute-start.13 = (bf16[512,384]{1,0:T(8,128)(2,1)}, bf16[512,384]{1,0:T(8,128)(2,1)}, u32[]{:S(2)}, u32[]{:S(2)}) collective-permute-start(bf16[512,384]{1,0:T(8,128)(2,1)} %get-tuple-element.75), channel_id=1, source_target_pairs={{0,224},{32,0},{64,32},{96,64},{128,96},{160,128},{192,160},{224,1... | collective-permute-start | bytes 1179656 | tf_op jit(solution)/shard_map/ppermute | solution.py:411
  153.8 18.5 %collective-permute-start.12 = (bf16[512,640]{1,0:T(8,128)(2,1)}, bf16[512,640]{1,0:T(8,128)(2,1)S(1)}, u32[]{:S(2)}, u32[]{:S(2)}) collective-permute-start(bf16[512,640]{1,0:T(8,128)(2,1)} %get-tuple-element.74), channel_id=1, source_target_pairs={{0,32},{32,64},{64,96},{96,128},{128,160},{160,192},{192,224},{224... | collective-permute-start | bytes 1966088 | tf_op jit(solution)/shard_map/ppermute | solution.py:411
  165.0 1.0 copy-start.3
  166.0 2.5 %copy-start.1 = (bf16[128,512]{1,0:T(8,128)(2,1)S(1)}, bf16[128,512]{1,0:T(8,128)(2,1)}, u32[]{:S(2)}) copy-start(bf16[128,512]{1,0:T(8,128)(2,1)} %copy-done) | copy-start | bytes 393220

commit v6 on v4

--- a/solution.py
+++ b/solution.py
@@ -10,14 +10,14 @@
 BLOCK = 128
 BLK_DEV = 8
 META = 128
-GAP = 0
+GAP = 2
 STEPS = 4
-LOW_BLOCKS = 5
+LOW_BLOCKS = 4
 MIB = 1 << 20
 F32 = jnp.float32
 BF16 = jnp.bfloat16
-HOPS_US = (3,) * 10
-OWN_US, SUM_US, HIGH_US, STATE_US, LAST_US = 100, 0, 0, 0, 0
+HOPS_US = (3, 3, 3, 3, 3, 3, 3, 3, 30, 30)
+SUM_US, HIGH_US, STATE_US, LAST_US = 0, 2, 4, 20
 
 
 def cost(us):
@@ -171,16 +171,14 @@
     rows_ref,
     meta_ref,
     low_weight,
-    high_weight,
     grad_ref,
     far_ref,
     near_ref,
     acc,
     sems,
 ):
-    steps, depth, some = low_weight.shape
+    steps, depth, _ = low_weight.shape
     weights = weight_loads(weight_ref, low_weight, sems.at[0], 0)
-    others = weight_loads(weight_ref, high_weight, sems.at[1], some)
     loads = []
     for k in range(steps):
         cut = pl.ds(k * depth, depth)
@@ -190,8 +188,6 @@
         weights[k].start()
         loads[k].start()
     last.start()
-    for other in others:
-        other.start()
 
     def ready(k):
         if k == steps:
@@ -201,14 +197,20 @@
             loads[k].wait()
 
     score_half(0, chunks_ref, rows_ref, meta_ref, low_weight, grad_ref, far_ref, near_ref, acc, ready)
-    for other in others:
-        other.wait()
-
-
-def high_kernel(base, chunks_ref, rows_ref, meta_ref, weight, grad_ref, far_ref, near_ref, acc):
-    score_half(
-        base, chunks_ref, rows_ref, meta_ref, weight, grad_ref, far_ref, near_ref, acc, lambda k: None
-    )
+
+
+def high_kernel(
+    base, chunks_ref, rows_ref, meta_ref, weight_ref, weight, grad_ref, far_ref, near_ref, acc, sems
+):
+    loads = weight_loads(weight_ref, weight, sems, base)
+    for load in loads:
+        load.start()
+
+    def ready(k):
+        if k < len(loads):
+            loads[k].wait()
+
+    score_half(base, chunks_ref, rows_ref, meta_ref, weight, grad_ref, far_ref, near_ref, acc, ready)
 
 
 def back_kernel(
@@ -241,28 +243,37 @@
     token_ref[...] = jnp.zeros_like(token_ref)
 
 
-def own_kernel(
-    chunks_ref, low_near_ref, high_near_ref, rows_ref, low_ref, high_ref, after_ref, out_ref, token_ref
+def last_kernel(
+    chunks_ref,
+    low_far_ref,
+    low_near_ref,
+    high_far_ref,
+    high_near_ref,
+    got_ref,
+    low_ref,
+    high_ref,
+    after_ref,
+    out_ref,
+    rows,
+    out,
+    sems,
 ):
-    token_ref[...] = jnp.zeros_like(token_ref)
-    base = 0
-    for near_ref, grad_ref in ((low_near_ref, low_ref), (high_near_ref, high_ref)):
-        own = lax.dot_general(rows_ref[...], grad_ref[...], CONTRACT_ROWS, preferred_element_type=F32)
-        out_ref[:, base : base + grad_ref.shape[1]] = near_ref[...].astype(F32) + own
-        base += grad_ref.shape[1]
-
-
-def last_kernel(low_far_ref, high_far_ref, own_ref, after_ref, out_ref, out, sems):
-    pieces = sems.shape[0]
-    piece = out.shape[0] // pieces
-    base = low_far_ref.shape[1]
+    chunk, base = low_far_ref.shape
+    cut = pl.ds(pl.multiple_of(chunks_ref[0] * chunk, chunk), chunk)
+    load = pltpu.make_async_copy(got_ref.at[:, cut], rows, sems.at[2])
+    load.start()
+    load.wait()
     stores = []
-    for k in range(pieces):
-        rows = slice(k * piece, (k + 1) * piece)
-        out[rows, :base] = (own_ref[rows, :base] + low_far_ref[rows, :].astype(F32)).astype(BF16)
-        out[rows, base:] = (own_ref[rows, base:] + high_far_ref[rows, :].astype(F32)).astype(BF16)
-        cut = pl.ds(k * piece, piece)
-        stores.append(pltpu.make_async_copy(out.at[cut, :], out_ref.at[cut, :], sems.at[k]))
+    for k, (far_ref, near_ref, grad_ref, words) in enumerate(
+        (
+            (low_far_ref, low_near_ref, low_ref, slice(0, base)),
+            (high_far_ref, high_near_ref, high_ref, slice(base, out.shape[1])),
+        )
+    ):
+        own = lax.dot_general(rows[...], grad_ref[...], CONTRACT_ROWS, preferred_element_type=F32)
+        out[:, words] = (own + (far_ref[...].astype(F32) + near_ref[...].astype(F32))).astype(BF16)
+        cut = pl.ds(words.start, words.stop - words.start)
+        stores.append(pltpu.make_async_copy(out.at[:, cut], out_ref.at[:, cut], sems.at[k]))
         stores[k].start()
     for store in stores:
         store.wait()
@@ -371,15 +382,14 @@
     token = jax.ShapeDtypeStruct((8, 128), F32)
     depth = width // STEPS
     rest = words - base
-    rows, meta, low_weight, high_weight, low, low_far, low_near = pl.pallas_call(
+    rows, meta, low_weight, low, low_far, low_near = pl.pallas_call(
         low_kernel,
         in_specs=[smem, hbm, hbm, anywhere],
-        out_specs=[vmem] * 7,
+        out_specs=[vmem] * 6,
         out_shape=[
             like(slots, width),
             like(slots, META),
             like(STEPS, depth, base),
-            like(STEPS, depth, rest),
             like(slots, base),
             like(chunk, base),
             like(chunk, base),
@@ -389,16 +399,16 @@
         cost_estimate=cost(0),
         name="low_scores",
     )(chunks, got, weights, placed)
-    high, high_far, high_near = pl.pallas_call(
+    high_weight, high, high_far, high_near = pl.pallas_call(
         functools.partial(high_kernel, base),
-        in_specs=[smem, vmem, vmem, vmem],
-        out_specs=[vmem] * 3,
-        out_shape=[like(slots, rest), like(chunk, rest), like(chunk, rest)],
-        scratch_shapes=[pltpu.VMEM((slots, rest), F32)],
+        in_specs=[smem, vmem, vmem, hbm],
+        out_specs=[vmem] * 4,
+        out_shape=[like(STEPS, depth, rest), like(slots, rest), like(chunk, rest), like(chunk, rest)],
+        scratch_shapes=[pltpu.VMEM((slots, rest), F32), pltpu.SemaphoreType.DMA((STEPS,))],
         compiler_params=params(16),
         cost_estimate=cost(HIGH_US),
         name="high_scores",
-    )(chunks, rows, meta, high_weight)
+    )(chunks, rows, meta, weights)
 
     def hop(x, d):
         return lax.ppermute(x, "dp", [(i, (i + d) % planes) for i in range(planes)])
@@ -461,26 +471,6 @@
         part.reshape(peers, capacity, width), "vocab", split_axis=0, concat_axis=0, tiled=True
     ).reshape(slots, width)
 
-    own, after = pl.pallas_call(
-        own_kernel,
-        grid_spec=pltpu.PrefetchScalarGridSpec(
-            num_scalar_prefetch=1,
-            grid=(1,),
-            in_specs=[
-                message_spec(base),
-                message_spec(rest),
-                rows_spec(0),
-                message_spec(base),
-                message_spec(rest),
-                anywhere,
-            ],
-            out_specs=[pl.BlockSpec((chunk, words), lambda i, c: (0, 0)), token_spec],
-        ),
-        out_shape=[jax.ShapeDtypeStruct((chunk, words), F32), token],
-        compiler_params=params(16),
-        cost_estimate=cost(OWN_US),
-        name="own_part",
-    )(chunks, messages[1], messages[3], got, low, high, after)
     hidden_grad, after = pl.pallas_call(
         sum_kernel,
         in_specs=[vmem, hbm, anywhere],
@@ -497,14 +487,18 @@
     )(placed, in_hbm(back), after)
     weight_grad = pl.pallas_call(
         last_kernel,
-        in_specs=[vmem, vmem, vmem, anywhere],
+        in_specs=[smem] + [vmem] * 4 + [hbm, vmem, vmem, anywhere],
         out_specs=hbm,
         out_shape=pltpu.HBM((chunk, words), BF16),
-        scratch_shapes=[pltpu.VMEM((chunk, words), BF16), pltpu.SemaphoreType.DMA((2,))],
+        scratch_shapes=[
+            pltpu.VMEM((slots, chunk), BF16),
+            pltpu.VMEM((chunk, words), BF16),
+            pltpu.SemaphoreType.DMA((3,)),
+        ],
         compiler_params=params(12),
         cost_estimate=cost(LAST_US),
         name="last_add",
-    )(messages[0], messages[2], own, after)
+    )(chunks, messages[0], messages[1], messages[2], messages[3], got, low, high, after)
     return (hidden_grad, weight_grad)
 
 

time: 175 us -> 177 us (1.011)
  waiting for transfers between devices: 78.3 us -> 84 us
  Pallas kernels: 56 us -> 52.1 us
    ppermute x14, waiting for transfers between devices: 25.6 us -> 30.6 us  [hop(): return lax.ppermute(x, 'dp', [(i, (i + d) % planes) for i in range(planes)])]
    pallas_call x1, Pallas kernels: 10.1 us -> 6.39 us  [body(): pl.pallas_call(low_kernel, in_specs=[smem, hbm, hbm, anywhere], out_specs...]
    pallas_call x1, Pallas kernels: 3.71 us -> 5.82 us  [body(): pl.pallas_call(functools.partial(high_kernel, base), in_specs=[smem, vmem...]
    pallas_call x2 -> x1, Pallas kernels: 4.55 us -> 3.86 us  [body(): pl.pallas_call(last_kernel, in_specs=[smem] + [vmem] * 4 + [hbm, vmem, vm...]
  transfers between devices with their start and end apart: 16 -> 16, of which waited for: 8 -> 10; matrix products, arithmetic and copies ran while one was open for 0% -> 0% of each run, Pallas kernels for 22% -> 21%
where the time goes in v6:
time: 177 us; the launch traced here: 176 us
  waiting for transfers between devices  84 us (47%)
  Pallas kernels  52.1 us (29%)
  starting transfers between devices  38.9 us (22%)
    all_to_all x1, waiting for transfers between devices, body(): lax.all_to_all(send.reshape(peers, capacity, sent), 'vocab', split_axis=0...  52.7 us
    ppermute x14, waiting for transfers between devices, hop(): return lax.ppermute(x, 'dp', [(i, (i + d) % planes) for i in range(planes)])  30.6 us
    ppermute x14, starting transfers between devices, hop(): return lax.ppermute(x, 'dp', [(i, (i + d) % planes) for i in range(planes)])  24.1 us
    pallas_call x10, Pallas kernels, add(): pl.pallas_call(add_kernel, grid_spec=pltpu.PrefetchScalarGridSpec(num_sca...  22.3 us
    all_to_all x1, starting transfers between devices, body(): lax.all_to_all(send.reshape(peers, capacity, sent), 'vocab', split_axis=0...  7.68 us
    all_to_all x1, starting transfers between devices, body(): lax.all_to_all(part.reshape(peers, capacity, width), 'vocab', split_axis=...  7.09 us
    pallas_call x1, Pallas kernels, body(): pl.pallas_call(low_kernel, in_specs=[smem, hbm, hbm, anywhere], out_specs...  6.39 us
    pallas_call x1, Pallas kernels, body(): pl.pallas_call(functools.partial(high_kernel, base), in_specs=[smem, vmem...  5.82 us
  transfers between devices with their start and end apart: 16, of which 10 were waited for; matrix products, arithmetic and copies ran while one was open for 0% of the time, Pallas kernels for 21%

profile of v6, /device:TPU:98, one launch (start us, length us, event | category | flops | bytes accessed | tf_op | source)
XLA Modules:
  0.0 176.0 jit_solution(9946733799399461769)
XLA Ops:
  0.6 4.8 %place_rows.1 = (bf16[512,4224]{1,0:T(8,128)(2,1)}, bf16[512,128]{1,0:T(8,128)(2,1)S(1)}) custom-call(bf16[128,4096]{1,0:T(8,128)(2,1)} %hidden_ref.1, s32[3,128]{1,0:T(4,128)} %bitcast.15, s32[3,2,128]{2,1,0:T(2,128)} %bitcast.13, s32[3,2,128]{2,1,0:T(2,128)} %bitcast.14, s32[1,128]{1,0:T(1,128)} %bitcast.16, s32[1,128]{1,0:T(1,128)} %bitcast.17, ...), custom_call_target="tpu_custom_call" | custom-call | tf_op jit(solution)/shard_map/place_rows/pallas_call | solution.py:344
  5.5 7.7 %all-to-all-start = ((bf16[32,16,4224]{2,1,0:T(8,128)(2,1)}), bf16[32,16,4224]{2,1,0:T(8,128)(2,1)}, u32[]{:S(2)}, u32[]{:S(2)}) async-start(bf16[32,16,4224]{2,1,0:T(8,128)(2,1)} %bitcast.11), calls=%async_computation | async-start | bytes 8650752 | tf_op jit(solution)/shard_map/all_to_all | solution.py:362
  13.3 52.7 %all-to-all-done = bf16[32,16,4224]{2,1,0:T(8,128)(2,1)} async-done(((bf16[32,16,4224]{2,1,0:T(8,128)(2,1)}), bf16[32,16,4224]{2,1,0:T(8,128)(2,1)}, u32[]{:S(2)}, u32[]{:S(2)}) %all-to-all-start) | async-done | bytes 4325408 | tf_op jit(solution)/shard_map/all_to_all | solution.py:362
  66.0 6.4 %low_scores.1 = (bf16[512,4096]{1,0:T(8,128)(2,1)S(1)}, bf16[512,128]{1,0:T(8,128)(2,1)S(1)}, bf16[4,1024,512]{2,1,0:T(8,128)(2,1)S(1)}, bf16[512,512]{1,0:T(8,1...) custom-call(s32[8]{0:T(128)S(1)} %compare_select_fusion.chunks_ref, ...), custom_call_target="tpu_custom_call" | custom-call | tf_op jit(solution)/shard_map/low_scores/pallas_call | solution.py:385
  72.4 3.2 %collective-permute-start.1 = (bf16[512,512]{1,0:T(8,128)(2,1)S(1)}, bf16[512,512]{1,0:T(8,128)(2,1)S(1)}, u32[]{:S(2)}, u32[]{:S(2)}) collective-permute-start(bf16[512,512]{1,0:T(8,128)(2,1)S(1)} %get-tuple-element.47), channel_id=1, source_target_pairs={{0,32},{32,64},{64,96},{96,128},{128,160},{160,192},{192,224},{224... | collective-permute-start | bytes 1572872 | tf_op jit(solution)/shard_map/ppermute | solution.py:414
  75.6 5.8 %high_scores.1 = (bf16[4,1024,512]{2,1,0:T(8,128)(2,1)S(1)}, bf16[512,512]{1,0:T(8,128)(2,1)S(1)}, bf16[512,512]{1,0:T(8,128)(2,1)}, bf16[512,512]{1,0:T(8,128)(2,1)S(1)}) custom-call(s32[8]{0:T(128)S(1)} %compare_select_fusion.chunks_ref, bf16[512,4096]{1,0:T(8,128)(2,1)S(1)} %get-tuple-element.41.rows_ref, ...), custom_call_target="tpu_custom_call" | custom-call | flops 2300000000 | tf_op jit(solution)/shard_map/high_scores/pallas_call | solution.py:402
  81.5 3.5 %collective-permute-start.6 = (bf16[512,512]{1,0:T(8,128)(2,1)S(1)}, bf16[512,512]{1,0:T(8,128)(2,1)S(1)}, u32[]{:S(2)}, u32[]{:S(2)}) collective-permute-start(bf16[512,512]{1,0:T(8,128)(2,1)S(1)} %get-tuple-element.48.after_ref), channel_id=1, source_target_pairs={{0,32},{32,64},{64,96},{96,128},{128,160},{160,192},{192,224},{224... | collective-permute-start | bytes 1572872 | tf_op jit(solution)/shard_map/ppermute | solution.py:414
  85.0 2.9 %collective-permute-done.1.got_ref = bf16[512,512]{1,0:T(8,128)(2,1)S(1)} collective-permute-done((bf16[512,512]{1,0:T(8,128)(2,1)S(1)}, bf16[512,512]{1,0:T(8,128)(2,1)S(1)}, u32[]{:S(2)}, u32[]{:S(2)}) %collective-permute-start.1) | collective-permute-done | bytes 524320 | tf_op jit(solution)/shard_map/ppermute | solution.py:414
  87.9 2.1 %add_part.10 = (bf16[512,512]{1,0:T(8,128)(2,1)S(1)}, f32[8,128]{1,0:T(8,128)S(1)}) custom-call(s32[8]{0:T(128)S(1)} %compare_select_fusion.chunks_ref, bf16[512,512]{1,0:T(8,128)(2,1)S(1)} %collective-permute-done.1.got_ref, bf16[512,4224]{1,0:T(8,128)(2,1)} %bitcast.8.got_ref.rows_ref, bf16[512,512]{1,0:T(8,128)(2,1)S(1)} %get-tuple-element.40.grad_ref.low_ref, ...), custom_call_target="tpu_custom_call" | custom-call | flops 3449999872 | tf_op jit(solution)/shard_map/add_part/pallas_call | solution.py:441
  91.7 2.1 %add_part.11 = (bf16[512,512]{1,0:T(8,128)(2,1)S(1)}, f32[8,128]{1,0:T(8,128)S(1)}) custom-call(s32[8]{0:T(128)S(1)} %compare_select_fusion.chunks_ref, bf16[512,512]{1,0:T(8,128)(2,1)S(1)} %collective-permute-done.got_ref, bf16[512,4224]{1,0:T(8,128)(2,1)} %bitcast.8.got_ref.rows_ref, bf16[512,512]{1,0:T(8,128)(2,1)S(1)} %get-tuple-element.40.grad_ref.low_ref, ...), custom_call_target="tpu_custom_call" | custom-call | flops 3449999872 | tf_op jit(solution)/shard_map/add_part/pallas_call | solution.py:441
  93.7 5.5 %state_parts.1 = (bf16[512,4096]{1,0:T(8,128)(2,1)}, f32[8,128]{1,0:T(8,128)S(1)}) custom-call(bf16[512,512]{1,0:T(8,128)(2,1)S(1)} %get-tuple-element.40.grad_ref.low_ref, bf16[512,512]{1,0:T(8,128)(2,1)S(1)} %get-tuple-element.43.high_ref.grad_ref, bf16[4,1024,512]{2,1,0:T(8,128)(2,1)S(1)} %get-tuple-element.44.low_weight, ...), custom_call_target="tpu_custom_call" | custom-call | flops 4600000000 | tf_op jit(solution)/shard_map/state_parts/pallas_call | solution.py:425
  99.2 7.1 %all-to-all-start.1 = ((bf16[32,16,4096]{2,1,0:T(8,128)(2,1)}), bf16[32,16,4096]{2,1,0:T(8,128)(2,1)}, u32[]{:S(2)}, u32[]{:S(2)}) async-start(bf16[32,16,4096]{2,1,0:T(8,128)(2,1)} %bitcast.12), calls=%async_computation.1 | async-start | bytes 8388608 | tf_op jit(solution)/shard_map/all_to_all | solution.py:470
  106.4 3.2 %collective-permute-start.5 = (bf16[512,512]{1,0:T(8,128)(2,1)S(1)}, bf16[512,512]{1,0:T(8,128)(2,1)S(1)}, u32[]{:S(2)}, u32[]{:S(2)}) collective-permute-start(bf16[512,512]{1,0:T(8,128)(2,1)S(1)} %get-tuple-element.56), channel_id=1, source_target_pairs={{0,32},{32,64},{64,96},{96,128},{128,160},{160,192},{192,224},{224... | collective-permute-start | bytes 1572872 | tf_op jit(solution)/shard_map/ppermute | solution.py:414
  109.6 2.2 %add_part.12 = (bf16[512,512]{1,0:T(8,128)(2,1)S(1)}, f32[8,128]{1,0:T(8,128)S(1)}) custom-call(s32[8]{0:T(128)S(1)} %compare_select_fusion.chunks_ref, bf16[512,512]{1,0:T(8,128)(2,1)} %collective-permute-done.2.got_ref, bf16[512,4224]{1,0:T(8,128)(2,1)} %bitcast.8.got_ref.rows_ref, bf16[512,512]{1,0:T(8,128)(2,1)S(1)} %get-tuple-element.43.high_ref.grad_ref, ...), custom_call_target="tpu_custom_call" | custom-call | flops 3449999872 | tf_op jit(solution)/shard_map/add_part/pallas_call | solution.py:441
  111.9 2.1 %add_part.13 = (bf16[512,512]{1,0:T(8,128)(2,1)S(1)}, f32[8,128]{1,0:T(8,128)S(1)}) custom-call(s32[8]{0:T(128)S(1)} %compare_select_fusion.chunks_ref, bf16[512,512]{1,0:T(8,128)(2,1)S(1)} %collective-permute-done.6.got_ref, bf16[512,4224]{1,0:T(8,128)(2,1)} %bitcast.8.got_ref.rows_ref, bf16[512,512]{1,0:T(8,128)(2,1)S(1)} %get-tuple-element.43.high_ref.grad_ref, ...), custom_call_target="tpu_custom_call" | custom-call | flops 3449999872 | tf_op jit(solution)/shard_map/add_part/pallas_call | solution.py:441
  114.0 3.3 %collective-permute-start.9 = (bf16[512,512]{1,0:T(8,128)(2,1)S(1)}, bf16[512,512]{1,0:T(8,128)(2,1)S(1)}, u32[]{:S(2)}, u32[]{:S(2)}) collective-permute-start(bf16[512,512]{1,0:T(8,128)(2,1)S(1)} %get-tuple-element.63), channel_id=1, source_target_pairs={{0,32},{32,64},{64,96},{96,128},{128,160},{160,192},{192,224},{224... | collective-permute-start | bytes 1572872 | tf_op jit(solution)/shard_map/ppermute | solution.py:414
  117.3 4.6 %collective-permute-done.5.got_ref = bf16[512,512]{1,0:T(8,128)(2,1)S(1)} collective-permute-done((bf16[512,512]{1,0:T(8,128)(2,1)S(1)}, bf16[512,512]{1,0:T(8,128)(2,1)S(1)}, u32[]{:S(2)}, u32[]{:S(2)}) %collective-permute-start.5) | collective-permute-done | bytes 524320 | tf_op jit(solution)/shard_map/ppermute | solution.py:414
  121.9 2.1 %add_part.14 = (bf16[512,512]{1,0:T(8,128)(2,1)S(1)}, f32[8,128]{1,0:T(8,128)S(1)}) custom-call(s32[8]{0:T(128)S(1)} %compare_select_fusion.chunks_ref, bf16[512,512]{1,0:T(8,128)(2,1)S(1)} %collective-permute-done.5.got_ref, bf16[512,4224]{1,0:T(8,128)(2,1)} %bitcast.8.got_ref.rows_ref, bf16[512,512]{1,0:T(8,128)(2,1)S(1)} %get-tuple-element.40.grad_ref.low_ref, ...), custom_call_target="tpu_custom_call" | custom-call | flops 3449999872 | tf_op jit(solution)/shard_map/add_part/pallas_call | solution.py:441
  124.0 3.8 %collective-permute-start.8 = (bf16[512,512]{1,0:T(8,128)(2,1)S(1)}, bf16[512,512]{1,0:T(8,128)(2,1)S(1)}, u32[]{:S(2)}, u32[]{:S(2)}) collective-permute-start(bf16[512,512]{1,0:T(8,128)(2,1)S(1)} %get-tuple-element.62), channel_id=1, source_target_pairs={{0,32},{32,64},{64,96},{96,128},{128,160},{160,192},{192,224},{224... | collective-permute-start | bytes 1572872 | tf_op jit(solution)/shard_map/ppermute | solution.py:414
  127.8 2.1 %add_part.15 = (bf16[512,512]{1,0:T(8,128)(2,1)S(1)}, f32[8,128]{1,0:T(8,128)S(1)}) custom-call(s32[8]{0:T(128)S(1)} %compare_select_fusion.chunks_ref, bf16[512,512]{1,0:T(8,128)(2,1)S(1)} %collective-permute-done.4.got_ref, bf16[512,4224]{1,0:T(8,128)(2,1)} %bitcast.8.got_ref.rows_ref, bf16[512,512]{1,0:T(8,128)(2,1)S(1)} %get-tuple-element.40.grad_ref.low_ref, ...), custom_call_target="tpu_custom_call" | custom-call | flops 3449999872 | tf_op jit(solution)/shard_map/add_part/pallas_call | solution.py:441
  129.8 3.0 %collective-permute-done.3.got_ref = bf16[512,512]{1,0:T(8,128)(2,1)S(1)} collective-permute-done((bf16[512,512]{1,0:T(8,128)(2,1)S(1)}, bf16[512,512]{1,0:T(8,128)(2,1)S(1)}, u32[]{:S(2)}, u32[]{:S(2)}) %collective-permute-start.3) | collective-permute-done | bytes 524320 | tf_op jit(solution)/shard_map/ppermute | solution.py:414
  132.8 2.1 %add_part.16 = (bf16[512,512]{1,0:T(8,128)(2,1)S(1)}, f32[8,128]{1,0:T(8,128)S(1)}) custom-call(s32[8]{0:T(128)S(1)} %compare_select_fusion.chunks_ref, bf16[512,512]{1,0:T(8,128)(2,1)S(1)} %collective-permute-done.3.got_ref, bf16[512,4224]{1,0:T(8,128)(2,1)} %bitcast.8.got_ref.rows_ref, bf16[512,512]{1,0:T(8,128)(2,1)S(1)} %get-tuple-element.43.high_ref.grad_ref, ...), custom_call_target="tpu_custom_call" | custom-call | flops 3449999872 | tf_op jit(solution)/shard_map/add_part/pallas_call | solution.py:441
  135.0 2.1 %add_part.17 = (bf16[512,512]{1,0:T(8,128)(2,1)S(1)}, f32[8,128]{1,0:T(8,128)S(1)}) custom-call(s32[8]{0:T(128)S(1)} %compare_select_fusion.chunks_ref, bf16[512,512]{1,0:T(8,128)(2,1)S(1)} %collective-permute-done.9.got_ref, bf16[512,4224]{1,0:T(8,128)(2,1)} %bitcast.8.got_ref.rows_ref, bf16[512,512]{1,0:T(8,128)(2,1)S(1)} %get-tuple-element.43.high_ref.grad_ref, ...), custom_call_target="tpu_custom_call" | custom-call | flops 3449999872 | tf_op jit(solution)/shard_map/add_part/pallas_call | solution.py:441
  137.1 3.5 %collective-permute-start.13 = (bf16[512,512]{1,0:T(8,128)(2,1)S(1)}, bf16[512,512]{1,0:T(8,128)(2,1)S(1)}, u32[]{:S(2)}, u32[]{:S(2)}) collective-permute-start(bf16[512,512]{1,0:T(8,128)(2,1)S(1)} %get-tuple-element.72), channel_id=1, source_target_pairs={{0,32},{32,64},{64,96},{96,128},{128,160},{160,192},{192,224},{224... | collective-permute-start | bytes 1572872 | tf_op jit(solution)/shard_map/ppermute | solution.py:414
  140.6 3.8 %collective-permute-done.8.got_ref = bf16[512,512]{1,0:T(8,128)(2,1)S(1)} collective-permute-done((bf16[512,512]{1,0:T(8,128)(2,1)S(1)}, bf16[512,512]{1,0:T(8,128)(2,1)S(1)}, u32[]{:S(2)}, u32[]{:S(2)}) %collective-permute-start.8) | collective-permute-done | bytes 524320 | tf_op jit(solution)/shard_map/ppermute | solution.py:414
  144.4 2.9 %add_part.18 = (bf16[512,512]{1,0:T(8,128)(2,1)}, f32[8,128]{1,0:T(8,128)S(1)}) custom-call(s32[8]{0:T(128)S(1)} %compare_select_fusion.chunks_ref, bf16[512,512]{1,0:T(8,128)(2,1)S(1)} %collective-permute-done.8.got_ref, bf16[512,4224]{1,0:T(8,128)(2,1)} %bitcast.8.got_ref.rows_ref, bf16[512,512]{1,0:T(8,128)(2,1)S(1)} %get-tuple-element.40.grad_ref.low_ref, ...), custom_call_target="tpu_custom_call" | custom-call | flops 34500001792 | tf_op jit(solution)/shard_map/add_part/pallas_call | solution.py:441
  147.2 3.7 %collective-permute-done.7.got_ref = bf16[512,512]{1,0:T(8,128)(2,1)S(1)} collective-permute-done((bf16[512,512]{1,0:T(8,128)(2,1)S(1)}, bf16[512,512]{1,0:T(8,128)(2,1)S(1)}, u32[]{:S(2)}, u32[]{:S(2)}) %collective-permute-start.7) | collective-permute-done | bytes 524320 | tf_op jit(solution)/shard_map/ppermute | solution.py:414
  151.0 2.8 %add_part.19 = (bf16[512,512]{1,0:T(8,128)(2,1)}, f32[8,128]{1,0:T(8,128)S(1)}) custom-call(s32[8]{0:T(128)S(1)} %compare_select_fusion.chunks_ref, bf16[512,512]{1,0:T(8,128)(2,1)S(1)} %collective-permute-done.7.got_ref, bf16[512,4224]{1,0:T(8,128)(2,1)} %bitcast.8.got_ref.rows_ref, bf16[512,512]{1,0:T(8,128)(2,1)S(1)} %get-tuple-element.43.high_ref.grad_ref, ...), custom_call_target="tpu_custom_call" | custom-call | flops 34500001792 | tf_op jit(solution)/shard_map/add_part/pallas_call | solution.py:441
  153.8 3.2 %collective-permute-start.10 = (bf16[512,512]{1,0:T(8,128)(2,1)}, bf16[512,512]{1,0:T(8,128)(2,1)}, u32[]{:S(2)}, u32[]{:S(2)}) collective-permute-start(bf16[512,512]{1,0:T(8,128)(2,1)} %get-tuple-element.69), channel_id=1, source_target_pairs={{0,32},{32,64},{64,96},{96,128},{128,160},{160,192},{192,224},{224... | collective-permute-start | bytes 1572872 | tf_op jit(solution)/shard_map/ppermute | solution.py:414
  157.8 3.3 %sum_parts.1 = (bf16[128,4096]{1,0:T(8,128)(2,1)}, f32[8,128]{1,0:T(8,128)S(1)}) custom-call(bf16[128,512]{1,0:T(8,128)(2,1)S(1)} %turn_places.1.after_ref.placed_ref, bf16[512,4096]{1,0:T(8,128)(2,1)} %bitcast.10.back_ref, f32[8,128]{1,0:T(8,128)S(1)} %get-tuple-element.67.after_ref), custom_call_target="tpu_custom_call" | custom-call | tf_op jit(solution)/shard_map/sum_parts/pallas_call | solution.py:474
  162.2 9.7 %collective-permute-done.12.high_far_ref = bf16[512,512]{1,0:T(8,128)(2,1)} collective-permute-done((bf16[512,512]{1,0:T(8,128)(2,1)}, bf16[512,512]{1,0:T(8,128)(2,1)}, u32[]{:S(2)}, u32[]{:S(2)}) %collective-permute-start.12) | collective-permute-done | bytes 524320 | tf_op jit(solution)/shard_map/ppermute | solution.py:414
  172.0 3.9 %last_add.1 = bf16[512,1024]{1,0:T(8,128)(2,1)} custom-call(s32[8]{0:T(128)S(1)} %compare_select_fusion.chunks_ref, bf16[512,512]{1,0:T(8,128)(2,1)} %collective-permute-done.10.low_far_ref, bf16[512,512]{1,0:T(8,128)(2,1)S(1)} %collective-permute-done.11.low_near_ref, bf16[512,512]{1,0:T(8,128)(2,1)} %collective-permute-done.12.high_far_ref, ...), custom_call_target="tpu_custom_call" | custom-call | flops 23000000512 | tf_op jit(solution)/shard_map/last_add/pallas_call | solution.py:488
  (18 shorter events, 4.0 us)
Async XLA Ops:
  5.5 60.5 %all-to-all-start = ((bf16[32,16,4224]{2,1,0:T(8,128)(2,1)}), bf16[32,16,4224]{2,1,0:T(8,128)(2,1)}, u32[]{:S(2)}, u32[]{:S(2)}) async-start(bf16[32,16,4224]{2,1,0:T(8,128)(2,1)} %bitcast.11), calls=%async_computation | async-start | bytes 8650752 | tf_op jit(solution)/shard_map/all_to_all | solution.py:362
  72.4 15.6 %collective-permute-start.1 = (bf16[512,512]{1,0:T(8,128)(2,1)S(1)}, bf16[512,512]{1,0:T(8,128)(2,1)S(1)}, u32[]{:S(2)}, u32[]{:S(2)}) collective-permute-start(bf16[512,512]{1,0:T(8,128)(2,1)S(1)} %get-tuple-element.47), channel_id=1, source_target_pairs={{0,32},{32,64},{64,96},{96,128},{128,160},{160,192},{192,224},{224... | collective-permute-start | bytes 1572872 | tf_op jit(solution)/shard_map/ppermute | solution.py:414
  75.6 16.1 %collective-permute-start = (bf16[512,512]{1,0:T(8,128)(2,1)S(1)}, bf16[512,512]{1,0:T(8,128)(2,1)S(1)}, u32[]{:S(2)}, u32[]{:S(2)}) collective-permute-start(bf16[512,512]{1,0:T(8,128)(2,1)S(1)} %get-tuple-element.46), channel_id=1, source_target_pairs={{0,224},{32,0},{64,32},{96,64},{128,96},{160,128},{192,160},{224,1... | collective-permute-start | bytes 1572872 | tf_op jit(solution)/shard_map/ppermute | solution.py:414
  81.4 28.2 %collective-permute-start.2 = (bf16[512,512]{1,0:T(8,128)(2,1)}, bf16[512,512]{1,0:T(8,128)(2,1)}, u32[]{:S(2)}, u32[]{:S(2)}) collective-permute-start(bf16[512,512]{1,0:T(8,128)(2,1)} %get-tuple-element.52), channel_id=1, source_target_pairs={{0,224},{32,0},{64,32},{96,64},{128,96},{160,128},{192,160},{224,1... | collective-permute-start | bytes 1572872 | tf_op jit(solution)/shard_map/ppermute | solution.py:414
  81.5 30.4 %collective-permute-start.6 = (bf16[512,512]{1,0:T(8,128)(2,1)S(1)}, bf16[512,512]{1,0:T(8,128)(2,1)S(1)}, u32[]{:S(2)}, u32[]{:S(2)}) collective-permute-start(bf16[512,512]{1,0:T(8,128)(2,1)S(1)} %get-tuple-element.48.after_ref), channel_id=1, source_target_pairs={{0,32},{32,64},{64,96},{96,128},{128,160},{160,192},{192,224},{224... | collective-permute-start | bytes 1572872 | tf_op jit(solution)/shard_map/ppermute | solution.py:414
  99.2 58.6 %all-to-all-start.1 = ((bf16[32,16,4096]{2,1,0:T(8,128)(2,1)}), bf16[32,16,4096]{2,1,0:T(8,128)(2,1)}, u32[]{:S(2)}, u32[]{:S(2)}) async-start(bf16[32,16,4096]{2,1,0:T(8,128)(2,1)} %bitcast.12), calls=%async_computation.1 | async-start | bytes 8388608 | tf_op jit(solution)/shard_map/all_to_all | solution.py:470
  106.3 21.5 %collective-permute-start.4 = (bf16[512,512]{1,0:T(8,128)(2,1)S(1)}, bf16[512,512]{1,0:T(8,128)(2,1)S(1)}, u32[]{:S(2)}, u32[]{:S(2)}) collective-permute-start(bf16[512,512]{1,0:T(8,128)(2,1)S(1)} %get-tuple-element.55), channel_id=1, source_target_pairs={{0,224},{32,0},{64,32},{96,64},{128,96},{160,128},{192,160},{224,1... | collective-permute-start | bytes 1572872 | tf_op jit(solution)/shard_map/ppermute | solution.py:414
  106.4 15.5 %collective-permute-start.5 = (bf16[512,512]{1,0:T(8,128)(2,1)S(1)}, bf16[512,512]{1,0:T(8,128)(2,1)S(1)}, u32[]{:S(2)}, u32[]{:S(2)}) collective-permute-start(bf16[512,512]{1,0:T(8,128)(2,1)S(1)} %get-tuple-element.56), channel_id=1, source_target_pairs={{0,32},{32,64},{64,96},{96,128},{128,160},{160,192},{192,224},{224... | collective-permute-start | bytes 1572872 | tf_op jit(solution)/shard_map/ppermute | solution.py:414
  111.8 21.0 %collective-permute-start.3 = (bf16[512,512]{1,0:T(8,128)(2,1)S(1)}, bf16[512,512]{1,0:T(8,128)(2,1)S(1)}, u32[]{:S(2)}, u32[]{:S(2)}) collective-permute-start(bf16[512,512]{1,0:T(8,128)(2,1)S(1)} %get-tuple-element.54), channel_id=1, source_target_pairs={{0,224},{32,0},{64,32},{96,64},{128,96},{160,128},{192,160},{224,1... | collective-permute-start | bytes 1572872 | tf_op jit(solution)/shard_map/ppermute | solution.py:414
  114.0 21.0 %collective-permute-start.9 = (bf16[512,512]{1,0:T(8,128)(2,1)S(1)}, bf16[512,512]{1,0:T(8,128)(2,1)S(1)}, u32[]{:S(2)}, u32[]{:S(2)}) collective-permute-start(bf16[512,512]{1,0:T(8,128)(2,1)S(1)} %get-tuple-element.63), channel_id=1, source_target_pairs={{0,32},{32,64},{64,96},{96,128},{128,160},{160,192},{192,224},{224... | collective-permute-start | bytes 1572872 | tf_op jit(solution)/shard_map/ppermute | solution.py:414
  124.0 20.4 %collective-permute-start.8 = (bf16[512,512]{1,0:T(8,128)(2,1)S(1)}, bf16[512,512]{1,0:T(8,128)(2,1)S(1)}, u32[]{:S(2)}, u32[]{:S(2)}) collective-permute-start(bf16[512,512]{1,0:T(8,128)(2,1)S(1)} %get-tuple-element.62), channel_id=1, source_target_pairs={{0,32},{32,64},{64,96},{96,128},{128,160},{160,192},{192,224},{224... | collective-permute-start | bytes 1572872 | tf_op jit(solution)/shard_map/ppermute | solution.py:414
  134.8 16.1 %collective-permute-start.7 = (bf16[512,512]{1,0:T(8,128)(2,1)S(1)}, bf16[512,512]{1,0:T(8,128)(2,1)S(1)}, u32[]{:S(2)}, u32[]{:S(2)}) collective-permute-start(bf16[512,512]{1,0:T(8,128)(2,1)S(1)} %get-tuple-element.61), channel_id=1, source_target_pairs={{0,224},{32,0},{64,32},{96,64},{128,96},{160,128},{192,160},{224,1... | collective-permute-start | bytes 1572872 | tf_op jit(solution)/shard_map/ppermute | solution.py:414
  134.9 27.3 %collective-permute-start.11 = (bf16[512,512]{1,0:T(8,128)(2,1)S(1)}, bf16[512,512]{1,0:T(8,128)(2,1)S(1)}, u32[]{:S(2)}, u32[]{:S(2)}) collective-permute-start(bf16[512,512]{1,0:T(8,128)(2,1)S(1)} %get-tuple-element.70), channel_id=1, source_target_pairs={{0,224},{32,0},{64,32},{96,64},{128,96},{160,128},{192,160},{224,1... | collective-permute-start | bytes 1572872 | tf_op jit(solution)/shard_map/ppermute | solution.py:414
  137.1 25.1 %collective-permute-start.13 = (bf16[512,512]{1,0:T(8,128)(2,1)S(1)}, bf16[512,512]{1,0:T(8,128)(2,1)S(1)}, u32[]{:S(2)}, u32[]{:S(2)}) collective-permute-start(bf16[512,512]{1,0:T(8,128)(2,1)S(1)} %get-tuple-element.72), channel_id=1, source_target_pairs={{0,32},{32,64},{64,96},{96,128},{128,160},{160,192},{192,224},{224... | collective-permute-start | bytes 1572872 | tf_op jit(solution)/shard_map/ppermute | solution.py:414
  153.8 18.1 %collective-permute-start.12 = (bf16[512,512]{1,0:T(8,128)(2,1)}, bf16[512,512]{1,0:T(8,128)(2,1)}, u32[]{:S(2)}, u32[]{:S(2)}) collective-permute-start(bf16[512,512]{1,0:T(8,128)(2,1)} %get-tuple-element.71), channel_id=1, source_target_pairs={{0,224},{32,0},{64,32},{96,64},{128,96},{160,128},{192,160},{224,1... | collective-permute-start | bytes 1572872 | tf_op jit(solution)/shard_map/ppermute | solution.py:414
  153.8 18.1 %collective-permute-start.10 = (bf16[512,512]{1,0:T(8,128)(2,1)}, bf16[512,512]{1,0:T(8,128)(2,1)}, u32[]{:S(2)}, u32[]{:S(2)}) collective-permute-start(bf16[512,512]{1,0:T(8,128)(2,1)} %get-tuple-element.69), channel_id=1, source_target_pairs={{0,32},{32,64},{64,96},{96,128},{128,160},{160,192},{192,224},{224... | collective-permute-start | bytes 1572872 | tf_op jit(solution)/shard_map/ppermute | solution.py:414

commit v7 on v4

--- a/solution.py
+++ b/solution.py
@@ -10,7 +10,7 @@
 BLOCK = 128
 BLK_DEV = 8
 META = 128
-GAP = 0
+GAP = 1
 STEPS = 4
 LOW_BLOCKS = 5
 MIB = 1 << 20
@@ -171,16 +171,14 @@
     rows_ref,
     meta_ref,
     low_weight,
-    high_weight,
     grad_ref,
     far_ref,
     near_ref,
     acc,
     sems,
 ):
-    steps, depth, some = low_weight.shape
+    steps, depth, _ = low_weight.shape
     weights = weight_loads(weight_ref, low_weight, sems.at[0], 0)
-    others = weight_loads(weight_ref, high_weight, sems.at[1], some)
     loads = []
     for k in range(steps):
         cut = pl.ds(k * depth, depth)
@@ -190,8 +188,6 @@
         weights[k].start()
         loads[k].start()
     last.start()
-    for other in others:
-        other.start()
 
     def ready(k):
         if k == steps:
@@ -201,14 +197,20 @@
             loads[k].wait()
 
     score_half(0, chunks_ref, rows_ref, meta_ref, low_weight, grad_ref, far_ref, near_ref, acc, ready)
-    for other in others:
-        other.wait()
-
-
-def high_kernel(base, chunks_ref, rows_ref, meta_ref, weight, grad_ref, far_ref, near_ref, acc):
-    score_half(
-        base, chunks_ref, rows_ref, meta_ref, weight, grad_ref, far_ref, near_ref, acc, lambda k: None
-    )
+
+
+def high_kernel(
+    base, chunks_ref, rows_ref, meta_ref, weight_ref, weight, grad_ref, far_ref, near_ref, acc, sems
+):
+    loads = weight_loads(weight_ref, weight, sems, base)
+    for load in loads:
+        load.start()
+
+    def ready(k):
+        if k < len(loads):
+            loads[k].wait()
+
+    score_half(base, chunks_ref, rows_ref, meta_ref, weight, grad_ref, far_ref, near_ref, acc, ready)
 
 
 def back_kernel(
@@ -371,15 +373,14 @@
     token = jax.ShapeDtypeStruct((8, 128), F32)
     depth = width // STEPS
     rest = words - base
-    rows, meta, low_weight, high_weight, low, low_far, low_near = pl.pallas_call(
+    rows, meta, low_weight, low, low_far, low_near = pl.pallas_call(
         low_kernel,
         in_specs=[smem, hbm, hbm, anywhere],
-        out_specs=[vmem] * 7,
+        out_specs=[vmem] * 6,
         out_shape=[
             like(slots, width),
             like(slots, META),
             like(STEPS, depth, base),
-            like(STEPS, depth, rest),
             like(slots, base),
             like(chunk, base),
             like(chunk, base),
@@ -389,16 +390,16 @@
         cost_estimate=cost(0),
         name="low_scores",
     )(chunks, got, weights, placed)
-    high, high_far, high_near = pl.pallas_call(
+    high_weight, high, high_far, high_near = pl.pallas_call(
         functools.partial(high_kernel, base),
-        in_specs=[smem, vmem, vmem, vmem],
-        out_specs=[vmem] * 3,
-        out_shape=[like(slots, rest), like(chunk, rest), like(chunk, rest)],
-        scratch_shapes=[pltpu.VMEM((slots, rest), F32)],
+        in_specs=[smem, vmem, vmem, hbm],
+        out_specs=[vmem] * 4,
+        out_shape=[like(STEPS, depth, rest), like(slots, rest), like(chunk, rest), like(chunk, rest)],
+        scratch_shapes=[pltpu.VMEM((slots, rest), F32), pltpu.SemaphoreType.DMA((STEPS,))],
         compiler_params=params(16),
         cost_estimate=cost(HIGH_US),
         name="high_scores",
-    )(chunks, rows, meta, high_weight)
+    )(chunks, rows, meta, weights)
 
     def hop(x, d):
         return lax.ppermute(x, "dp", [(i, (i + d) % planes) for i in range(planes)])

time: 175 us -> 181 us (1.034)
  waiting for transfers between devices: 78.3 us -> 81.5 us
    ppermute x14, waiting for transfers between devices: 25.6 us -> 28.8 us  [hop(): return lax.ppermute(x, 'dp', [(i, (i + d) % planes) for i in range(planes)])]
    pallas_call x1, Pallas kernels: 3.71 us -> 5.55 us  [body(): pl.pallas_call(functools.partial(high_kernel, base), in_specs=[smem, vmem...]
  transfers between devices with their start and end apart: 16 -> 16, of which waited for: 8 -> 8; matrix products, arithmetic and copies ran while one was open for 0% -> 0% of each run, Pallas kernels for 22% -> 23%
where the time goes in v7:
time: 181 us; the launch traced here: 180 us
  waiting for transfers between devices  81.5 us (45%)
  Pallas kernels  57.3 us (32%)
  starting transfers between devices  39.1 us (22%)
    all_to_all x1, waiting for transfers between devices, body(): lax.all_to_all(send.reshape(peers, capacity, sent), 'vocab', split_axis=0...  52.7 us
    ppermute x14, waiting for transfers between devices, hop(): return lax.ppermute(x, 'dp', [(i, (i + d) % planes) for i in range(planes)])  28.8 us
    ppermute x14, starting transfers between devices, hop(): return lax.ppermute(x, 'dp', [(i, (i + d) % planes) for i in range(planes)])  24.6 us
    pallas_call x10, Pallas kernels, add(): pl.pallas_call(add_kernel, grid_spec=pltpu.PrefetchScalarGridSpec(num_sca...  23.3 us
    pallas_call x1, Pallas kernels, body(): pl.pallas_call(low_kernel, in_specs=[smem, hbm, hbm, anywhere], out_specs...  9.24 us
    all_to_all x1, starting transfers between devices, body(): lax.all_to_all(send.reshape(peers, capacity, sent), 'vocab', split_axis=0...  7.68 us
    all_to_all x1, starting transfers between devices, body(): lax.all_to_all(part.reshape(peers, capacity, width), 'vocab', split_axis=...  6.88 us
    pallas_call x1, Pallas kernels, state_parts(): pl.pallas_call(back_kernel, in_specs=[vmem, vmem, vmem, vmem, anywhere],...  6.55 us
  transfers between devices with their start and end apart: 16, of which 8 were waited for; matrix products, arithmetic and copies ran while one was open for 0% of the time, Pallas kernels for 23%

profile of v7, /device:TPU:98, one launch (start us, length us, event | category | flops | bytes accessed | tf_op | source)
XLA Modules:
  0.0 180.1 jit_solution(9907754477459872885)
XLA Ops:
  0.6 4.8 %place_rows.1 = (bf16[512,4224]{1,0:T(8,128)(2,1)}, bf16[512,128]{1,0:T(8,128)(2,1)S(1)}) custom-call(bf16[128,4096]{1,0:T(8,128)(2,1)} %hidden_ref.1, s32[3,128]{1,0:T(4,128)} %bitcast.15, s32[3,2,128]{2,1,0:T(2,128)} %bitcast.13, s32[3,2,128]{2,1,0:T(2,128)} %bitcast.14, s32[1,128]{1,0:T(1,128)} %bitcast.16, s32[1,128]{1,0:T(1,128)} %bitcast.17, ...), custom_call_target="tpu_custom_call" | custom-call | tf_op jit(solution)/shard_map/place_rows/pallas_call | solution.py:335
  5.4 7.7 %all-to-all-start = ((bf16[32,16,4224]{2,1,0:T(8,128)(2,1)}), bf16[32,16,4224]{2,1,0:T(8,128)(2,1)}, u32[]{:S(2)}, u32[]{:S(2)}) async-start(bf16[32,16,4224]{2,1,0:T(8,128)(2,1)} %bitcast.11), calls=%async_computation | async-start | bytes 8650752 | tf_op jit(solution)/shard_map/all_to_all | solution.py:353
  13.2 52.7 %all-to-all-done = bf16[32,16,4224]{2,1,0:T(8,128)(2,1)} async-done(((bf16[32,16,4224]{2,1,0:T(8,128)(2,1)}), bf16[32,16,4224]{2,1,0:T(8,128)(2,1)}, u32[]{:S(2)}, u32[]{:S(2)}) %all-to-all-start) | async-done | bytes 4325408 | tf_op jit(solution)/shard_map/all_to_all | solution.py:353
  65.9 9.2 %low_scores.1 = (bf16[512,4096]{1,0:T(8,128)(2,1)S(1)}, bf16[512,128]{1,0:T(8,128)(2,1)S(1)}, bf16[4,1024,640]{2,1,0:T(8,128)(2,1)S(1)}, bf16[512,640]{1,0:T(8,1...) custom-call(s32[8]{0:T(128)S(1)} %compare_select_fusion.chunks_ref, ...), custom_call_target="tpu_custom_call" | custom-call | tf_op jit(solution)/shard_map/low_scores/pallas_call | solution.py:376
  75.2 3.2 %collective-permute-start = (bf16[512,640]{1,0:T(8,128)(2,1)S(1)}, bf16[512,640]{1,0:T(8,128)(2,1)S(1)}, u32[]{:S(2)}, u32[]{:S(2)}) collective-permute-start(bf16[512,640]{1,0:T(8,128)(2,1)S(1)} %get-tuple-element.48), channel_id=1, source_target_pairs={{0,32},{32,64},{64,96},{96,128},{128,160},{160,192},{192,224},{224... | collective-permute-start | bytes 1966088 | tf_op jit(solution)/shard_map/ppermute | solution.py:405
  78.4 5.5 %high_scores.1 = (bf16[4,1024,384]{2,1,0:T(8,128)(2,1)S(1)}, bf16[512,384]{1,0:T(8,128)(2,1)S(1)}, bf16[512,384]{1,0:T(8,128)(2,1)}, bf16[512,384]{1,0:T(8,128)(2,1)S(1)}) custom-call(s32[8]{0:T(128)S(1)} %compare_select_fusion.chunks_ref, bf16[512,4096]{1,0:T(8,128)(2,1)S(1)} %get-tuple-element.43.rows_ref, ...), custom_call_target="tpu_custom_call" | custom-call | tf_op jit(solution)/shard_map/high_scores/pallas_call | solution.py:393
  84.1 3.5 %collective-permute-start.4 = (bf16[512,384]{1,0:T(8,128)(2,1)S(1)}, bf16[512,384]{1,0:T(8,128)(2,1)}, u32[]{:S(2)}, u32[]{:S(2)}) collective-permute-start(bf16[512,384]{1,0:T(8,128)(2,1)S(1)} %get-tuple-element.49.after_ref), channel_id=1, source_target_pairs={{0,32},{32,64},{64,96},{96,128},{128,160},{160,192},{192,224},{224... | collective-permute-start | bytes 1179656 | tf_op jit(solution)/shard_map/ppermute | solution.py:405
  87.5 6.0 %collective-permute-done.got_ref = bf16[512,640]{1,0:T(8,128)(2,1)S(1)} collective-permute-done((bf16[512,640]{1,0:T(8,128)(2,1)S(1)}, bf16[512,640]{1,0:T(8,128)(2,1)S(1)}, u32[]{:S(2)}, u32[]{:S(2)}) %collective-permute-start) | collective-permute-done | bytes 655392 | tf_op jit(solution)/shard_map/ppermute | solution.py:405
  93.6 2.2 %add_part.10 = (bf16[512,640]{1,0:T(8,128)(2,1)S(1)}, f32[8,128]{1,0:T(8,128)S(1)}) custom-call(s32[8]{0:T(128)S(1)} %compare_select_fusion.chunks_ref, bf16[512,640]{1,0:T(8,128)(2,1)S(1)} %collective-permute-done.got_ref, bf16[512,4224]{1,0:T(8,128)(2,1)} %bitcast.8.got_ref.rows_ref, bf16[512,640]{1,0:T(8,128)(2,1)S(1)} %get-tuple-element.42.grad_ref.low_ref, ...), custom_call_target="tpu_custom_call" | custom-call | flops 3449999872 | tf_op jit(solution)/shard_map/add_part/pallas_call | solution.py:432
  95.8 6.6 %state_parts.1 = (bf16[512,4096]{1,0:T(8,128)(2,1)}, f32[8,128]{1,0:T(8,128)S(1)}) custom-call(bf16[512,640]{1,0:T(8,128)(2,1)S(1)} %get-tuple-element.42.grad_ref.low_ref, bf16[512,384]{1,0:T(8,128)(2,1)S(1)} %get-tuple-element.45.high_ref.grad_ref, bf16[4,1024,640]{2,1,0:T(8,128)(2,1)S(1)} %get-tuple-element.46.low_weight, ...), custom_call_target="tpu_custom_call" | custom-call | tf_op jit(solution)/shard_map/state_parts/pallas_call | solution.py:416
  102.3 6.9 %all-to-all-start.1 = ((bf16[32,16,4096]{2,1,0:T(8,128)(2,1)}), bf16[32,16,4096]{2,1,0:T(8,128)(2,1)}, u32[]{:S(2)}, u32[]{:S(2)}) async-start(bf16[32,16,4096]{2,1,0:T(8,128)(2,1)} %bitcast.12), calls=%async_computation.1 | async-start | bytes 8388608 | tf_op jit(solution)/shard_map/all_to_all | solution.py:461
  109.2 3.8 %collective-permute-start.3 = (bf16[512,640]{1,0:T(8,128)(2,1)S(1)}, bf16[512,640]{1,0:T(8,128)(2,1)S(1)}, u32[]{:S(2)}, u32[]{:S(2)}) collective-permute-start(bf16[512,640]{1,0:T(8,128)(2,1)S(1)} %get-tuple-element.55), channel_id=1, source_target_pairs={{0,32},{32,64},{64,96},{96,128},{128,160},{160,192},{192,224},{224... | collective-permute-start | bytes 1966088 | tf_op jit(solution)/shard_map/ppermute | solution.py:405
  113.0 2.4 %add_part.11 = (bf16[512,640]{1,0:T(8,128)(2,1)S(1)}, f32[8,128]{1,0:T(8,128)S(1)}) custom-call(s32[8]{0:T(128)S(1)} %compare_select_fusion.chunks_ref, bf16[512,640]{1,0:T(8,128)(2,1)} %collective-permute-done.1.got_ref, bf16[512,4224]{1,0:T(8,128)(2,1)} %bitcast.8.got_ref.rows_ref, bf16[512,640]{1,0:T(8,128)(2,1)S(1)} %get-tuple-element.42.grad_ref.low_ref, ...), custom_call_target="tpu_custom_call" | custom-call | flops 3449999872 | tf_op jit(solution)/shard_map/add_part/pallas_call | solution.py:432
  115.5 2.2 %add_part.12 = (bf16[512,384]{1,0:T(8,128)(2,1)S(1)}, f32[8,128]{1,0:T(8,128)S(1)}) custom-call(s32[8]{0:T(128)S(1)} %compare_select_fusion.chunks_ref, bf16[512,384]{1,0:T(8,128)(2,1)} %collective-permute-done.5.got_ref, bf16[512,4224]{1,0:T(8,128)(2,1)} %bitcast.8.got_ref.rows_ref, bf16[512,384]{1,0:T(8,128)(2,1)S(1)} %get-tuple-element.45.high_ref.grad_ref, ...), custom_call_target="tpu_custom_call" | custom-call | flops 3449999872 | tf_op jit(solution)/shard_map/add_part/pallas_call | solution.py:432
  117.7 2.2 %add_part.13 = (bf16[512,384]{1,0:T(8,128)(2,1)S(1)}, f32[8,128]{1,0:T(8,128)S(1)}) custom-call(s32[8]{0:T(128)S(1)} %compare_select_fusion.chunks_ref, bf16[512,384]{1,0:T(8,128)(2,1)} %collective-permute-done.4.got_ref, bf16[512,4224]{1,0:T(8,128)(2,1)} %bitcast.8.got_ref.rows_ref, bf16[512,384]{1,0:T(8,128)(2,1)S(1)} %get-tuple-element.45.high_ref.grad_ref, ...), custom_call_target="tpu_custom_call" | custom-call | flops 3449999872 | tf_op jit(solution)/shard_map/add_part/pallas_call | solution.py:432
  119.8 3.3 %collective-permute-start.7 = (bf16[512,384]{1,0:T(8,128)(2,1)S(1)}, bf16[512,384]{1,0:T(8,128)(2,1)S(1)}, u32[]{:S(2)}, u32[]{:S(2)}) collective-permute-start(bf16[512,384]{1,0:T(8,128)(2,1)S(1)} %get-tuple-element.62), channel_id=1, source_target_pairs={{0,32},{32,64},{64,96},{96,128},{128,160},{160,192},{192,224},{224... | collective-permute-start | bytes 1179656 | tf_op jit(solution)/shard_map/ppermute | solution.py:405
  123.1 4.9 %collective-permute-done.3.got_ref = bf16[512,640]{1,0:T(8,128)(2,1)S(1)} collective-permute-done((bf16[512,640]{1,0:T(8,128)(2,1)S(1)}, bf16[512,640]{1,0:T(8,128)(2,1)S(1)}, u32[]{:S(2)}, u32[]{:S(2)}) %collective-permute-start.3) | collective-permute-done | bytes 655392 | tf_op jit(solution)/shard_map/ppermute | solution.py:405
  128.1 2.2 %add_part.14 = (bf16[512,640]{1,0:T(8,128)(2,1)S(1)}, f32[8,128]{1,0:T(8,128)S(1)}) custom-call(s32[8]{0:T(128)S(1)} %compare_select_fusion.chunks_ref, bf16[512,640]{1,0:T(8,128)(2,1)S(1)} %collective-permute-done.3.got_ref, bf16[512,4224]{1,0:T(8,128)(2,1)} %bitcast.8.got_ref.rows_ref, bf16[512,640]{1,0:T(8,128)(2,1)S(1)} %get-tuple-element.42.grad_ref.low_ref, ...), custom_call_target="tpu_custom_call" | custom-call | flops 3449999872 | tf_op jit(solution)/shard_map/add_part/pallas_call | solution.py:432
  130.3 3.8 %collective-permute-start.11 = (bf16[512,640]{1,0:T(8,128)(2,1)S(1)}, bf16[512,640]{1,0:T(8,128)(2,1)S(1)}, u32[]{:S(2)}, u32[]{:S(2)}) collective-permute-start(bf16[512,640]{1,0:T(8,128)(2,1)S(1)} %get-tuple-element.68), channel_id=1, source_target_pairs={{0,32},{32,64},{64,96},{96,128},{128,160},{160,192},{192,224},{224... | collective-permute-start | bytes 1966088 | tf_op jit(solution)/shard_map/ppermute | solution.py:405
  134.3 2.2 %add_part.15 = (bf16[512,640]{1,0:T(8,128)(2,1)S(1)}, f32[8,128]{1,0:T(8,128)S(1)}) custom-call(s32[8]{0:T(128)S(1)} %compare_select_fusion.chunks_ref, bf16[512,640]{1,0:T(8,128)(2,1)S(1)} %collective-permute-done.2.got_ref, bf16[512,4224]{1,0:T(8,128)(2,1)} %bitcast.8.got_ref.rows_ref, bf16[512,640]{1,0:T(8,128)(2,1)S(1)} %get-tuple-element.42.grad_ref.low_ref, ...), custom_call_target="tpu_custom_call" | custom-call | flops 3449999872 | tf_op jit(solution)/shard_map/add_part/pallas_call | solution.py:432
  136.5 5.1 %collective-permute-done.8.got_ref = bf16[512,384]{1,0:T(8,128)(2,1)S(1)} collective-permute-done((bf16[512,384]{1,0:T(8,128)(2,1)S(1)}, bf16[512,384]{1,0:T(8,128)(2,1)S(1)}, u32[]{:S(2)}, u32[]{:S(2)}) %collective-permute-start.8) | collective-permute-done | bytes 393248 | tf_op jit(solution)/shard_map/ppermute | solution.py:405
  141.6 2.1 %add_part.16 = (bf16[512,384]{1,0:T(8,128)(2,1)S(1)}, f32[8,128]{1,0:T(8,128)S(1)}) custom-call(s32[8]{0:T(128)S(1)} %compare_select_fusion.chunks_ref, bf16[512,384]{1,0:T(8,128)(2,1)S(1)} %collective-permute-done.8.got_ref, bf16[512,4224]{1,0:T(8,128)(2,1)} %bitcast.8.got_ref.rows_ref, bf16[512,384]{1,0:T(8,128)(2,1)S(1)} %get-tuple-element.45.high_ref.grad_ref, ...), custom_call_target="tpu_custom_call" | custom-call | flops 3449999872 | tf_op jit(solution)/shard_map/add_part/pallas_call | solution.py:432
  144.1 2.1 %add_part.17 = (bf16[512,384]{1,0:T(8,128)(2,1)S(1)}, f32[8,128]{1,0:T(8,128)S(1)}) custom-call(s32[8]{0:T(128)S(1)} %compare_select_fusion.chunks_ref, bf16[512,384]{1,0:T(8,128)(2,1)S(1)} %collective-permute-done.7.got_ref, bf16[512,4224]{1,0:T(8,128)(2,1)} %bitcast.8.got_ref.rows_ref, bf16[512,384]{1,0:T(8,128)(2,1)S(1)} %get-tuple-element.45.high_ref.grad_ref, ...), custom_call_target="tpu_custom_call" | custom-call | flops 3449999872 | tf_op jit(solution)/shard_map/add_part/pallas_call | solution.py:432
  146.1 3.3 %collective-permute-start.9 = (bf16[512,384]{1,0:T(8,128)(2,1)S(1)}, bf16[512,384]{1,0:T(8,128)(2,1)S(1)}, u32[]{:S(2)}, u32[]{:S(2)}) collective-permute-start(bf16[512,384]{1,0:T(8,128)(2,1)S(1)} %get-tuple-element.66), channel_id=1, source_target_pairs={{0,32},{32,64},{64,96},{96,128},{128,160},{160,192},{192,224},{224... | collective-permute-start | bytes 1179656 | tf_op jit(solution)/shard_map/ppermute | solution.py:405
  150.5 3.0 %add_part.18 = (bf16[512,640]{1,0:T(8,128)(2,1)}, f32[8,128]{1,0:T(8,128)S(1)}) custom-call(s32[8]{0:T(128)S(1)} %compare_select_fusion.chunks_ref, bf16[512,640]{1,0:T(8,128)(2,1)S(1)} %collective-permute-done.11.got_ref, bf16[512,4224]{1,0:T(8,128)(2,1)} %bitcast.8.got_ref.rows_ref, bf16[512,640]{1,0:T(8,128)(2,1)S(1)} %get-tuple-element.42.grad_ref.low_ref, ...), custom_call_target="tpu_custom_call" | custom-call | flops 3449999872 | tf_op jit(solution)/shard_map/add_part/pallas_call | solution.py:432
  153.6 3.4 %collective-permute-done.10.got_ref = bf16[512,384]{1,0:T(8,128)(2,1)S(1)} collective-permute-done((bf16[512,384]{1,0:T(8,128)(2,1)S(1)}, bf16[512,384]{1,0:T(8,128)(2,1)S(1)}, u32[]{:S(2)}, u32[]{:S(2)}) %collective-permute-start.10) | collective-permute-done | bytes 393248 | tf_op jit(solution)/shard_map/ppermute | solution.py:405
  157.0 2.8 %add_part.19 = (bf16[512,384]{1,0:T(8,128)(2,1)}, f32[8,128]{1,0:T(8,128)S(1)}) custom-call(s32[8]{0:T(128)S(1)} %compare_select_fusion.chunks_ref, bf16[512,384]{1,0:T(8,128)(2,1)S(1)} %collective-permute-done.10.got_ref, bf16[512,4224]{1,0:T(8,128)(2,1)} %bitcast.8.got_ref.rows_ref, bf16[512,384]{1,0:T(8,128)(2,1)S(1)} %get-tuple-element.45.high_ref.grad_ref, ...), custom_call_target="tpu_custom_call" | custom-call | flops 3449999872 | tf_op jit(solution)/shard_map/add_part/pallas_call | solution.py:432
  159.8 3.2 %collective-permute-start.12 = (bf16[512,640]{1,0:T(8,128)(2,1)}, bf16[512,640]{1,0:T(8,128)(2,1)S(1)}, u32[]{:S(2)}, u32[]{:S(2)}) collective-permute-start(bf16[512,640]{1,0:T(8,128)(2,1)} %get-tuple-element.74), channel_id=1, source_target_pairs={{0,32},{32,64},{64,96},{96,128},{128,160},{160,192},{192,224},{224... | collective-permute-start | bytes 1966088 | tf_op jit(solution)/shard_map/ppermute | solution.py:405
  163.1 8.0 %collective-permute-done.6.low_near_ref = bf16[512,640]{1,0:T(8,128)(2,1)S(1)} collective-permute-done((bf16[512,640]{1,0:T(8,128)(2,1)S(1)}, bf16[512,640]{1,0:T(8,128)(2,1)S(1)}, u32[]{:S(2)}, u32[]{:S(2)}) %collective-permute-start.6) | collective-permute-done | bytes 655392 | tf_op jit(solution)/shard_map/ppermute | solution.py:405
  172.0 2.5 %own_part.1 = (f32[512,1024]{1,0:T(8,128)S(1)}, f32[8,128]{1,0:T(8,128)S(1)}) custom-call(s32[8]{0:T(128)S(1)} %compare_select_fusion.chunks_ref, bf16[512,640]{1,0:T(8,128)(2,1)S(1)} %collective-permute-done.6.low_near_ref, bf16[512,384]{1,0:T(8,128)(2,1)S(1)} %collective-permute-done.9.high_near_ref, bf16[512,4224]{1,0:T(8,128)(2,1)} %bitcast.8.got_ref.rows_ref, ...), custom_call_target="tpu_custom_call" | custom-call | flops 115000000512 | tf_op jit(solution)/shard_map/own_part/pallas_call | solution.py:465
  174.5 3.3 %sum_parts.1 = (bf16[128,4096]{1,0:T(8,128)(2,1)}, f32[8,128]{1,0:T(8,128)S(1)}) custom-call(bf16[128,512]{1,0:T(8,128)(2,1)S(1)} %copy-done.1, bf16[512,4096]{1,0:T(8,128)(2,1)} %bitcast.10.back_ref, f32[8,128]{1,0:T(8,128)S(1)} %get-tuple-element.72.after_ref), custom_call_target="tpu_custom_call" | custom-call | tf_op jit(solution)/shard_map/sum_parts/pallas_call | solution.py:485
  177.8 2.1 %last_add.1 = bf16[512,1024]{1,0:T(8,128)(2,1)} custom-call(bf16[512,640]{1,0:T(8,128)(2,1)S(1)} %collective-permute-done.12.low_far_ref, bf16[512,384]{1,0:T(8,128)(2,1)} %collective-permute-done.13.high_far_ref, f32[512,1024]{1,0:T(8,128)S(1)} %get-tuple-element.76.own_ref, f32[8,128]{1,0:T(8,128)S(1)} %get-tuple-element.77.after_ref), custom_call_target="tpu_custom_call" | custom-call | tf_op jit(solution)/shard_map/last_add/pallas_call | solution.py:499
  (27 shorter events, 3.0 us)
Async XLA Ops:
  5.4 60.5 %all-to-all-start = ((bf16[32,16,4224]{2,1,0:T(8,128)(2,1)}), bf16[32,16,4224]{2,1,0:T(8,128)(2,1)}, u32[]{:S(2)}, u32[]{:S(2)}) async-start(bf16[32,16,4224]{2,1,0:T(8,128)(2,1)} %bitcast.11), calls=%async_computation | async-start | bytes 8650752 | tf_op jit(solution)/shard_map/all_to_all | solution.py:353
  13.2 62.0 %copy-start = (bf16[128,512]{1,0:T(8,128)(2,1)}, bf16[128,512]{1,0:T(8,128)(2,1)S(1)}, u32[]{:S(2)}) copy-start(bf16[128,512]{1,0:T(8,128)(2,1)S(1)} %turn_places.1.after_ref.placed_ref) | copy-start | bytes 393220
  75.2 18.4 %collective-permute-start = (bf16[512,640]{1,0:T(8,128)(2,1)S(1)}, bf16[512,640]{1,0:T(8,128)(2,1)S(1)}, u32[]{:S(2)}, u32[]{:S(2)}) collective-permute-start(bf16[512,640]{1,0:T(8,128)(2,1)S(1)} %get-tuple-element.48), channel_id=1, source_target_pairs={{0,32},{32,64},{64,96},{96,128},{128,160},{160,192},{192,224},{224... | collective-permute-start | bytes 1966088 | tf_op jit(solution)/shard_map/ppermute | solution.py:405
  78.4 34.6 %collective-permute-start.1 = (bf16[512,640]{1,0:T(8,128)(2,1)S(1)}, bf16[512,640]{1,0:T(8,128)(2,1)}, u32[]{:S(2)}, u32[]{:S(2)}) collective-permute-start(bf16[512,640]{1,0:T(8,128)(2,1)S(1)} %get-tuple-element.52), channel_id=1, source_target_pairs={{0,224},{32,0},{64,32},{96,64},{128,96},{160,128},{192,160},{224,1... | collective-permute-start | bytes 1966088 | tf_op jit(solution)/shard_map/ppermute | solution.py:405
  83.9 73.0 %copy-start.2 = (bf16[512,384]{1,0:T(8,128)(2,1)}, bf16[512,384]{1,0:T(8,128)(2,1)S(1)}, u32[]{:S(2)}) copy-start(bf16[512,384]{1,0:T(8,128)(2,1)S(1)} %get-tuple-element.45.high_ref.grad_ref) | copy-start | bytes 1179652
  84.0 31.5 %collective-permute-start.5 = (bf16[512,384]{1,0:T(8,128)(2,1)}, bf16[512,384]{1,0:T(8,128)(2,1)}, u32[]{:S(2)}, u32[]{:S(2)}) collective-permute-start(bf16[512,384]{1,0:T(8,128)(2,1)} %get-tuple-element.56), channel_id=1, source_target_pairs={{0,224},{32,0},{64,32},{96,64},{128,96},{160,128},{192,160},{224,1... | collective-permute-start | bytes 1179656 | tf_op jit(solution)/shard_map/ppermute | solution.py:405
  84.1 33.6 %collective-permute-start.4 = (bf16[512,384]{1,0:T(8,128)(2,1)S(1)}, bf16[512,384]{1,0:T(8,128)(2,1)}, u32[]{:S(2)}, u32[]{:S(2)}) collective-permute-start(bf16[512,384]{1,0:T(8,128)(2,1)S(1)} %get-tuple-element.49.after_ref), channel_id=1, source_target_pairs={{0,32},{32,64},{64,96},{96,128},{128,160},{160,192},{192,224},{224... | collective-permute-start | bytes 1179656 | tf_op jit(solution)/shard_map/ppermute | solution.py:405
  102.3 72.2 %all-to-all-start.1 = ((bf16[32,16,4096]{2,1,0:T(8,128)(2,1)}), bf16[32,16,4096]{2,1,0:T(8,128)(2,1)}, u32[]{:S(2)}, u32[]{:S(2)}) async-start(bf16[32,16,4096]{2,1,0:T(8,128)(2,1)} %bitcast.12), calls=%async_computation.1 | async-start | bytes 8388608 | tf_op jit(solution)/shard_map/all_to_all | solution.py:461
  109.2 18.9 %collective-permute-start.3 = (bf16[512,640]{1,0:T(8,128)(2,1)S(1)}, bf16[512,640]{1,0:T(8,128)(2,1)S(1)}, u32[]{:S(2)}, u32[]{:S(2)}) collective-permute-start(bf16[512,640]{1,0:T(8,128)(2,1)S(1)} %get-tuple-element.55), channel_id=1, source_target_pairs={{0,32},{32,64},{64,96},{96,128},{128,160},{160,192},{192,224},{224... | collective-permute-start | bytes 1966088 | tf_op jit(solution)/shard_map/ppermute | solution.py:405
  115.4 18.9 %collective-permute-start.2 = (bf16[512,640]{1,0:T(8,128)(2,1)S(1)}, bf16[512,640]{1,0:T(8,128)(2,1)S(1)}, u32[]{:S(2)}, u32[]{:S(2)}) collective-permute-start(bf16[512,640]{1,0:T(8,128)(2,1)S(1)} %get-tuple-element.54), channel_id=1, source_target_pairs={{0,224},{32,0},{64,32},{96,64},{128,96},{160,128},{192,160},{224,1... | collective-permute-start | bytes 1966088 | tf_op jit(solution)/shard_map/ppermute | solution.py:405
  119.8 24.2 %collective-permute-start.7 = (bf16[512,384]{1,0:T(8,128)(2,1)S(1)}, bf16[512,384]{1,0:T(8,128)(2,1)S(1)}, u32[]{:S(2)}, u32[]{:S(2)}) collective-permute-start(bf16[512,384]{1,0:T(8,128)(2,1)S(1)} %get-tuple-element.62), channel_id=1, source_target_pairs={{0,32},{32,64},{64,96},{96,128},{128,160},{160,192},{192,224},{224... | collective-permute-start | bytes 1179656 | tf_op jit(solution)/shard_map/ppermute | solution.py:405
  123.1 18.5 %collective-permute-start.8 = (bf16[512,384]{1,0:T(8,128)(2,1)S(1)}, bf16[512,384]{1,0:T(8,128)(2,1)S(1)}, u32[]{:S(2)}, u32[]{:S(2)}) collective-permute-start(bf16[512,384]{1,0:T(8,128)(2,1)S(1)} %get-tuple-element.63), channel_id=1, source_target_pairs={{0,224},{32,0},{64,32},{96,64},{128,96},{160,128},{192,160},{224,1... | collective-permute-start | bytes 1179656 | tf_op jit(solution)/shard_map/ppermute | solution.py:405
  130.3 20.3 %collective-permute-start.11 = (bf16[512,640]{1,0:T(8,128)(2,1)S(1)}, bf16[512,640]{1,0:T(8,128)(2,1)S(1)}, u32[]{:S(2)}, u32[]{:S(2)}) collective-permute-start(bf16[512,640]{1,0:T(8,128)(2,1)S(1)} %get-tuple-element.68), channel_id=1, source_target_pairs={{0,32},{32,64},{64,96},{96,128},{128,160},{160,192},{192,224},{224... | collective-permute-start | bytes 1966088 | tf_op jit(solution)/shard_map/ppermute | solution.py:405
  143.6 13.3 %collective-permute-start.10 = (bf16[512,384]{1,0:T(8,128)(2,1)S(1)}, bf16[512,384]{1,0:T(8,128)(2,1)S(1)}, u32[]{:S(2)}, u32[]{:S(2)}) collective-permute-start(bf16[512,384]{1,0:T(8,128)(2,1)S(1)} %get-tuple-element.67), channel_id=1, source_target_pairs={{0,224},{32,0},{64,32},{96,64},{128,96},{160,128},{192,160},{224,1... | collective-permute-start | bytes 1179656 | tf_op jit(solution)/shard_map/ppermute | solution.py:405
  143.7 27.3 %collective-permute-start.6 = (bf16[512,640]{1,0:T(8,128)(2,1)S(1)}, bf16[512,640]{1,0:T(8,128)(2,1)S(1)}, u32[]{:S(2)}, u32[]{:S(2)}) collective-permute-start(bf16[512,640]{1,0:T(8,128)(2,1)S(1)} %get-tuple-element.61), channel_id=1, source_target_pairs={{0,224},{32,0},{64,32},{96,64},{128,96},{160,128},{192,160},{224,1... | collective-permute-start | bytes 1966088 | tf_op jit(solution)/shard_map/ppermute | solution.py:405
  146.1 16.9 %collective-permute-start.9 = (bf16[512,384]{1,0:T(8,128)(2,1)S(1)}, bf16[512,384]{1,0:T(8,128)(2,1)S(1)}, u32[]{:S(2)}, u32[]{:S(2)}) collective-permute-start(bf16[512,384]{1,0:T(8,128)(2,1)S(1)} %get-tuple-element.66), channel_id=1, source_target_pairs={{0,32},{32,64},{64,96},{96,128},{128,160},{160,192},{192,224},{224... | collective-permute-start | bytes 1179656 | tf_op jit(solution)/shard_map/ppermute | solution.py:405
  159.8 18.0 %collective-permute-start.13 = (bf16[512,384]{1,0:T(8,128)(2,1)}, bf16[512,384]{1,0:T(8,128)(2,1)}, u32[]{:S(2)}, u32[]{:S(2)}) collective-permute-start(bf16[512,384]{1,0:T(8,128)(2,1)} %get-tuple-element.75), channel_id=1, source_target_pairs={{0,224},{32,0},{64,32},{96,64},{128,96},{160,128},{192,160},{224,1... | collective-permute-start | bytes 1179656 | tf_op jit(solution)/shard_map/ppermute | solution.py:405
  159.8 18.0 %collective-permute-start.12 = (bf16[512,640]{1,0:T(8,128)(2,1)}, bf16[512,640]{1,0:T(8,128)(2,1)S(1)}, u32[]{:S(2)}, u32[]{:S(2)}) collective-permute-start(bf16[512,640]{1,0:T(8,128)(2,1)} %get-tuple-element.74), channel_id=1, source_target_pairs={{0,32},{32,64},{64,96},{96,128},{128,160},{160,192},{192,224},{224... | collective-permute-start | bytes 1966088 | tf_op jit(solution)/shard_map/ppermute | solution.py:405
  171.0 1.0 copy-start.3
  172.0 2.5 %copy-start.1 = (bf16[128,512]{1,0:T(8,128)(2,1)S(1)}, bf16[128,512]{1,0:T(8,128)(2,1)}, u32[]{:S(2)}) copy-start(bf16[128,512]{1,0:T(8,128)(2,1)} %copy-done) | copy-start | bytes 393220

commit v8 on v3

--- a/solution.py
+++ b/solution.py
@@ -242,15 +242,38 @@
         out_ref[:, k * half : (k + 1) * half] = near_ref[...].astype(F32) + own
 
 
-def last_kernel(low_far_ref, high_far_ref, own_ref, after_ref, out_ref):
-    half = low_far_ref.shape[1]
-    for k, far_ref in enumerate((low_far_ref, high_far_ref)):
-        cut = slice(k * half, (k + 1) * half)
-        out_ref[:, cut] = (own_ref[:, cut] + far_ref[...].astype(F32)).astype(BF16)
-
-
-def sum_kernel(placed_ref, back_ref, after_ref, out_ref, token_ref):
-    out_ref[...] = jnp.dot(placed_ref[...], back_ref[...], preferred_element_type=F32).astype(BF16)
+def last_kernel(low_far_ref, high_far_ref, own_ref, after_ref, out_ref, out, sems):
+    pieces = sems.shape[0]
+    piece = out.shape[0] // pieces
+    base = low_far_ref.shape[1]
+    stores = []
+    for k in range(pieces):
+        rows = slice(k * piece, (k + 1) * piece)
+        out[rows, :base] = (own_ref[rows, :base] + low_far_ref[rows, :].astype(F32)).astype(BF16)
+        out[rows, base:] = (own_ref[rows, base:] + high_far_ref[rows, :].astype(F32)).astype(BF16)
+        cut = pl.ds(k * piece, piece)
+        stores.append(pltpu.make_async_copy(out.at[cut, :], out_ref.at[cut, :], sems.at[k]))
+        stores[k].start()
+    for store in stores:
+        store.wait()
+
+
+def sum_kernel(placed_ref, back_ref, after_ref, out_ref, token_ref, back, out, sems):
+    pieces = sems.shape[1]
+    piece = back.shape[1] // pieces
+    loads, stores = [], []
+    for k in range(pieces):
+        cut = pl.ds(k * piece, piece)
+        loads.append(pltpu.make_async_copy(back_ref.at[:, cut], back.at[:, cut], sems.at[0, k]))
+        stores.append(pltpu.make_async_copy(out.at[:, cut], out_ref.at[:, cut], sems.at[1, k]))
+        loads[k].start()
+    for k in range(pieces):
+        loads[k].wait()
+        cut = slice(k * piece, (k + 1) * piece)
+        out[:, cut] = jnp.dot(placed_ref[...], back[:, cut], preferred_element_type=F32).astype(BF16)
+        stores[k].start()
+    for store in stores:
+        store.wait()
     token_ref[...] = jnp.zeros_like(token_ref)
 
 
@@ -437,27 +460,26 @@
         cost_estimate=cost(OWN_US),
         name="own_part",
     )(chunks, messages[1], messages[3], got, low, high, after)
-    pieces = 4
     hidden_grad, after = pl.pallas_call(
         sum_kernel,
-        grid=(pieces,),
-        in_specs=[
-            whole(tokens, slots),
-            pl.BlockSpec((slots, width // pieces), lambda i: (0, i)),
-            anywhere,
+        in_specs=[vmem, hbm, anywhere],
+        out_specs=[hbm, vmem],
+        out_shape=[pltpu.HBM((tokens, width), BF16), token],
+        scratch_shapes=[
+            pltpu.VMEM((slots, width), BF16),
+            pltpu.VMEM((tokens, width), BF16),
+            pltpu.SemaphoreType.DMA((2, STEPS)),
         ],
-        out_specs=[pl.BlockSpec((tokens, width // pieces), lambda i: (0, i)), whole(8, 128)],
-        out_shape=[jax.ShapeDtypeStruct((tokens, width), BF16), token],
         compiler_params=params(12),
         cost_estimate=cost(SUM_US),
         name="sum_parts",
     )(placed, in_hbm(back), after)
-
     weight_grad = pl.pallas_call(
         last_kernel,
         in_specs=[vmem, vmem, vmem, anywhere],
-        out_specs=vmem,
-        out_shape=jax.ShapeDtypeStruct((chunk, words), BF16),
+        out_specs=hbm,
+        out_shape=pltpu.HBM((chunk, words), BF16),
+        scratch_shapes=[pltpu.VMEM((chunk, words), BF16), pltpu.SemaphoreType.DMA((2,))],
         compiler_params=params(12),
         cost_estimate=cost(0),
         name="last_add",

time: 175 us -> 175 us (level)
  transfers between devices with their start and end apart: 16 -> 16, of which waited for: 7 -> 7; matrix products, arithmetic and copies ran while one was open for 0% -> 0% of each run, Pallas kernels for 25% -> 24%
where the time goes in v8:
time: 175 us; the launch traced here: 174 us
  waiting for transfers between devices  80.4 us (46%)
  Pallas kernels  56 us (32%)
  starting transfers between devices  37 us (21%)
    all_to_all x1, waiting for transfers between devices, body(): lax.all_to_all(send.reshape(peers, capacity, sent), 'vocab', split_axis=0...  52.7 us
    ppermute x14, waiting for transfers between devices, hop(): return lax.ppermute(x, 'dp', [(i, (i + d) % planes) for i in range(planes)])  27.7 us
    pallas_call x10, Pallas kernels, add(): pl.pallas_call(add_kernel, grid_spec=pltpu.PrefetchScalarGridSpec(num_sca...  22.5 us
    ppermute x14, starting transfers between devices, hop(): return lax.ppermute(x, 'dp', [(i, (i + d) % planes) for i in range(planes)])  22.2 us
    pallas_call x1, Pallas kernels, state_parts(): pl.pallas_call(back_kernel, in_specs=[vmem, vmem, hbm, anywhere], out_spe...  8.14 us
    all_to_all x1, starting transfers between devices, body(): lax.all_to_all(send.reshape(peers, capacity, sent), 'vocab', split_axis=0...  7.68 us
    pallas_call x1, Pallas kernels, body(): pl.pallas_call(low_kernel, in_specs=[smem, hbm, hbm, anywhere], out_specs...  7.14 us
    all_to_all x1, starting transfers between devices, body(): lax.all_to_all(part.reshape(peers, capacity, width), 'vocab', split_axis=...  7.09 us
  transfers between devices with their start and end apart: 16, of which 7 were waited for; matrix products, arithmetic and copies ran while one was open for 0% of the time, Pallas kernels for 24%

profile of v8, /device:TPU:98, one launch (start us, length us, event | category | flops | bytes accessed | tf_op | source)
XLA Modules:
  0.0 174.3 jit_solution(4119269458159866800)
XLA Ops:
  0.6 4.8 %place_rows.1 = (bf16[512,4224]{1,0:T(8,128)(2,1)}, bf16[512,128]{1,0:T(8,128)(2,1)S(1)}) custom-call(bf16[128,4096]{1,0:T(8,128)(2,1)} %hidden_ref.1, s32[3,128]{1,0:T(4,128)} %bitcast.15, s32[3,2,128]{2,1,0:T(2,128)} %bitcast.13, s32[3,2,128]{2,1,0:T(2,128)} %bitcast.14, s32[1,128]{1,0:T(1,128)} %bitcast.16, s32[1,128]{1,0:T(1,128)} %bitcast.17, ...), custom_call_target="tpu_custom_call" | custom-call | tf_op jit(solution)/shard_map/place_rows/pallas_call | solution.py:323
  5.5 7.7 %all-to-all-start = ((bf16[32,16,4224]{2,1,0:T(8,128)(2,1)}), bf16[32,16,4224]{2,1,0:T(8,128)(2,1)}, u32[]{:S(2)}, u32[]{:S(2)}) async-start(bf16[32,16,4224]{2,1,0:T(8,128)(2,1)} %bitcast.11), calls=%async_computation | async-start | bytes 8650752 | tf_op jit(solution)/shard_map/all_to_all | solution.py:341
  13.3 52.7 %all-to-all-done = bf16[32,16,4224]{2,1,0:T(8,128)(2,1)} async-done(((bf16[32,16,4224]{2,1,0:T(8,128)(2,1)}), bf16[32,16,4224]{2,1,0:T(8,128)(2,1)}, u32[]{:S(2)}, u32[]{:S(2)}) %all-to-all-start) | async-done | bytes 4325408 | tf_op jit(solution)/shard_map/all_to_all | solution.py:341
  66.0 7.1 %low_scores.1 = (bf16[512,4096]{1,0:T(8,128)(2,1)S(1)}, bf16[512,128]{1,0:T(8,128)(2,1)S(1)}, bf16[512,512]{1,0:T(8,128)(2,1)S(1)}, bf16[512,512]{1,0:T(8,128)(2,1)}, bf16[512,512]{1,0:T(8,128)(2,1)}) custom-call(s32[8]{0:T(128)S(1)} %compare_select_fusion.chunks_ref, bf16[512,4224]{1,0:T(8,128)(2,1)} %bitcast.8.got_ref.rows_ref, ...), custom_call_target="tpu_custom_call" | custom-call | tf_op jit(solution)/shard_map/low_scores/pallas_call | solution.py:363
  73.1 3.2 %collective-permute-start.1 = (bf16[512,512]{1,0:T(8,128)(2,1)}, bf16[512,512]{1,0:T(8,128)(2,1)}, u32[]{:S(2)}, u32[]{:S(2)}) collective-permute-start(bf16[512,512]{1,0:T(8,128)(2,1)} %get-tuple-element.47), channel_id=1, source_target_pairs={{0,32},{32,64},{64,96},{96,128},{128,160},{160,192},{192,224},{224... | collective-permute-start | bytes 1572872 | tf_op jit(solution)/shard_map/ppermute | solution.py:391
  76.3 5.3 %high_scores.1 = (bf16[512,512]{1,0:T(8,128)(2,1)S(1)}, bf16[512,512]{1,0:T(8,128)(2,1)S(1)}, bf16[512,512]{1,0:T(8,128)(2,1)S(1)}) custom-call(s32[8]{0:T(128)S(1)} %compare_select_fusion.chunks_ref, bf16[512,4096]{1,0:T(8,128)(2,1)S(1)} %get-tuple-element.41.rows_ref, bf16[512,128]{1,0:T(8,128)(2,1)S(1)} %get-tuple-element.42.meta_ref, ...), custom_call_target="tpu_custom_call" | custom-call | tf_op jit(solution)/shard_map/high_scores/pallas_call | solution.py:379
  81.7 3.5 %collective-permute-start.4 = (bf16[512,512]{1,0:T(8,128)(2,1)S(1)}, bf16[512,512]{1,0:T(8,128)(2,1)S(1)}, u32[]{:S(2)}, u32[]{:S(2)}) collective-permute-start(bf16[512,512]{1,0:T(8,128)(2,1)S(1)} %get-tuple-element.44.after_ref), channel_id=1, source_target_pairs={{0,32},{32,64},{64,96},{96,128},{128,160},{160,192},{192,224},{224... | collective-permute-start | bytes 1572872 | tf_op jit(solution)/shard_map/ppermute | solution.py:391
  85.2 8.1 %state_parts.1 = (bf16[512,4096]{1,0:T(8,128)(2,1)}, f32[8,128]{1,0:T(8,128)S(1)}) custom-call(bf16[512,512]{1,0:T(8,128)(2,1)S(1)} %get-tuple-element.40.low_ref.grad_ref, bf16[512,512]{1,0:T(8,128)(2,1)S(1)} %get-tuple-element.43.high_ref.grad_ref, bf16[4096,1024]{1,0:T(8,128)(2,1)} %weight_ref.5, bf16[512,512]{1,0:T(8,128)(2,1)S(1)} %get-tuple-element.44.after_ref), custom_call_target="tpu_custom_call" | custom-call | tf_op jit(solution)/shard_map/state_parts/pallas_call | solution.py:400
  93.4 7.1 %all-to-all-start.1 = ((bf16[32,16,4096]{2,1,0:T(8,128)(2,1)}), bf16[32,16,4096]{2,1,0:T(8,128)(2,1)}, u32[]{:S(2)}, u32[]{:S(2)}) async-start(bf16[32,16,4096]{2,1,0:T(8,128)(2,1)} %bitcast.12), calls=%async_computation.1 | async-start | bytes 8388608 | tf_op jit(solution)/shard_map/all_to_all | solution.py:446
  100.5 2.2 %add_part.10 = (bf16[512,512]{1,0:T(8,128)(2,1)S(1)}, f32[8,128]{1,0:T(8,128)S(1)}) custom-call(s32[8]{0:T(128)S(1)} %compare_select_fusion.chunks_ref, bf16[512,512]{1,0:T(8,128)(2,1)} %collective-permute-done.1.got_ref, bf16[512,4224]{1,0:T(8,128)(2,1)} %bitcast.8.got_ref.rows_ref, bf16[512,512]{1,0:T(8,128)(2,1)S(1)} %get-tuple-element.40.low_ref.grad_ref, ...), custom_call_target="tpu_custom_call" | custom-call | flops 3449999872 | tf_op jit(solution)/shard_map/add_part/pallas_call | solution.py:417
  102.7 1.8 %collective-permute-start.3 = (bf16[512,512]{1,0:T(8,128)(2,1)S(1)}, bf16[512,512]{1,0:T(8,128)(2,1)S(1)}, u32[]{:S(2)}, u32[]{:S(2)}) collective-permute-start(bf16[512,512]{1,0:T(8,128)(2,1)S(1)} %get-tuple-element.51), channel_id=1, source_target_pairs={{0,32},{32,64},{64,96},{96,128},{128,160},{160,192},{192,224},{224... | collective-permute-start | bytes 1572872 | tf_op jit(solution)/shard_map/ppermute | solution.py:391
  104.5 2.2 %add_part.11 = (bf16[512,512]{1,0:T(8,128)(2,1)S(1)}, f32[8,128]{1,0:T(8,128)S(1)}) custom-call(s32[8]{0:T(128)S(1)} %compare_select_fusion.chunks_ref, bf16[512,512]{1,0:T(8,128)(2,1)} %collective-permute-done.got_ref, bf16[512,4224]{1,0:T(8,128)(2,1)} %bitcast.8.got_ref.rows_ref, bf16[512,512]{1,0:T(8,128)(2,1)S(1)} %get-tuple-element.40.low_ref.grad_ref, ...), custom_call_target="tpu_custom_call" | custom-call | flops 3449999872 | tf_op jit(solution)/shard_map/add_part/pallas_call | solution.py:417
  107.1 2.1 %add_part.12 = (bf16[512,512]{1,0:T(8,128)(2,1)S(1)}, f32[8,128]{1,0:T(8,128)S(1)}) custom-call(s32[8]{0:T(128)S(1)} %compare_select_fusion.chunks_ref, bf16[512,512]{1,0:T(8,128)(2,1)S(1)} %collective-permute-done.5.got_ref, bf16[512,4224]{1,0:T(8,128)(2,1)} %bitcast.8.got_ref.rows_ref, bf16[512,512]{1,0:T(8,128)(2,1)S(1)} %get-tuple-element.43.high_ref.grad_ref, ...), custom_call_target="tpu_custom_call" | custom-call | flops 3449999872 | tf_op jit(solution)/shard_map/add_part/pallas_call | solution.py:417
  109.3 2.1 %add_part.13 = (bf16[512,512]{1,0:T(8,128)(2,1)S(1)}, f32[8,128]{1,0:T(8,128)S(1)}) custom-call(s32[8]{0:T(128)S(1)} %compare_select_fusion.chunks_ref, bf16[512,512]{1,0:T(8,128)(2,1)S(1)} %collective-permute-done.4.got_ref, bf16[512,4224]{1,0:T(8,128)(2,1)} %bitcast.8.got_ref.rows_ref, bf16[512,512]{1,0:T(8,128)(2,1)S(1)} %get-tuple-element.43.high_ref.grad_ref, ...), custom_call_target="tpu_custom_call" | custom-call | flops 3449999872 | tf_op jit(solution)/shard_map/add_part/pallas_call | solution.py:417
  111.3 3.3 %collective-permute-start.7 = (bf16[512,512]{1,0:T(8,128)(2,1)S(1)}, bf16[512,512]{1,0:T(8,128)(2,1)S(1)}, u32[]{:S(2)}, u32[]{:S(2)}) collective-permute-start(bf16[512,512]{1,0:T(8,128)(2,1)S(1)} %get-tuple-element.58), channel_id=1, source_target_pairs={{0,32},{32,64},{64,96},{96,128},{128,160},{160,192},{192,224},{224... | collective-permute-start | bytes 1572872 | tf_op jit(solution)/shard_map/ppermute | solution.py:391
  114.6 2.9 %collective-permute-done.3.got_ref = bf16[512,512]{1,0:T(8,128)(2,1)S(1)} collective-permute-done((bf16[512,512]{1,0:T(8,128)(2,1)S(1)}, bf16[512,512]{1,0:T(8,128)(2,1)S(1)}, u32[]{:S(2)}, u32[]{:S(2)}) %collective-permute-start.3) | collective-permute-done | bytes 524320 | tf_op jit(solution)/shard_map/ppermute | solution.py:391
  117.5 2.1 %add_part.14 = (bf16[512,512]{1,0:T(8,128)(2,1)S(1)}, f32[8,128]{1,0:T(8,128)S(1)}) custom-call(s32[8]{0:T(128)S(1)} %compare_select_fusion.chunks_ref, bf16[512,512]{1,0:T(8,128)(2,1)S(1)} %collective-permute-done.3.got_ref, bf16[512,4224]{1,0:T(8,128)(2,1)} %bitcast.8.got_ref.rows_ref, bf16[512,512]{1,0:T(8,128)(2,1)S(1)} %get-tuple-element.40.low_ref.grad_ref, ...), custom_call_target="tpu_custom_call" | custom-call | flops 3449999872 | tf_op jit(solution)/shard_map/add_part/pallas_call | solution.py:417
  119.6 3.0 %collective-permute-start.11 = (bf16[512,512]{1,0:T(8,128)(2,1)S(1)}, bf16[512,512]{1,0:T(8,128)(2,1)S(1)}, u32[]{:S(2)}, u32[]{:S(2)}) collective-permute-start(bf16[512,512]{1,0:T(8,128)(2,1)S(1)} %get-tuple-element.64), channel_id=1, source_target_pairs={{0,32},{32,64},{64,96},{96,128},{128,160},{160,192},{192,224},{224... | collective-permute-start | bytes 1572872 | tf_op jit(solution)/shard_map/ppermute | solution.py:391
  122.8 2.1 %add_part.15 = (bf16[512,512]{1,0:T(8,128)(2,1)S(1)}, f32[8,128]{1,0:T(8,128)S(1)}) custom-call(s32[8]{0:T(128)S(1)} %compare_select_fusion.chunks_ref, bf16[512,512]{1,0:T(8,128)(2,1)S(1)} %collective-permute-done.2.got_ref, bf16[512,4224]{1,0:T(8,128)(2,1)} %bitcast.8.got_ref.rows_ref, bf16[512,512]{1,0:T(8,128)(2,1)S(1)} %get-tuple-element.40.low_ref.grad_ref, ...), custom_call_target="tpu_custom_call" | custom-call | flops 3449999872 | tf_op jit(solution)/shard_map/add_part/pallas_call | solution.py:417
  124.9 8.1 %collective-permute-done.8.got_ref = bf16[512,512]{1,0:T(8,128)(2,1)S(1)} collective-permute-done((bf16[512,512]{1,0:T(8,128)(2,1)S(1)}, bf16[512,512]{1,0:T(8,128)(2,1)S(1)}, u32[]{:S(2)}, u32[]{:S(2)}) %collective-permute-start.8) | collective-permute-done | bytes 524320 | tf_op jit(solution)/shard_map/ppermute | solution.py:391
  133.0 2.1 %add_part.16 = (bf16[512,512]{1,0:T(8,128)(2,1)S(1)}, f32[8,128]{1,0:T(8,128)S(1)}) custom-call(s32[8]{0:T(128)S(1)} %compare_select_fusion.chunks_ref, bf16[512,512]{1,0:T(8,128)(2,1)S(1)} %collective-permute-done.8.got_ref, bf16[512,4224]{1,0:T(8,128)(2,1)} %bitcast.8.got_ref.rows_ref, bf16[512,512]{1,0:T(8,128)(2,1)S(1)} %get-tuple-element.43.high_ref.grad_ref, ...), custom_call_target="tpu_custom_call" | custom-call | flops 3449999872 | tf_op jit(solution)/shard_map/add_part/pallas_call | solution.py:417
  135.1 2.1 %add_part.17 = (bf16[512,512]{1,0:T(8,128)(2,1)S(1)}, f32[8,128]{1,0:T(8,128)S(1)}) custom-call(s32[8]{0:T(128)S(1)} %compare_select_fusion.chunks_ref, bf16[512,512]{1,0:T(8,128)(2,1)S(1)} %collective-permute-done.7.got_ref, bf16[512,4224]{1,0:T(8,128)(2,1)} %bitcast.8.got_ref.rows_ref, bf16[512,512]{1,0:T(8,128)(2,1)S(1)} %get-tuple-element.43.high_ref.grad_ref, ...), custom_call_target="tpu_custom_call" | custom-call | flops 3449999872 | tf_op jit(solution)/shard_map/add_part/pallas_call | solution.py:417
  137.2 3.5 %collective-permute-start.9 = (bf16[512,512]{1,0:T(8,128)(2,1)S(1)}, bf16[512,512]{1,0:T(8,128)(2,1)S(1)}, u32[]{:S(2)}, u32[]{:S(2)}) collective-permute-start(bf16[512,512]{1,0:T(8,128)(2,1)S(1)} %get-tuple-element.62), channel_id=1, source_target_pairs={{0,32},{32,64},{64,96},{96,128},{128,160},{160,192},{192,224},{224... | collective-permute-start | bytes 1572872 | tf_op jit(solution)/shard_map/ppermute | solution.py:391
  140.7 2.9 %add_part.18 = (bf16[512,512]{1,0:T(8,128)(2,1)}, f32[8,128]{1,0:T(8,128)S(1)}) custom-call(s32[8]{0:T(128)S(1)} %compare_select_fusion.chunks_ref, bf16[512,512]{1,0:T(8,128)(2,1)S(1)} %collective-permute-done.11.got_ref, bf16[512,4224]{1,0:T(8,128)(2,1)} %bitcast.8.got_ref.rows_ref, bf16[512,512]{1,0:T(8,128)(2,1)S(1)} %get-tuple-element.40.low_ref.grad_ref, ...), custom_call_target="tpu_custom_call" | custom-call | flops 3449999872 | tf_op jit(solution)/shard_map/add_part/pallas_call | solution.py:417
  143.6 7.6 %collective-permute-done.10.got_ref = bf16[512,512]{1,0:T(8,128)(2,1)S(1)} collective-permute-done((bf16[512,512]{1,0:T(8,128)(2,1)S(1)}, bf16[512,512]{1,0:T(8,128)(2,1)S(1)}, u32[]{:S(2)}, u32[]{:S(2)}) %collective-permute-start.10) | collective-permute-done | bytes 524320 | tf_op jit(solution)/shard_map/ppermute | solution.py:391
  151.2 2.9 %add_part.19 = (bf16[512,512]{1,0:T(8,128)(2,1)}, f32[8,128]{1,0:T(8,128)S(1)}) custom-call(s32[8]{0:T(128)S(1)} %compare_select_fusion.chunks_ref, bf16[512,512]{1,0:T(8,128)(2,1)S(1)} %collective-permute-done.10.got_ref, bf16[512,4224]{1,0:T(8,128)(2,1)} %bitcast.8.got_ref.rows_ref, bf16[512,512]{1,0:T(8,128)(2,1)S(1)} %get-tuple-element.43.high_ref.grad_ref, ...), custom_call_target="tpu_custom_call" | custom-call | flops 3449999872 | tf_op jit(solution)/shard_map/add_part/pallas_call | solution.py:417
  154.1 3.2 %collective-permute-start.12 = (bf16[512,512]{1,0:T(8,128)(2,1)}, bf16[512,512]{1,0:T(8,128)(2,1)}, u32[]{:S(2)}, u32[]{:S(2)}) collective-permute-start(bf16[512,512]{1,0:T(8,128)(2,1)} %get-tuple-element.70), channel_id=1, source_target_pairs={{0,32},{32,64},{64,96},{96,128},{128,160},{160,192},{192,224},{224... | collective-permute-start | bytes 1572872 | tf_op jit(solution)/shard_map/ppermute | solution.py:391
  157.3 5.1 %collective-permute-done.6.low_near_ref = bf16[512,512]{1,0:T(8,128)(2,1)S(1)} collective-permute-done((bf16[512,512]{1,0:T(8,128)(2,1)S(1)}, bf16[512,512]{1,0:T(8,128)(2,1)S(1)}, u32[]{:S(2)}, u32[]{:S(2)}) %collective-permute-start.6) | collective-permute-done | bytes 524320 | tf_op jit(solution)/shard_map/ppermute | solution.py:391
  162.4 2.3 %own_part.1 = (f32[512,1024]{1,0:T(8,128)S(1)}, f32[8,128]{1,0:T(8,128)S(1)}) custom-call(s32[8]{0:T(128)S(1)} %compare_select_fusion.chunks_ref, bf16[512,512]{1,0:T(8,128)(2,1)S(1)} %collective-permute-done.6.low_near_ref, bf16[512,512]{1,0:T(8,128)(2,1)S(1)} %collective-permute-done.9.high_near_ref, bf16[512,4224]{1,0:T(8,128)(2,1)} %bitcast.8.got_ref.rows_ref, ...), custom_call_target="tpu_custom_call" | custom-call | flops 115000000512 | tf_op jit(solution)/shard_map/own_part/pallas_call | solution.py:450
  164.8 3.3 %sum_parts.1 = (bf16[128,4096]{1,0:T(8,128)(2,1)}, f32[8,128]{1,0:T(8,128)S(1)}) custom-call(bf16[128,512]{1,0:T(8,128)(2,1)S(1)} %copy-done.1, bf16[512,4096]{1,0:T(8,128)(2,1)} %bitcast.10.back_ref, f32[8,128]{1,0:T(8,128)S(1)} %get-tuple-element.68.after_ref), custom_call_target="tpu_custom_call" | custom-call | tf_op jit(solution)/shard_map/sum_parts/pallas_call | solution.py:463
  168.1 3.7 %collective-permute-done.13.high_far_ref = bf16[512,512]{1,0:T(8,128)(2,1)} collective-permute-done((bf16[512,512]{1,0:T(8,128)(2,1)}, bf16[512,512]{1,0:T(8,128)(2,1)}, u32[]{:S(2)}, u32[]{:S(2)}) %collective-permute-start.13) | collective-permute-done | bytes 524320 | tf_op jit(solution)/shard_map/ppermute | solution.py:391
  171.8 2.3 %last_add.1 = bf16[512,1024]{1,0:T(8,128)(2,1)} custom-call(bf16[512,512]{1,0:T(8,128)(2,1)} %collective-permute-done.12.low_far_ref, bf16[512,512]{1,0:T(8,128)(2,1)} %collective-permute-done.13.high_far_ref, f32[512,1024]{1,0:T(8,128)S(1)} %get-tuple-element.72.own_ref, f32[8,128]{1,0:T(8,128)S(1)} %get-tuple-element.73.after_ref), custom_call_target="tpu_custom_call" | custom-call | tf_op jit(solution)/shard_map/last_add/pallas_call | solution.py:477
  (23 shorter events, 1.0 us)
Async XLA Ops:
  5.5 60.5 %all-to-all-start = ((bf16[32,16,4224]{2,1,0:T(8,128)(2,1)}), bf16[32,16,4224]{2,1,0:T(8,128)(2,1)}, u32[]{:S(2)}, u32[]{:S(2)}) async-start(bf16[32,16,4224]{2,1,0:T(8,128)(2,1)} %bitcast.11), calls=%async_computation | async-start | bytes 8650752 | tf_op jit(solution)/shard_map/all_to_all | solution.py:341
  13.3 59.9 %copy-start = (bf16[128,512]{1,0:T(8,128)(2,1)}, bf16[128,512]{1,0:T(8,128)(2,1)S(1)}, u32[]{:S(2)}) copy-start(bf16[128,512]{1,0:T(8,128)(2,1)S(1)} %turn_places.1.after_ref.placed_ref) | copy-start | bytes 393220
  73.1 27.3 %collective-permute-start.1 = (bf16[512,512]{1,0:T(8,128)(2,1)}, bf16[512,512]{1,0:T(8,128)(2,1)}, u32[]{:S(2)}, u32[]{:S(2)}) collective-permute-start(bf16[512,512]{1,0:T(8,128)(2,1)} %get-tuple-element.47), channel_id=1, source_target_pairs={{0,32},{32,64},{64,96},{96,128},{128,160},{160,192},{192,224},{224... | collective-permute-start | bytes 1572872 | tf_op jit(solution)/shard_map/ppermute | solution.py:391
  76.3 28.2 %collective-permute-start = (bf16[512,512]{1,0:T(8,128)(2,1)}, bf16[512,512]{1,0:T(8,128)(2,1)}, u32[]{:S(2)}, u32[]{:S(2)}) collective-permute-start(bf16[512,512]{1,0:T(8,128)(2,1)} %get-tuple-element.46), channel_id=1, source_target_pairs={{0,224},{32,0},{64,32},{96,64},{128,96},{160,128},{192,160},{224,1... | collective-permute-start | bytes 1572872 | tf_op jit(solution)/shard_map/ppermute | solution.py:391
  81.7 25.4 %collective-permute-start.5 = (bf16[512,512]{1,0:T(8,128)(2,1)S(1)}, bf16[512,512]{1,0:T(8,128)(2,1)S(1)}, u32[]{:S(2)}, u32[]{:S(2)}) collective-permute-start(bf16[512,512]{1,0:T(8,128)(2,1)S(1)} %get-tuple-element.52), channel_id=1, source_target_pairs={{0,224},{32,0},{64,32},{96,64},{128,96},{160,128},{192,160},{224,1... | collective-permute-start | bytes 1572872 | tf_op jit(solution)/shard_map/ppermute | solution.py:391
  81.7 27.5 %collective-permute-start.4 = (bf16[512,512]{1,0:T(8,128)(2,1)S(1)}, bf16[512,512]{1,0:T(8,128)(2,1)S(1)}, u32[]{:S(2)}, u32[]{:S(2)}) collective-permute-start(bf16[512,512]{1,0:T(8,128)(2,1)S(1)} %get-tuple-element.44.after_ref), channel_id=1, source_target_pairs={{0,32},{32,64},{64,96},{96,128},{128,160},{160,192},{192,224},{224... | collective-permute-start | bytes 1572872 | tf_op jit(solution)/shard_map/ppermute | solution.py:391
  93.4 71.4 %all-to-all-start.1 = ((bf16[32,16,4096]{2,1,0:T(8,128)(2,1)}), bf16[32,16,4096]{2,1,0:T(8,128)(2,1)}, u32[]{:S(2)}, u32[]{:S(2)}) async-start(bf16[32,16,4096]{2,1,0:T(8,128)(2,1)} %bitcast.12), calls=%async_computation.1 | async-start | bytes 8388608 | tf_op jit(solution)/shard_map/all_to_all | solution.py:446
  102.7 14.8 %collective-permute-start.3 = (bf16[512,512]{1,0:T(8,128)(2,1)S(1)}, bf16[512,512]{1,0:T(8,128)(2,1)S(1)}, u32[]{:S(2)}, u32[]{:S(2)}) collective-permute-start(bf16[512,512]{1,0:T(8,128)(2,1)S(1)} %get-tuple-element.51), channel_id=1, source_target_pairs={{0,32},{32,64},{64,96},{96,128},{128,160},{160,192},{192,224},{224... | collective-permute-start | bytes 1572872 | tf_op jit(solution)/shard_map/ppermute | solution.py:391
  106.7 16.1 %collective-permute-start.2 = (bf16[512,512]{1,0:T(8,128)(2,1)S(1)}, bf16[512,512]{1,0:T(8,128)(2,1)S(1)}, u32[]{:S(2)}, u32[]{:S(2)}) collective-permute-start(bf16[512,512]{1,0:T(8,128)(2,1)S(1)} %get-tuple-element.50), channel_id=1, source_target_pairs={{0,224},{32,0},{64,32},{96,64},{128,96},{160,128},{192,160},{224,1... | collective-permute-start | bytes 1572872 | tf_op jit(solution)/shard_map/ppermute | solution.py:391
  109.2 23.8 %collective-permute-start.8 = (bf16[512,512]{1,0:T(8,128)(2,1)S(1)}, bf16[512,512]{1,0:T(8,128)(2,1)S(1)}, u32[]{:S(2)}, u32[]{:S(2)}) collective-permute-start(bf16[512,512]{1,0:T(8,128)(2,1)S(1)} %get-tuple-element.59), channel_id=1, source_target_pairs={{0,224},{32,0},{64,32},{96,64},{128,96},{160,128},{192,160},{224,1... | collective-permute-start | bytes 1572872 | tf_op jit(solution)/shard_map/ppermute | solution.py:391
  111.3 23.8 %collective-permute-start.7 = (bf16[512,512]{1,0:T(8,128)(2,1)S(1)}, bf16[512,512]{1,0:T(8,128)(2,1)S(1)}, u32[]{:S(2)}, u32[]{:S(2)}) collective-permute-start(bf16[512,512]{1,0:T(8,128)(2,1)S(1)} %get-tuple-element.58), channel_id=1, source_target_pairs={{0,32},{32,64},{64,96},{96,128},{128,160},{160,192},{192,224},{224... | collective-permute-start | bytes 1572872 | tf_op jit(solution)/shard_map/ppermute | solution.py:391
  119.6 21.1 %collective-permute-start.11 = (bf16[512,512]{1,0:T(8,128)(2,1)S(1)}, bf16[512,512]{1,0:T(8,128)(2,1)S(1)}, u32[]{:S(2)}, u32[]{:S(2)}) collective-permute-start(bf16[512,512]{1,0:T(8,128)(2,1)S(1)} %get-tuple-element.64), channel_id=1, source_target_pairs={{0,32},{32,64},{64,96},{96,128},{128,160},{160,192},{192,224},{224... | collective-permute-start | bytes 1572872 | tf_op jit(solution)/shard_map/ppermute | solution.py:391
  135.0 16.1 %collective-permute-start.10 = (bf16[512,512]{1,0:T(8,128)(2,1)S(1)}, bf16[512,512]{1,0:T(8,128)(2,1)S(1)}, u32[]{:S(2)}, u32[]{:S(2)}) collective-permute-start(bf16[512,512]{1,0:T(8,128)(2,1)S(1)} %get-tuple-element.63), channel_id=1, source_target_pairs={{0,224},{32,0},{64,32},{96,64},{128,96},{160,128},{192,160},{224,1... | collective-permute-start | bytes 1572872 | tf_op jit(solution)/shard_map/ppermute | solution.py:391
  137.2 20.1 %collective-permute-start.9 = (bf16[512,512]{1,0:T(8,128)(2,1)S(1)}, bf16[512,512]{1,0:T(8,128)(2,1)S(1)}, u32[]{:S(2)}, u32[]{:S(2)}) collective-permute-start(bf16[512,512]{1,0:T(8,128)(2,1)S(1)} %get-tuple-element.62), channel_id=1, source_target_pairs={{0,32},{32,64},{64,96},{96,128},{128,160},{160,192},{192,224},{224... | collective-permute-start | bytes 1572872 | tf_op jit(solution)/shard_map/ppermute | solution.py:391
  140.7 21.7 %collective-permute-start.6 = (bf16[512,512]{1,0:T(8,128)(2,1)S(1)}, bf16[512,512]{1,0:T(8,128)(2,1)S(1)}, u32[]{:S(2)}, u32[]{:S(2)}) collective-permute-start(bf16[512,512]{1,0:T(8,128)(2,1)S(1)} %get-tuple-element.57), channel_id=1, source_target_pairs={{0,224},{32,0},{64,32},{96,64},{128,96},{160,128},{192,160},{224,1... | collective-permute-start | bytes 1572872 | tf_op jit(solution)/shard_map/ppermute | solution.py:391
  154.1 17.8 %collective-permute-start.13 = (bf16[512,512]{1,0:T(8,128)(2,1)}, bf16[512,512]{1,0:T(8,128)(2,1)}, u32[]{:S(2)}, u32[]{:S(2)}) collective-permute-start(bf16[512,512]{1,0:T(8,128)(2,1)} %get-tuple-element.71), channel_id=1, source_target_pairs={{0,224},{32,0},{64,32},{96,64},{128,96},{160,128},{192,160},{224,1... | collective-permute-start | bytes 1572872 | tf_op jit(solution)/shard_map/ppermute | solution.py:391
  154.1 17.8 %collective-permute-start.12 = (bf16[512,512]{1,0:T(8,128)(2,1)}, bf16[512,512]{1,0:T(8,128)(2,1)}, u32[]{:S(2)}, u32[]{:S(2)}) collective-permute-start(bf16[512,512]{1,0:T(8,128)(2,1)} %get-tuple-element.70), channel_id=1, source_target_pairs={{0,32},{32,64},{64,96},{96,128},{128,160},{160,192},{192,224},{224... | collective-permute-start | bytes 1572872 | tf_op jit(solution)/shard_map/ppermute | solution.py:391
  162.4 2.4 %copy-start.1 = (bf16[128,512]{1,0:T(8,128)(2,1)S(1)}, bf16[128,512]{1,0:T(8,128)(2,1)}, u32[]{:S(2)}) copy-start(bf16[128,512]{1,0:T(8,128)(2,1)} %copy-done) | copy-start | bytes 393220
